TPU v7x, 32 devices: a whole 2x2x4 slice. The times are simulated.
32 devices in a mesh: seq: 8 (over y, x, core), head: 4 (over z).
Axes of the slice: x: 2, y: 2, z: 4, core: 2. Of those that a mesh axis runs over, the one named last changes fastest.
Arguments:
- query_rows: bfloat16 [256, 512], P('seq', 'head'), may hold values from -6 to 6
- key_rows: bfloat16 [4096, 512], P('seq', 'head'), may hold values from -6 to 6
- value_rows: bfloat16 [4096, 512], P('seq', 'head'), may hold values from -6 to 6
- attn_out: bfloat16 [256, 512], P(('seq', 'head')), may hold values from -3 to 3
- out_grad: bfloat16 [256, 512], P(('seq', 'head')), may hold values from -48 to 48
- logsumexp: bfloat16 [4, 256], P('head', 'seq'), may hold values from 4.5 to 6.5
- shard_pick: int32 [4, 256, 4], P('head', 'seq'), may hold values from 0 to 7, all different within a row; in each aligned block of 32 rows (0 to 31, 32 to 63, ..., all dimensions but the last counted through in order) at most 32 rows name the same one
- block_pick: int32 [4, 256, 4, 4], P('head', 'seq'), may hold values from 0 to 7, as said below
Outputs:
- query_grad: bfloat16 [256, 512], P('seq', 'head')
- key_grad: bfloat16 [4096, 512], P('seq', 'head')
- value_grad: bfloat16 [4096, 512], P('seq', 'head')
Inputs may be any that keep to these rules, and one draw needn't show every extreme that they name: `shard_pick`: each query row of each head names 4 different shards; among the 32 rows of one device (one head, one shard of query rows) no shard is named more than 32 times. `block_pick`: the 4 entries of one query row, head and group are different.
All inputs are finite; a program needn't handle non-finite values.
Results may differ from a plain program's by a relative error of at most 0.0077.
Values may be sent and summed in bfloat16 or wider, within the bound.
No kernel may reach another device: no remote copies, remote signals or barrier semaphores. Data moves between devices by JAX's collectives and lax.ppermute only.
A program may use at most 64 MiB of HBM per device.

v0:
```python
import jax
import jax.numpy as jnp
from jax import lax
from jax.sharding import PartitionSpec as P

BLK = 64


def block_terms(row_data, small_data, key_rows, value_rows, own_shard, groups):
    count = row_data.shape[0]
    head_size = key_rows.shape[1]
    per_shard = key_rows.shape[0] // BLK
    queries = row_data[:, :head_size]
    grads = row_data[:, head_size:]
    stats = small_data[:, :2].astype(jnp.float32)
    shards_of = small_data[:, 2 : 2 + groups].astype(jnp.int32)
    picks_of = small_data[:, 2 + groups :].astype(jnp.int32).reshape(count, groups, -1)
    local_ids = jnp.arange(per_shard, dtype=jnp.int32)
    matched = (shards_of == own_shard + 1)[:, :, None, None] & (
        picks_of[:, :, :, None] == local_ids[None, None, None, :]
    )
    chosen = jnp.any(matched, axis=(1, 2))
    mask = jnp.broadcast_to(chosen[:, :, None], (count, per_shard, BLK)).reshape(
        count, key_rows.shape[0]
    )
    scores = jnp.dot(queries, key_rows.T, preferred_element_type=jnp.float32) * head_size ** (-0.5)
    probs = jnp.where(mask, jnp.exp(scores - stats[:, 0:1]), 0.0)
    probs_low = probs.astype(jnp.bfloat16)
    value_add = jnp.dot(probs_low.T, grads, preferred_element_type=jnp.float32)
    dprob = jnp.dot(grads, value_rows.T, preferred_element_type=jnp.float32)
    dscore = (probs * (dprob - stats[:, 1:2])).astype(jnp.bfloat16)
    key_add = jnp.dot(dscore.T, queries, preferred_element_type=jnp.float32)
    query_part = jnp.dot(dscore, key_rows, preferred_element_type=jnp.float32)
    return (query_part, key_add, value_add)


def sweep(rows_in, small_in, key_rows, value_rows, own_shard, groups):
    sources, per_source = (rows_in.shape[0], rows_in.shape[1])
    merged = 1
    while merged * 2 <= sources and sources % (merged * 2) == 0 and (merged * per_source < 512):
        merged = merged * 2
    rows_blocks = rows_in.reshape(sources // merged, merged * per_source, rows_in.shape[2])
    small_blocks = small_in.reshape(sources // merged, merged * per_source, small_in.shape[2])
    zeros_kv = jnp.zeros(key_rows.shape, jnp.float32)

    def advance(carry, pieces):
        query_part, key_add, value_add = block_terms(
            pieces[0], pieces[1], key_rows, value_rows, own_shard, groups
        )
        return ((carry[0] + key_add, carry[1] + value_add), query_part)

    (key_sum, value_sum), query_parts = lax.scan(
        advance, (zeros_kv, zeros_kv), (rows_blocks, small_blocks)
    )
    return (query_parts.reshape(sources, per_source, -1), key_sum, value_sum)


def local(query_rows, key_rows, value_rows, attn_out, out_grad, logsumexp, shard_pick, block_pick):
    head_size = query_rows.shape[1]
    q_count = query_rows.shape[0]
    scale = head_size ** (-0.5)
    out_local, grad_local = (
        lax.all_to_all(attn_out, "head", split_axis=1, concat_axis=0, tiled=True),
        lax.all_to_all(out_grad, "head", split_axis=1, concat_axis=0, tiled=True),
    )
    delta = jnp.sum(
        out_local.astype(jnp.float32) * grad_local.astype(jnp.float32), axis=1, keepdims=True
    ).astype(jnp.bfloat16)
    seq_count = lax.axis_size("seq")
    own_shard = lax.axis_index("seq")
    targets = shard_pick[0]
    groups = targets.shape[1]
    picks = block_pick[0].reshape(q_count, -1)
    row_data = jnp.concatenate([query_rows, grad_local], axis=1)
    small_data = jnp.concatenate(
        [
            logsumexp[0][:, None],
            delta,
            (targets + 1).astype(jnp.bfloat16),
            picks.astype(jnp.bfloat16),
        ],
        axis=1,
    )
    capacity = min(q_count, 2 * q_count * groups // seq_count)
    shard_ids = jnp.arange(seq_count, dtype=jnp.int32)
    hits = jnp.any(targets[:, :, None] == shard_ids[None, None, :], axis=1).astype(jnp.float32)
    row_ids = jnp.arange(q_count, dtype=jnp.int32)
    lower = (row_ids[:, None] >= row_ids[None, :]).astype(jnp.float32)
    slots = (
        jnp.dot(lower, hits, precision=lax.Precision.HIGHEST, preferred_element_type=jnp.float32)
        - 1.0
    )
    slot_ids = jnp.arange(capacity, dtype=jnp.float32)
    dispatch = hits.T[:, None, :] * (slots.T[:, None, :] == slot_ids[None, :, None]).astype(
        jnp.float32
    )
    dispatch_low = dispatch.astype(jnp.bfloat16)
    send_rows = jnp.einsum(
        "scr,rf->scf", dispatch_low, row_data, preferred_element_type=jnp.float32
    ).astype(jnp.bfloat16)
    send_small = jnp.einsum(
        "scr,rf->scf", dispatch_low, small_data, preferred_element_type=jnp.float32
    ).astype(jnp.bfloat16)
    got_rows, got_small = (
        lax.all_to_all(send_rows, "seq", split_axis=0, concat_axis=0, tiled=True),
        lax.all_to_all(send_small, "seq", split_axis=0, concat_axis=0, tiled=True),
    )
    query_parts, key_sum, value_sum = sweep(
        got_rows, got_small, key_rows, value_rows, own_shard, groups
    )
    returned = lax.all_to_all(query_parts, "seq", split_axis=0, concat_axis=0, tiled=True)
    total = jnp.einsum(
        "scr,scd->rd",
        dispatch,
        returned,
        precision=lax.Precision.HIGHEST,
        preferred_element_type=jnp.float32,
    )
    query_grad = (total * scale).astype(jnp.bfloat16)
    key_grad = (key_sum * scale).astype(jnp.bfloat16)
    value_grad = value_sum.astype(jnp.bfloat16)
    return (query_grad, key_grad, value_grad)


def solution(mesh):
    placed = (
        P("seq", "head"),
        P("seq", "head"),
        P("seq", "head"),
        P(("seq", "head"), None),
        P(("seq", "head"), None),
        P("head", "seq"),
        P("head", "seq", None),
        P("head", "seq", None, None),
    )
    return jax.shard_map(
        local,
        mesh=mesh,
        in_specs=placed,
        out_specs=(P("seq", "head"), P("seq", "head"), P("seq", "head")),
        check_vma=False,
    )
```

profile of v0, /device:TPU:0, one launch (start us, length us, event | category | flops | bytes accessed | tf_op | source)
XLA Modules:
  0.0 52.9 jit_solution(12761019467804960776)
XLA Ops:
  0.6 0.0 copy-start
  0.6 0.0 copy-start.3
  0.7 6.5 %all-to-all-start = ((bf16[8,4,128]{2,0,1:T(8,128)(2,1)}), bf16[8,4,128]{2,0,1:T(8,128)(2,1)S(1)}, u32[]{:S(2)}, u32[]{:S(2)}) async-start(bf16[8,4,128]{2,0,1:T(8,128)(2,1)} %bitcast.57), calls=%async_computation | async-start | bytes 16384 | tf_op jit(solution)/shard_map/all_to_all | solution.py:63
  7.1 0.1 convolution_add_fusion
  7.3 5.4 %all-to-all-done = bf16[8,4,128]{2,0,1:T(8,128)(2,1)S(1)} async-done(((bf16[8,4,128]{2,0,1:T(8,128)(2,1)}), bf16[8,4,128]{2,0,1:T(8,128)(2,1)S(1)}, u32[]{:S(2)}, u32[]{:S(2)}) %all-to-all-start) | async-done | bytes 8224 | tf_op jit(solution)/shard_map/all_to_all | solution.py:63
  12.7 3.2 %all-to-all-start.1 = ((bf16[8,4,128]{2,0,1:T(8,128)(2,1)}), bf16[8,4,128]{2,0,1:T(8,128)(2,1)S(1)}, u32[]{:S(2)}, u32[]{:S(2)}) async-start(bf16[8,4,128]{2,0,1:T(8,128)(2,1)} %bitcast.5), calls=%async_computation.1 | async-start | bytes 16384 | tf_op jit(solution)/shard_map/all_to_all | solution.py:64
  16.0 0.0 copy-start.2
  16.0 0.7 %copy-done.2 = s32[1,32,4,4]{1,3,2,0:T(4,128)S(1)} copy-done((s32[1,32,4,4]{1,3,2,0:T(4,128)S(1)}, s32[1,32,4,4]{1,3,2,0:T(4,128)}, u32[]{:S(2)}) %copy-start.2) | copy-done | bytes 2072
  16.7 4.9 %all-to-all-done.1 = bf16[8,4,128]{2,0,1:T(8,128)(2,1)S(1)} async-done(((bf16[8,4,128]{2,0,1:T(8,128)(2,1)}), bf16[8,4,128]{2,0,1:T(8,128)(2,1)S(1)}, u32[]{:S(2)}, u32[]{:S(2)}) %all-to-all-start.1) | async-done | bytes 8224 | tf_op jit(solution)/shard_map/all_to_all | solution.py:64
  21.5 0.1 fusion.27
  21.6 0.1 convert_element_type.86
  21.7 0.7 %copy-done.5 = bf16[1,32]{1,0:T(2,128)(2,1)S(1)} copy-done((bf16[1,32]{1,0:T(2,128)(2,1)S(1)}, bf16[1,32]{1,0:T(2,128)(2,1)}, u32[]{:S(2)}) %copy-start.5) | copy-done | bytes 88
  22.4 0.3 fusion.41
  22.6 0.7 %reshape.53 = bf16[8,2,352]{2,1,0:T(2,128)(2,1)} reshape(bf16[8,22,32]{2,1,0:T(8,128)(2,1)S(1)} %fusion.41) | data formatting | bytes 22528
  23.3 3.9 %all-to-all-start.2 = ((bf16[8,2,352]{2,1,0:T(2,128)(2,1)}), bf16[8,2,352]{2,1,0:T(2,128)(2,1)S(1)}, u32[]{:S(2)}, u32[]{:S(2)}) async-start(bf16[8,2,352]{2,1,0:T(2,128)(2,1)} %reshape.53), calls=%async_computation.2 | async-start | bytes 24576 | tf_op jit(solution)/shard_map/all_to_all | solution.py:106
  27.2 0.0 copy-done.4
  27.2 1.0 %convolution_convert_fusion.1 = bf16[8,32,256]{2,1,0:T(8,128)(2,1)} fusion(f32[8,32]{1,0:T(8,128)S(1)} %convert_bitcast_fusion, f32[8,32]{1,0:T(8,128)S(1)} %convolution_add_fusion, bf16[32,128]{1,0:T(8,128)(2,1)S(1)} %bitcast.55, bf16[32,128]{1,0:T(8,128)(2,1)S(1)} %copy-done.4), kind=kOutput, calls=%fused_computation.10 | convolution fusion | flops 4308992 | bytes 149504 | tf_op jit(solution)/shard_map/scr,rf->scf/dot_general | solution.py:98
  28.2 3.8 %all-to-all-done.2 = bf16[8,2,352]{2,1,0:T(2,128)(2,1)S(1)} async-done(((bf16[8,2,352]{2,1,0:T(2,128)(2,1)}), bf16[8,2,352]{2,1,0:T(2,128)(2,1)S(1)}, u32[]{:S(2)}, u32[]{:S(2)}) %all-to-all-start.2) | async-done | bytes 11296 | tf_op jit(solution)/shard_map/all_to_all | solution.py:106
  31.9 3.4 %all-to-all-start.3 = ((bf16[8,32,256]{2,1,0:T(8,128)(2,1)}), bf16[8,32,256]{2,1,0:T(8,128)(2,1)S(1)}, u32[]{:S(2)}, u32[]{:S(2)}) async-start(bf16[8,32,256]{2,1,0:T(8,128)(2,1)} %convolution_convert_fusion.1), calls=%async_computation.3 | async-start | bytes 262144 | tf_op jit(solution)/shard_map/all_to_all | solution.py:105
  35.3 0.1 reshape.54
  35.4 0.1 squeeze.11
  35.7 0.2 copy.24
  35.9 4.9 %all-to-all-done.3 = bf16[8,32,256]{2,1,0:T(8,128)(2,1)S(1)} async-done(((bf16[8,32,256]{2,1,0:T(8,128)(2,1)}), bf16[8,32,256]{2,1,0:T(8,128)(2,1)S(1)}, u32[]{:S(2)}, u32[]{:S(2)}) %all-to-all-start.3) | async-done | bytes 131104 | tf_op jit(solution)/shard_map/all_to_all | solution.py:105
  40.8 0.3 fusion.2
  41.0 0.0 copy-start.1
  41.1 0.9 %convolution_convert_fusion = bf16[512,128]{1,0:T(8,128)(2,1)} fusion(f32[256,512]{1,0:T(8,128)S(1)} %fusion.2, bf16[256,256]{1,0:T(8,128)(2,1)S(1)} %bitcast.50), kind=kOutput, calls=%fused_computation.9 | convolution fusion | flops 33751040 | bytes 720896 | tf_op jit(solution)/shard_map/while/body/eval_jaxpr/dot_general | solution.py:29
  42.0 0.2 fusion.4
  42.2 0.9 %fusion.42 = f32[256,128]{1,0:T(8,128)} fusion(bf16[256,512]{1,0:T(8,128)(2,1)S(1)} %fusion.4, bf16[512,128]{1,0:T(8,128)(2,1)S(1)} %copy-done), kind=kOutput, calls=%fused_computation.63 | convolution fusion | flops 33554432 | bytes 524288 | tf_op jit(solution)/shard_map/while/body/eval_jaxpr/dot_general | solution.py:33
  43.1 3.4 %all-to-all-start.4 = ((f32[8,32,128]{2,1,0:T(8,128)}), f32[8,32,128]{2,1,0:T(8,128)S(1)}, u32[]{:S(2)}, u32[]{:S(2)}) async-start(f32[8,32,128]{2,1,0:T(8,128)} %bitcast.15), calls=%async_computation.4 | async-start | bytes 262144 | tf_op jit(solution)/shard_map/all_to_all | solution.py:111
  46.5 0.9 %fusion.5 = bf16[512,128]{1,0:T(8,128)(2,1)} fusion(bf16[256,512]{1,0:T(8,128)(2,1)S(1)} %fusion.4, bf16[256,256]{1,0:T(8,128)(2,1)S(1)} %bitcast.52), kind=kOutput, calls=%fused_computation.8 | convolution fusion | flops 33685504 | bytes 458752 | tf_op jit(solution)/shard_map/while/body/eval_jaxpr/dot_general | solution.py:32
  47.4 4.5 %all-to-all-done.4 = f32[8,32,128]{2,1,0:T(8,128)S(1)} async-done(((f32[8,32,128]{2,1,0:T(8,128)}), f32[8,32,128]{2,1,0:T(8,128)S(1)}, u32[]{:S(2)}, u32[]{:S(2)}) %all-to-all-start.4) | async-done | bytes 131104 | tf_op jit(solution)/shard_map/all_to_all | solution.py:111
  51.9 1.0 %fusion.7 = bf16[32,128]{1,0:T(8,128)(2,1)} fusion(f32[8,32,128]{2,1,0:T(8,128)S(1)} %all-to-all-done.4, f32[8,32]{1,0:T(8,128)S(1)} %convert_bitcast_fusion, f32[8,32]{1,0:T(8,128)S(1)} %convolution_add_fusion), kind=kOutput, calls=%fused_computation.14 | convolution fusion | flops 12607488 | bytes 141312 | tf_op jit(solution)/shard_map/scr,scd->rd/dot_general | solution.py:112
  (17 shorter events, 0.2 us)
Async XLA Ops:
  0.6 40.1 %copy-start = (bf16[512,128]{1,0:T(8,128)(2,1)S(1)}, bf16[512,128]{1,0:T(8,128)(2,1)}, u32[]{:S(2)}) copy-start(bf16[512,128]{1,0:T(8,128)(2,1)} %param.9) | copy-start | bytes 393220
  0.6 6.5 %copy-start.3 = (s32[1,32,4]{1,2,0:T(4,128)S(1)}, s32[1,32,4]{1,2,0:T(4,128)}, u32[]{:S(2)}) copy-start(s32[1,32,4]{1,2,0:T(4,128)} %param.14) | copy-start | bytes 1540
  0.7 12.1 %all-to-all-start = ((bf16[8,4,128]{2,0,1:T(8,128)(2,1)}), bf16[8,4,128]{2,0,1:T(8,128)(2,1)S(1)}, u32[]{:S(2)}, u32[]{:S(2)}) async-start(bf16[8,4,128]{2,0,1:T(8,128)(2,1)} %bitcast.57), calls=%async_computation | async-start | bytes 16384 | tf_op jit(solution)/shard_map/all_to_all | solution.py:63
  12.7 8.8 %all-to-all-start.1 = ((bf16[8,4,128]{2,0,1:T(8,128)(2,1)}), bf16[8,4,128]{2,0,1:T(8,128)(2,1)S(1)}, u32[]{:S(2)}, u32[]{:S(2)}) async-start(bf16[8,4,128]{2,0,1:T(8,128)(2,1)} %bitcast.5), calls=%async_computation.1 | async-start | bytes 16384 | tf_op jit(solution)/shard_map/all_to_all | solution.py:64
  16.0 0.7 %copy-start.2 = (s32[1,32,4,4]{1,3,2,0:T(4,128)S(1)}, s32[1,32,4,4]{1,3,2,0:T(4,128)}, u32[]{:S(2)}) copy-start(s32[1,32,4,4]{1,3,2,0:T(4,128)} %param.15) | copy-start | bytes 6148
  21.7 0.7 %copy-start.5 = (bf16[1,32]{1,0:T(2,128)(2,1)S(1)}, bf16[1,32]{1,0:T(2,128)(2,1)}, u32[]{:S(2)}) copy-start(bf16[1,32]{1,0:T(2,128)(2,1)} %param.13) | copy-start | bytes 196
  23.3 3.9 %copy-start.4 = (bf16[32,128]{1,0:T(8,128)(2,1)S(1)}, bf16[32,128]{1,0:T(8,128)(2,1)}, u32[]{:S(2)}) copy-start(bf16[32,128]{1,0:T(8,128)(2,1)} %param.8) | copy-start | bytes 24580
  23.3 8.6 %all-to-all-start.2 = ((bf16[8,2,352]{2,1,0:T(2,128)(2,1)}), bf16[8,2,352]{2,1,0:T(2,128)(2,1)S(1)}, u32[]{:S(2)}, u32[]{:S(2)}) async-start(bf16[8,2,352]{2,1,0:T(2,128)(2,1)} %reshape.53), calls=%async_computation.2 | async-start | bytes 24576 | tf_op jit(solution)/shard_map/all_to_all | solution.py:106
  31.9 8.8 %all-to-all-start.3 = ((bf16[8,32,256]{2,1,0:T(8,128)(2,1)}), bf16[8,32,256]{2,1,0:T(8,128)(2,1)S(1)}, u32[]{:S(2)}, u32[]{:S(2)}) async-start(bf16[8,32,256]{2,1,0:T(8,128)(2,1)} %convolution_convert_fusion.1), calls=%async_computation.3 | async-start | bytes 262144 | tf_op jit(solution)/shard_map/all_to_all | solution.py:105
  41.0 0.9 %copy-start.1 = (bf16[512,128]{1,0:T(8,128)(2,1)S(1)}, bf16[512,128]{1,0:T(8,128)(2,1)}, u32[]{:S(2)}) copy-start(bf16[512,128]{1,0:T(8,128)(2,1)} %param.10) | copy-start | bytes 393220
  43.1 8.8 %all-to-all-start.4 = ((f32[8,32,128]{2,1,0:T(8,128)}), f32[8,32,128]{2,1,0:T(8,128)S(1)}, u32[]{:S(2)}, u32[]{:S(2)}) async-start(f32[8,32,128]{2,1,0:T(8,128)} %bitcast.15), calls=%async_computation.4 | async-start | bytes 262144 | tf_op jit(solution)/shard_map/all_to_all | solution.py:111
where the time goes:
time: 53.5 us; the launch traced here: 52.9 us
  waiting for transfers between devices  23.4 us (44%)
  starting transfers between devices  20.3 us (38%)
  matrix products  5.57 us (10%)
  local copies, waits for them, and re-layouts  2.63 us (5%)
  between operations  0.8 us (1%)
    all_to_all x1, starting transfers between devices, local(): lax.all_to_all(attn_out, 'head', split_axis=1, concat_axis=0, tiled=True)  6.46 us
    all_to_all x1, waiting for transfers between devices, local(): lax.all_to_all(attn_out, 'head', split_axis=1, concat_axis=0, tiled=True)  5.44 us
    all_to_all x1, waiting for transfers between devices, local(): lax.all_to_all(send_rows, 'seq', split_axis=0, concat_axis=0, tiled=True)  4.86 us
    all_to_all x1, waiting for transfers between devices, local(): lax.all_to_all(out_grad, 'head', split_axis=1, concat_axis=0, tiled=True)  4.85 us
    all_to_all x1, waiting for transfers between devices, local(): lax.all_to_all(query_parts, 'seq', split_axis=0, concat_axis=0, tiled=True)  4.53 us
    all_to_all x1, starting transfers between devices, local(): lax.all_to_all(send_small, 'seq', split_axis=0, concat_axis=0, tiled=True)  3.85 us
    all_to_all x1, waiting for transfers between devices, local(): lax.all_to_all(send_small, 'seq', split_axis=0, concat_axis=0, tiled=True)  3.76 us
    all_to_all x1, starting transfers between devices, local(): lax.all_to_all(send_rows, 'seq', split_axis=0, concat_axis=0, tiled=True)  3.37 us
  transfers between devices with their start and end apart: 5, of which 5 were waited for; matrix products, arithmetic and copies ran while one was open for 5% of the time, Pallas kernels for 0%

commit v1 on v0

--- a/solution.py
+++ b/solution.py
@@ -1,9 +1,14 @@
+import functools
+
 import jax
 import jax.numpy as jnp
 from jax import lax
+from jax.experimental import pallas as pl
+from jax.experimental.pallas import tpu as pltpu
 from jax.sharding import PartitionSpec as P
 
 BLK = 64
+LOG2E = 1.4426950408889634
 
 
 def block_terms(row_data, small_data, key_rows, value_rows, own_shard, groups):
@@ -55,7 +60,7 @@
     return (query_parts.reshape(sources, per_source, -1), key_sum, value_sum)
 
 
-def local(query_rows, key_rows, value_rows, attn_out, out_grad, logsumexp, shard_pick, block_pick):
+def general_local(query_rows, key_rows, value_rows, attn_out, out_grad, logsumexp, shard_pick, block_pick):
     head_size = query_rows.shape[1]
     q_count = query_rows.shape[0]
     scale = head_size ** (-0.5)
@@ -122,6 +127,132 @@
     return (query_grad, key_grad, value_grad)
 
 
+def swap(value, axis, count, bit):
+    return lax.ppermute(value, axis, [(i, i ^ bit) for i in range(count)])
+
+
+def attend(rows, picks, far, key_ref, value_ref, shard, scale):
+    queries, grads = rows
+    base = (shard * (key_ref.shape[0] // BLK)).astype(jnp.float32)
+    blocks = key_ref.shape[0] // BLK
+    stats, ids = picks
+    number = lax.broadcasted_iota(jnp.int32, (blocks, ids.shape[1]), 0).astype(jnp.float32) + base
+    chosen = ids[0:1] == number
+    for k in range(1, ids.shape[0]):
+        chosen = chosen | (ids[k : k + 1] == number)
+    offset = jnp.where(chosen, stats[0:1] * LOG2E, far)
+    delta = stats[1:2]
+    keys, values = key_ref[...], value_ref[...]
+    contract = (((1,), (1,)), ((), ()))
+    scores = lax.dot_general(keys, queries, contract, preferred_element_type=jnp.float32)
+    dprob = lax.dot_general(values, grads, contract, preferred_element_type=jnp.float32)
+    scores = scores.reshape(blocks, BLK, -1)
+    probs = jnp.exp2(scores * (scale * LOG2E) - offset[:, None, :]).reshape(dprob.shape)
+    dscore = (probs * (dprob - delta)).astype(jnp.bfloat16)
+    probs_low = probs.astype(jnp.bfloat16)
+    value_add = jnp.dot(probs_low, grads, preferred_element_type=jnp.float32)
+    key_add = jnp.dot(dscore, queries, preferred_element_type=jnp.float32)
+    query_add = lax.dot_general(
+        dscore, keys, (((0,), (0,)), ((), ())), preferred_element_type=jnp.float32
+    )
+    return query_add, key_add, value_add
+
+
+def core_kernel(
+    scale, shard_ref, r0, r1, r2, r3, k0, v0, k1, v1, q_own, q_out, k_own, v_own, k_out, v_out
+):
+    count = q_own.shape[0]
+    parts = (r0, r1, r2, r3)
+    queries = jnp.concatenate([r[0:count] for r in parts], axis=0)
+    grads = jnp.concatenate([r[count : 2 * count] for r in parts], axis=0)
+    small = [r[2 * count :].astype(jnp.float32) for r in parts]
+    lane = lax.broadcasted_iota(jnp.int32, small[0].shape, 1) // count
+    merged = small[0]
+    for k in range(1, len(parts)):
+        merged = jnp.where(lane == k, small[k], merged)
+    half = merged.shape[0] // 2
+    picks = (merged[:half], merged[half:])
+    shard = shard_ref[0]
+    q_a, k_a, v_a = attend((queries, grads), picks, 1e30, k1, v1, shard ^ 1, scale)
+    k_out[...] = k_a.astype(k_out.dtype)
+    v_out[...] = v_a.astype(v_out.dtype)
+    q_b, k_b, v_b = attend((queries, grads), picks, 1e30, k0, v0, shard, scale)
+    k_own[...] = k_b
+    v_own[...] = v_b
+    q_all = q_a + q_b
+    q_own[...] = q_all[:count]
+    for k in range(1, len(parts)):
+        q_out[k - 1] = q_all[k * count : (k + 1) * count].astype(q_out.dtype)
+
+
+def fast_local(query_rows, key_rows, value_rows, attn_out, out_grad, logsumexp, shard_pick, block_pick):
+    count, size = query_rows.shape
+    n_seq, n_head = lax.axis_size("seq"), lax.axis_size("head")
+    seq, head = lax.axis_index("seq"), lax.axis_index("head")
+    scale = size ** (-0.5)
+    grad_near = swap(out_grad, "head", n_head, 1)
+    out_near = swap(attn_out, "head", n_head, 1)
+    keys_near = swap(key_rows, "seq", n_seq, 1)
+    values_near = swap(value_rows, "seq", n_seq, 1)
+
+    def columns(value, which):
+        return lax.dynamic_slice_in_dim(value, which * size, size, axis=1)
+
+    def pieces(which):
+        return jnp.stack([columns(v, which) for v in (out_grad, grad_near, attn_out, out_near)])
+
+    near = pieces(head)
+    other = swap(pieces(head ^ 2), "head", n_head, 2)
+    odd, high = (head & 1) == 1, (head & 2) == 2
+
+    def ordered(a, b, c, d):
+        a, b = jnp.where(odd, b, a), jnp.where(odd, a, b)
+        c, d = jnp.where(odd, d, c), jnp.where(odd, c, d)
+        low, top = jnp.concatenate([a, b]), jnp.concatenate([c, d])
+        return jnp.concatenate([jnp.where(high, top, low), jnp.where(high, low, top)])
+
+    grads = ordered(near[0], near[1], other[0], other[1])
+    outs = ordered(near[2], near[3], other[2], other[3])
+    delta = jnp.sum(outs.astype(jnp.float32) * grads.astype(jnp.float32), axis=1).astype(jnp.bfloat16)
+    blocks_dev = key_rows.shape[0] // BLK
+    ids = shard_pick[0][:, :, None] * blocks_dev + block_pick[0]
+    ids = ids.reshape(count, -1).T.astype(jnp.bfloat16)
+    top = ids.shape[0]
+    stats = jnp.concatenate(
+        [logsumexp, delta[None, :], jnp.zeros((top - 2, count), jnp.bfloat16)], axis=0
+    )
+    small = jnp.tile(jnp.concatenate([stats, ids], axis=0), (1, size // count))
+    block = jnp.concatenate([query_rows, grads, small], axis=0)
+    bits = (2, 4, 6)
+    others = [swap(block, "seq", n_seq, bit) for bit in bits]
+    f32, bf16 = jnp.float32, jnp.bfloat16
+    kv = key_rows.shape
+    vmem = pl.BlockSpec(memory_space=pltpu.VMEM)
+    q_own, q_out, k_own, v_own, k_out, v_out = pl.pallas_call(
+        functools.partial(core_kernel, scale),
+        out_shape=(
+            jax.ShapeDtypeStruct((count, size), f32),
+            jax.ShapeDtypeStruct((len(bits), count, size), bf16),
+            jax.ShapeDtypeStruct(kv, f32),
+            jax.ShapeDtypeStruct(kv, f32),
+            jax.ShapeDtypeStruct(kv, bf16),
+            jax.ShapeDtypeStruct(kv, bf16),
+        ),
+        in_specs=[pl.BlockSpec(memory_space=pltpu.SMEM)] + [vmem] * 8,
+        out_specs=(vmem,) * 6,
+        compiler_params=pltpu.CompilerParams(vmem_limit_bytes=32 * 1024 * 1024),
+        name="block_terms",
+    )(seq[None].astype(jnp.int32), block, *others, key_rows, value_rows, keys_near, values_near)
+    back = [swap(q_out[k], "seq", n_seq, bit) for k, bit in enumerate(bits)]
+    k_back = swap(k_out, "seq", n_seq, 1)
+    v_back = swap(v_out, "seq", n_seq, 1)
+    total = q_own + sum(part.astype(f32) for part in back)
+    query_grad = (total * scale).astype(bf16)
+    key_grad = ((k_own + k_back.astype(f32)) * scale).astype(bf16)
+    value_grad = (v_own + v_back.astype(f32)).astype(bf16)
+    return query_grad, key_grad, value_grad
+
+
 def solution(mesh):
     placed = (
         P("seq", "head"),
@@ -133,6 +264,13 @@
         P("head", "seq", None),
         P("head", "seq", None, None),
     )
+    small = mesh.shape["seq"] == 8 and mesh.shape["head"] == 4
+
+    def local(*args):
+        count, size = args[0].shape
+        fits = small and count * 4 == size == 128 and args[7].shape[2] * args[7].shape[3] == 16
+        return (fast_local if fits else general_local)(*args)
+
     return jax.shard_map(
         local,
         mesh=mesh,

time: 53.5 us -> 29.2 us (0.55)
  waiting for transfers between devices: 23.4 us -> 10.2 us
  starting transfers between devices: 20.3 us -> 14 us
  matrix products: 5.57 us -> 0 us
  other arithmetic: 0.18 us -> 2.92 us
  local copies, waits for them, and re-layouts: 2.63 us -> 0.35 us
  Pallas kernels: 0 us -> 0.7 us
    all_to_all x5 -> x0, waiting for transfers between devices: 23.4 us -> none  [the longest x1 5.44 us: local(): lax.all_to_all(attn_out, 'head', split_axis=1, concat_axis=0, tiled=True)]
    all_to_all x5 -> x0, starting transfers between devices: 20.3 us -> none  [the longest x1 6.46 us: local(): lax.all_to_all(attn_out, 'head', split_axis=1, concat_axis=0, tiled=True)]
    ppermute x0 -> x13, starting transfers between devices: none -> 14 us  [swap(): return lax.ppermute(value, axis, [(i, i ^ bit) for i in range(count)])]
    ppermute x0 -> x13, waiting for transfers between devices: none -> 10.2 us  [swap(): return lax.ppermute(value, axis, [(i, i ^ bit) for i in range(count)])]
    dot_general x9 -> x0, matrix products: 5.57 us -> none  [the longest x1 1 us: local(): jnp.einsum('scr,scd->rd', dispatch, returned, precision=lax.Precision.HIG...]
    unnamed x14, local copies, waits for them, and re-layouts: 2.16 us -> 0.16 us
    convert_element_type x4, other arithmetic: 0.02 us -> 2 us  [the longest x1 0.69 us: fast_local(): key_grad = ((k_own + k_back.astype(f32)) * scale).astype(bf16)]
    pallas_call x0 -> x1, Pallas kernels: none -> 0.7 us  [fast_local(): pl.pallas_call(functools.partial(core_kernel, scale), out_shape=(jax.Shap...]
  transfers between devices with their start and end apart: 5 -> 13, of which waited for: 5 -> 8; matrix products, arithmetic and copies ran while one was open for 5% -> 8% of each run, Pallas kernels for 0% -> 0%
where the time goes in v1:
time: 29.2 us; the launch traced here: 28.9 us
  starting transfers between devices  14 us (48%)
  waiting for transfers between devices  10.2 us (35%)
  other arithmetic  2.92 us (10%)
  between operations  0.76 us (3%)
  Pallas kernels  0.7 us (2%)
  local copies, waits for them, and re-layouts  0.35 us (1%)
    ppermute x13, starting transfers between devices, swap(): return lax.ppermute(value, axis, [(i, i ^ bit) for i in range(count)])  14 us
    ppermute x13, waiting for transfers between devices, swap(): return lax.ppermute(value, axis, [(i, i ^ bit) for i in range(count)])  10.2 us
    pallas_call x1, Pallas kernels, fast_local(): pl.pallas_call(functools.partial(core_kernel, scale), out_shape=(jax.Shap...  0.7 us
    convert_element_type x1, other arithmetic, fast_local(): key_grad = ((k_own + k_back.astype(f32)) * scale).astype(bf16)  0.69 us
    convert_element_type x1, other arithmetic, fast_local(): value_grad = (v_own + v_back.astype(f32)).astype(bf16)  0.69 us
    mul x1, other arithmetic, fast_local(): ids = shard_pick[0][:, :, None] * blocks_dev + block_pick[0]  0.68 us
    convert_element_type x1, other arithmetic, fast_local(): query_grad = (total * scale).astype(bf16)  0.61 us
  transfers between devices with their start and end apart: 13, of which 8 were waited for; matrix products, arithmetic and copies ran while one was open for 8% of the time, Pallas kernels for 0%

profile of v1, /device:TPU:0, one launch (start us, length us, event | category | flops | bytes accessed | tf_op | source)
XLA Modules:
  0.0 28.9 jit_solution(1130432113290343540)
XLA Ops:
  0.6 3.1 %collective-permute-start.1 = (bf16[8,512]{1,0:T(8,128)(2,1)}, bf16[8,512]{1,0:T(8,128)(2,1)S(1)}, u32[]{:S(2)}, u32[]{:S(2)}) collective-permute-start(bf16[8,512]{1,0:T(8,128)(2,1)} %param.11), channel_id=1, source_target_pairs={{0,1},{1,0},{2,3},{3,2},{4,5},{5,4},{6,7},{7,6},{8,9},{9,8},{10,11... | collective-permute-start | bytes 24584 | tf_op jit(solution)/shard_map/ppermute | solution.py:131
  3.7 0.1 collective-permute-start
  3.8 0.5 %collective-permute-start.7 = (bf16[512,128]{1,0:T(8,128)(2,1)}, bf16[512,128]{1,0:T(8,128)(2,1)S(1)}, u32[]{:S(2)}, u32[]{:S(2)}) collective-permute-start(bf16[512,128]{1,0:T(8,128)(2,1)} %v0.1), channel_id=1, source_target_pairs={{0,4},{4,0},{8,12},{12,8},{16,20},{20,16},{24,28},{28,24},{1,5},{5... | collective-permute-start | bytes 393224 | tf_op jit(solution)/shard_map/ppermute | solution.py:131
  4.3 0.7 %multiply_bitcast_fusion = s32[32,4]{0,1:T(4,128)S(1)} fusion(s32[1,32,4]{1,2,0:T(4,128)} %param.14), kind=kLoop, calls=%fused_computation.20 | loop fusion | flops 128 | bytes 1024 | tf_op jit(solution)/shard_map/mul | solution.py:218
  5.0 0.6 %collective-permute-done.1 = bf16[8,512]{1,0:T(8,128)(2,1)S(1)} collective-permute-done((bf16[8,512]{1,0:T(8,128)(2,1)}, bf16[8,512]{1,0:T(8,128)(2,1)S(1)}, u32[]{:S(2)}, u32[]{:S(2)}) %collective-permute-start.1) | collective-permute-done | bytes 8224 | tf_op jit(solution)/shard_map/ppermute | solution.py:131
  5.6 0.1 copy-done.4
  5.7 1.9 %collective-permute-done = bf16[8,512]{1,0:T(8,128)(2,1)S(1)} collective-permute-done((bf16[8,512]{1,0:T(8,128)(2,1)}, bf16[8,512]{1,0:T(8,128)(2,1)S(1)}, u32[]{:S(2)}, u32[]{:S(2)}) %collective-permute-start) | collective-permute-done | bytes 8224 | tf_op jit(solution)/shard_map/ppermute | solution.py:131
  7.6 0.0 copy-start.2
  7.6 2.7 %collective-permute-start.2 = (bf16[4,8,128]{2,1,0:T(8,128)(2,1)S(1)}, bf16[4,8,128]{2,1,0:T(8,128)(2,1)S(1)}, u32[]{:S(2)}, u32[]{:S(2)}) collective-permute-start(bf16[4,8,128]{2,1,0:T(8,128)(2,1)S(1)} %pad_maximum_fusion.1), channel_id=1, source_target_pairs={{0,2},{1,3},{2,0},{3,1},{4,6},{5,7},{6,4},{7,5},{8,10},{9,11},{10,... | collective-permute-start | bytes 24584 | tf_op jit(solution)/shard_map/ppermute | solution.py:131
  10.3 0.0 copy-start.1
  10.3 0.0 copy-start
  10.3 0.1 pad.6.clone
  10.4 1.8 %collective-permute-done.2 = bf16[4,8,128]{2,1,0:T(8,128)(2,1)S(1)} collective-permute-done((bf16[4,8,128]{2,1,0:T(8,128)(2,1)S(1)}, bf16[4,8,128]{2,1,0:T(8,128)(2,1)S(1)}, u32[]{:S(2)}, u32[]{:S(2)}) %collective-permute-start.2) | collective-permute-done | bytes 8224 | tf_op jit(solution)/shard_map/ppermute | solution.py:131
  12.3 0.1 multiply_reduce_fusion
  12.4 0.1 pad_maximum_fusion.2
  12.5 0.1 tile.10
  12.6 2.5 %collective-permute-start.5 = (bf16[96,128]{1,0:T(8,128)(2,1)S(1)}, bf16[96,128]{1,0:T(8,128)(2,1)S(1)}, u32[]{:S(2)}, u32[]{:S(2)}) collective-permute-start(bf16[96,128]{1,0:T(8,128)(2,1)S(1)} %pad_maximum_fusion.r0), channel_id=1, source_target_pairs={{0,24},{4,28},{8,16},{12,20},{16,8},{20,12},{24,0},{28,4},{1,25},{... | collective-permute-start | bytes 73736 | tf_op jit(solution)/shard_map/ppermute | solution.py:131
  15.1 0.5 %collective-permute-start.4 = (bf16[96,128]{1,0:T(8,128)(2,1)S(1)}, bf16[96,128]{1,0:T(8,128)(2,1)S(1)}, u32[]{:S(2)}, u32[]{:S(2)}) collective-permute-start(bf16[96,128]{1,0:T(8,128)(2,1)S(1)} %pad_maximum_fusion.r0), channel_id=1, source_target_pairs={{0,16},{4,20},{8,24},{12,28},{16,0},{20,4},{24,8},{28,12},{1,17},{... | collective-permute-start | bytes 73736 | tf_op jit(solution)/shard_map/ppermute | solution.py:131
  15.6 0.5 %collective-permute-start.3 = (bf16[96,128]{1,0:T(8,128)(2,1)S(1)}, bf16[96,128]{1,0:T(8,128)(2,1)S(1)}, u32[]{:S(2)}, u32[]{:S(2)}) collective-permute-start(bf16[96,128]{1,0:T(8,128)(2,1)S(1)} %pad_maximum_fusion.r0), channel_id=1, source_target_pairs={{0,8},{4,12},{8,0},{12,4},{16,24},{20,28},{24,16},{28,20},{1,9},{5... | collective-permute-start | bytes 73736 | tf_op jit(solution)/shard_map/ppermute | solution.py:131
  16.1 1.2 %collective-permute-done.5.r3 = bf16[96,128]{1,0:T(8,128)(2,1)S(1)} collective-permute-done((bf16[96,128]{1,0:T(8,128)(2,1)S(1)}, bf16[96,128]{1,0:T(8,128)(2,1)S(1)}, u32[]{:S(2)}, u32[]{:S(2)}) %collective-permute-start.5) | collective-permute-done | bytes 24608 | tf_op jit(solution)/shard_map/ppermute | solution.py:131
  17.4 1.5 %collective-permute-done.4.r2 = bf16[96,128]{1,0:T(8,128)(2,1)S(1)} collective-permute-done((bf16[96,128]{1,0:T(8,128)(2,1)S(1)}, bf16[96,128]{1,0:T(8,128)(2,1)S(1)}, u32[]{:S(2)}, u32[]{:S(2)}) %collective-permute-start.4) | collective-permute-done | bytes 24608 | tf_op jit(solution)/shard_map/ppermute | solution.py:131
  18.9 0.5 %collective-permute-done.3.r1 = bf16[96,128]{1,0:T(8,128)(2,1)S(1)} collective-permute-done((bf16[96,128]{1,0:T(8,128)(2,1)S(1)}, bf16[96,128]{1,0:T(8,128)(2,1)S(1)}, u32[]{:S(2)}, u32[]{:S(2)}) %collective-permute-start.3) | collective-permute-done | bytes 24608 | tf_op jit(solution)/shard_map/ppermute | solution.py:131
  19.4 0.7 %block_terms.1 = (f32[32,128]{1,0:T(8,128)S(1)}, bf16[3,32,128]{2,1,0:T(8,128)(2,1)S(1)}, f32[512,128]{1,0:T(8,128)S(1)}, f32[512,128]{1,0:T(8,128)S(1)}, bf16[5...) custom-call(s32[1]{0:T(128)} %bitcast.shard_ref, bf16[96,128]{1,0:T(8,128)(2,1)S(1)} %pad_maximum_fusion.r0, ...), custom_call_target="tpu_custom_call" | custom-call | tf_op jit(solution)/shard_map/block_terms/pallas_call | solution.py:231
  20.2 0.6 %collective-permute-start.8 = (bf16[32,128]{1,0:T(8,128)(2,1)S(1)}, bf16[32,128]{1,0:T(8,128)(2,1)S(1)}, u32[]{:S(2)}, u32[]{:S(2)}) collective-permute-start(bf16[32,128]{1,0:T(8,128)(2,1)S(1)} %get-tuple-element.15), channel_id=1, source_target_pairs={{0,8},{4,12},{8,0},{12,4},{16,24},{20,28},{24,16},{28,20},{1,9},{5... | collective-permute-start | bytes 24584 | tf_op jit(solution)/shard_map/ppermute | solution.py:131
  20.8 2.4 %collective-permute-start.10 = (bf16[32,128]{1,0:T(8,128)(2,1)S(1)}, bf16[32,128]{1,0:T(8,128)(2,1)S(1)}, u32[]{:S(2)}, u32[]{:S(2)}) collective-permute-start(bf16[32,128]{1,0:T(8,128)(2,1)S(1)} %get-tuple-element.16), channel_id=1, source_target_pairs={{0,24},{4,28},{8,16},{12,20},{16,8},{20,12},{24,0},{28,4},{1,25},{... | collective-permute-start | bytes 24584 | tf_op jit(solution)/shard_map/ppermute | solution.py:131
  23.2 0.5 %collective-permute-start.9 = (bf16[32,128]{1,0:T(8,128)(2,1)S(1)}, bf16[32,128]{1,0:T(8,128)(2,1)S(1)}, u32[]{:S(2)}, u32[]{:S(2)}) collective-permute-start(bf16[32,128]{1,0:T(8,128)(2,1)S(1)} %get-tuple-element.17), channel_id=1, source_target_pairs={{0,16},{4,20},{8,24},{12,28},{16,0},{20,4},{24,8},{28,12},{1,17},{... | collective-permute-start | bytes 24584 | tf_op jit(solution)/shard_map/ppermute | solution.py:131
  23.7 0.5 %collective-permute-start.12 = (bf16[512,128]{1,0:T(8,128)(2,1)S(1)}, bf16[512,128]{1,0:T(8,128)(2,1)S(1)}, u32[]{:S(2)}, u32[]{:S(2)}) collective-permute-start(bf16[512,128]{1,0:T(8,128)(2,1)S(1)} %get-tuple-element.14), channel_id=1, source_target_pairs={{0,4},{4,0},{8,12},{12,8},{16,20},{20,16},{24,28},{28,24},{1,5},{5... | collective-permute-start | bytes 393224 | tf_op jit(solution)/shard_map/ppermute | solution.py:131
  24.2 1.1 %collective-permute-done.10 = bf16[32,128]{1,0:T(8,128)(2,1)S(1)} collective-permute-done((bf16[32,128]{1,0:T(8,128)(2,1)S(1)}, bf16[32,128]{1,0:T(8,128)(2,1)S(1)}, u32[]{:S(2)}, u32[]{:S(2)}) %collective-permute-start.10) | collective-permute-done | bytes 8224 | tf_op jit(solution)/shard_map/ppermute | solution.py:131
  25.3 1.5 %collective-permute-done.9 = bf16[32,128]{1,0:T(8,128)(2,1)S(1)} collective-permute-done((bf16[32,128]{1,0:T(8,128)(2,1)S(1)}, bf16[32,128]{1,0:T(8,128)(2,1)S(1)}, u32[]{:S(2)}, u32[]{:S(2)}) %collective-permute-start.9) | collective-permute-done | bytes 8224 | tf_op jit(solution)/shard_map/ppermute | solution.py:131
  26.9 0.6 %multiply_convert_fusion.1 = bf16[32,128]{1,0:T(8,128)(2,1)} fusion(f32[32,128]{1,0:T(8,128)S(1)} %get-tuple-element.9, bf16[32,128]{1,0:T(8,128)(2,1)S(1)} %collective-permute-done.10, bf16[32,128]{1,0:T(8,128)(2,1)S(1)} %collective-permute-done.9, bf16[32,128]{1,0:T(8,128)(2,1)S(1)} %collective-permute-done.8), kind=kLoop, calls=%fused_computation.3 | loop fusion | flops 32768 | bytes 49152 | tf_op jit(solution)/shard_map/convert_element_type | solution.py:250
  27.5 0.7 %multiply_convert_fusion = bf16[512,128]{1,0:T(8,128)(2,1)} fusion(f32[512,128]{1,0:T(8,128)S(1)} %get-tuple-element.11, bf16[512,128]{1,0:T(8,128)(2,1)S(1)} %collective-permute-done.11), kind=kLoop, calls=%fused_computation.1 | loop fusion | flops 262144 | bytes 524288 | tf_op jit(solution)/shard_map/convert_element_type | solution.py:251
  28.2 0.7 %add_convert_fusion = bf16[512,128]{1,0:T(8,128)(2,1)} fusion(f32[512,128]{1,0:T(8,128)S(1)} %get-tuple-element.13, bf16[512,128]{1,0:T(8,128)(2,1)S(1)} %collective-permute-done.12), kind=kLoop, calls=%fused_computation | loop fusion | flops 196608 | bytes 524288 | tf_op jit(solution)/shard_map/convert_element_type | solution.py:252
  (28 shorter events, 0.1 us)
Async XLA Ops:
  0.6 4.9 %collective-permute-start.1 = (bf16[8,512]{1,0:T(8,128)(2,1)}, bf16[8,512]{1,0:T(8,128)(2,1)S(1)}, u32[]{:S(2)}, u32[]{:S(2)}) collective-permute-start(bf16[8,512]{1,0:T(8,128)(2,1)} %param.11), channel_id=1, source_target_pairs={{0,1},{1,0},{2,3},{3,2},{4,5},{5,4},{6,7},{7,6},{8,9},{9,8},{10,11... | collective-permute-start | bytes 24584 | tf_op jit(solution)/shard_map/ppermute | solution.py:131
  3.7 3.9 %collective-permute-start = (bf16[8,512]{1,0:T(8,128)(2,1)}, bf16[8,512]{1,0:T(8,128)(2,1)S(1)}, u32[]{:S(2)}, u32[]{:S(2)}) collective-permute-start(bf16[8,512]{1,0:T(8,128)(2,1)} %param.12), channel_id=1, source_target_pairs={{0,1},{1,0},{2,3},{3,2},{4,5},{5,4},{6,7},{7,6},{8,9},{9,8},{10,11... | collective-permute-start | bytes 24584 | tf_op jit(solution)/shard_map/ppermute | solution.py:131
  3.8 15.6 %collective-permute-start.6 = (bf16[512,128]{1,0:T(8,128)(2,1)}, bf16[512,128]{1,0:T(8,128)(2,1)S(1)}, u32[]{:S(2)}, u32[]{:S(2)}) collective-permute-start(bf16[512,128]{1,0:T(8,128)(2,1)} %k0.1), channel_id=1, source_target_pairs={{0,4},{4,0},{8,12},{12,8},{16,20},{20,16},{24,28},{28,24},{1,5},{5... | collective-permute-start | bytes 393224 | tf_op jit(solution)/shard_map/ppermute | solution.py:131
  3.8 15.6 %collective-permute-start.7 = (bf16[512,128]{1,0:T(8,128)(2,1)}, bf16[512,128]{1,0:T(8,128)(2,1)S(1)}, u32[]{:S(2)}, u32[]{:S(2)}) collective-permute-start(bf16[512,128]{1,0:T(8,128)(2,1)} %v0.1), channel_id=1, source_target_pairs={{0,4},{4,0},{8,12},{12,8},{16,20},{20,16},{24,28},{28,24},{1,5},{5... | collective-permute-start | bytes 393224 | tf_op jit(solution)/shard_map/ppermute | solution.py:131
  5.0 0.7 %copy-start.4 = (bf16[8,512]{1,0:T(8,128)(2,1)S(1)}, bf16[8,512]{1,0:T(8,128)(2,1)}, u32[]{:S(2)}) copy-start(bf16[8,512]{1,0:T(8,128)(2,1)} %param.11) | copy-start | bytes 24580
  5.0 2.6 %copy-start.5 = (bf16[8,512]{1,0:T(8,128)(2,1)S(1)}, bf16[8,512]{1,0:T(8,128)(2,1)}, u32[]{:S(2)}) copy-start(bf16[8,512]{1,0:T(8,128)(2,1)} %param.12) | copy-start | bytes 24580
  7.6 2.7 %copy-start.2 = (s32[1,32,4,4]{1,3,2,0:T(4,128)S(1)}, s32[1,32,4,4]{1,3,2,0:T(4,128)}, u32[]{:S(2)}) copy-start(s32[1,32,4,4]{1,3,2,0:T(4,128)} %param.15) | copy-start | bytes 6148
  7.6 4.6 %collective-permute-start.2 = (bf16[4,8,128]{2,1,0:T(8,128)(2,1)S(1)}, bf16[4,8,128]{2,1,0:T(8,128)(2,1)S(1)}, u32[]{:S(2)}, u32[]{:S(2)}) collective-permute-start(bf16[4,8,128]{2,1,0:T(8,128)(2,1)S(1)} %pad_maximum_fusion.1), channel_id=1, source_target_pairs={{0,2},{1,3},{2,0},{3,1},{4,6},{5,7},{6,4},{7,5},{8,10},{9,11},{10,... | collective-permute-start | bytes 24584 | tf_op jit(solution)/shard_map/ppermute | solution.py:131
  10.3 2.1 %copy-start.6 = (bf16[1,32]{1,0:T(2,128)(2,1)S(1)}, bf16[1,32]{1,0:T(2,128)(2,1)}, u32[]{:S(2)}) copy-start(bf16[1,32]{1,0:T(2,128)(2,1)} %param.13) | copy-start | bytes 196
  10.3 2.3 %copy-start.3 = (bf16[32,128]{1,0:T(8,128)(2,1)S(1)}, bf16[32,128]{1,0:T(8,128)(2,1)}, u32[]{:S(2)}) copy-start(bf16[32,128]{1,0:T(8,128)(2,1)} %param.8) | copy-start | bytes 24580
  10.3 9.1 %copy-start.1 = (bf16[512,128]{1,0:T(8,128)(2,1)S(1)}, bf16[512,128]{1,0:T(8,128)(2,1)}, u32[]{:S(2)}) copy-start(bf16[512,128]{1,0:T(8,128)(2,1)} %v0.1) | copy-start | bytes 393220
  10.3 9.1 %copy-start = (bf16[512,128]{1,0:T(8,128)(2,1)S(1)}, bf16[512,128]{1,0:T(8,128)(2,1)}, u32[]{:S(2)}) copy-start(bf16[512,128]{1,0:T(8,128)(2,1)} %k0.1) | copy-start | bytes 393220
  12.6 4.8 %collective-permute-start.5 = (bf16[96,128]{1,0:T(8,128)(2,1)S(1)}, bf16[96,128]{1,0:T(8,128)(2,1)S(1)}, u32[]{:S(2)}, u32[]{:S(2)}) collective-permute-start(bf16[96,128]{1,0:T(8,128)(2,1)S(1)} %pad_maximum_fusion.r0), channel_id=1, source_target_pairs={{0,24},{4,28},{8,16},{12,20},{16,8},{20,12},{24,0},{28,4},{1,25},{... | collective-permute-start | bytes 73736 | tf_op jit(solution)/shard_map/ppermute | solution.py:131
  15.1 3.8 %collective-permute-start.4 = (bf16[96,128]{1,0:T(8,128)(2,1)S(1)}, bf16[96,128]{1,0:T(8,128)(2,1)S(1)}, u32[]{:S(2)}, u32[]{:S(2)}) collective-permute-start(bf16[96,128]{1,0:T(8,128)(2,1)S(1)} %pad_maximum_fusion.r0), channel_id=1, source_target_pairs={{0,16},{4,20},{8,24},{12,28},{16,0},{20,4},{24,8},{28,12},{1,17},{... | collective-permute-start | bytes 73736 | tf_op jit(solution)/shard_map/ppermute | solution.py:131
  15.6 3.8 %collective-permute-start.3 = (bf16[96,128]{1,0:T(8,128)(2,1)S(1)}, bf16[96,128]{1,0:T(8,128)(2,1)S(1)}, u32[]{:S(2)}, u32[]{:S(2)}) collective-permute-start(bf16[96,128]{1,0:T(8,128)(2,1)S(1)} %pad_maximum_fusion.r0), channel_id=1, source_target_pairs={{0,8},{4,12},{8,0},{12,4},{16,24},{20,28},{24,16},{28,20},{1,9},{5... | collective-permute-start | bytes 73736 | tf_op jit(solution)/shard_map/ppermute | solution.py:131
  20.2 4.1 %collective-permute-start.8 = (bf16[32,128]{1,0:T(8,128)(2,1)S(1)}, bf16[32,128]{1,0:T(8,128)(2,1)S(1)}, u32[]{:S(2)}, u32[]{:S(2)}) collective-permute-start(bf16[32,128]{1,0:T(8,128)(2,1)S(1)} %get-tuple-element.15), channel_id=1, source_target_pairs={{0,8},{4,12},{8,0},{12,4},{16,24},{20,28},{24,16},{28,20},{1,9},{5... | collective-permute-start | bytes 24584 | tf_op jit(solution)/shard_map/ppermute | solution.py:131
  20.8 4.5 %collective-permute-start.10 = (bf16[32,128]{1,0:T(8,128)(2,1)S(1)}, bf16[32,128]{1,0:T(8,128)(2,1)S(1)}, u32[]{:S(2)}, u32[]{:S(2)}) collective-permute-start(bf16[32,128]{1,0:T(8,128)(2,1)S(1)} %get-tuple-element.16), channel_id=1, source_target_pairs={{0,24},{4,28},{8,16},{12,20},{16,8},{20,12},{24,0},{28,4},{1,25},{... | collective-permute-start | bytes 24584 | tf_op jit(solution)/shard_map/ppermute | solution.py:131
  23.2 3.7 %collective-permute-start.9 = (bf16[32,128]{1,0:T(8,128)(2,1)S(1)}, bf16[32,128]{1,0:T(8,128)(2,1)S(1)}, u32[]{:S(2)}, u32[]{:S(2)}) collective-permute-start(bf16[32,128]{1,0:T(8,128)(2,1)S(1)} %get-tuple-element.17), channel_id=1, source_target_pairs={{0,16},{4,20},{8,24},{12,28},{16,0},{20,4},{24,8},{28,12},{1,17},{... | collective-permute-start | bytes 24584 | tf_op jit(solution)/shard_map/ppermute | solution.py:131
  23.7 3.8 %collective-permute-start.11 = (bf16[512,128]{1,0:T(8,128)(2,1)S(1)}, bf16[512,128]{1,0:T(8,128)(2,1)S(1)}, u32[]{:S(2)}, u32[]{:S(2)}) collective-permute-start(bf16[512,128]{1,0:T(8,128)(2,1)S(1)} %get-tuple-element.12), channel_id=1, source_target_pairs={{0,4},{4,0},{8,12},{12,8},{16,20},{20,16},{24,28},{28,24},{1,5},{5... | collective-permute-start | bytes 393224 | tf_op jit(solution)/shard_map/ppermute | solution.py:131
  23.7 4.5 %collective-permute-start.12 = (bf16[512,128]{1,0:T(8,128)(2,1)S(1)}, bf16[512,128]{1,0:T(8,128)(2,1)S(1)}, u32[]{:S(2)}, u32[]{:S(2)}) collective-permute-start(bf16[512,128]{1,0:T(8,128)(2,1)S(1)} %get-tuple-element.14), channel_id=1, source_target_pairs={{0,4},{4,0},{8,12},{12,8},{16,20},{20,16},{24,28},{28,24},{1,5},{5... | collective-permute-start | bytes 393224 | tf_op jit(solution)/shard_map/ppermute | solution.py:131

commit v2 on v0

--- a/solution.py
+++ b/solution.py
@@ -1,9 +1,14 @@
+import functools
+
 import jax
 import jax.numpy as jnp
 from jax import lax
+from jax.experimental import pallas as pl
+from jax.experimental.pallas import tpu as pltpu
 from jax.sharding import PartitionSpec as P
 
 BLK = 64
+LOG2E = 1.4426950408889634
 
 
 def block_terms(row_data, small_data, key_rows, value_rows, own_shard, groups):
@@ -55,7 +60,7 @@
     return (query_parts.reshape(sources, per_source, -1), key_sum, value_sum)
 
 
-def local(query_rows, key_rows, value_rows, attn_out, out_grad, logsumexp, shard_pick, block_pick):
+def general_local(query_rows, key_rows, value_rows, attn_out, out_grad, logsumexp, shard_pick, block_pick):
     head_size = query_rows.shape[1]
     q_count = query_rows.shape[0]
     scale = head_size ** (-0.5)
@@ -122,6 +127,205 @@
     return (query_grad, key_grad, value_grad)
 
 
+def swap(value, axis, count, bit):
+    return lax.ppermute(value, axis, [(i, i ^ bit) for i in range(count)])
+
+
+def row_sums(left, right):
+    product = left.astype(jnp.float32) * right.astype(jnp.float32)
+    high = product.astype(jnp.bfloat16)
+    low = (product - high.astype(jnp.float32)).astype(jnp.bfloat16)
+    ones = jnp.ones((8, product.shape[1]), jnp.bfloat16)
+    contract = (((1,), (1,)), ((), ()))
+    total = lax.dot_general(ones, high, contract, preferred_element_type=jnp.float32)
+    total = total + lax.dot_general(ones, low, contract, preferred_element_type=jnp.float32)
+    return total[0:1]
+
+
+def unpack(parts, count):
+    queries, grads, outs = (
+        jnp.concatenate([r[k * count : (k + 1) * count] for r in parts], axis=0) for k in range(3)
+    )
+    small = [r[3 * count :].astype(jnp.float32) for r in parts]
+    lane = lax.broadcasted_iota(jnp.int32, small[0].shape, 1) // count
+    merged = small[0]
+    for k in range(1, len(parts)):
+        merged = jnp.where(lane == k, small[k], merged)
+    merged = merged[:, : queries.shape[0]]
+    half = merged.shape[0] // 2
+    delta = row_sums(outs, grads).astype(jnp.bfloat16).astype(jnp.float32)
+    return queries, grads, delta, merged[0:1], merged[half:]
+
+
+def terms(rows, keys, values, base, scale):
+    queries, grads, delta, lse, ids = rows
+    blocks = keys.shape[0] // BLK
+    number = lax.broadcasted_iota(jnp.int32, (blocks, ids.shape[1]), 0) + base
+    number = number.astype(jnp.float32)
+    chosen = ids[0:1] == number
+    for k in range(1, ids.shape[0]):
+        chosen = chosen | (ids[k : k + 1] == number)
+    offset = jnp.where(chosen, lse * LOG2E, 1e30)
+    contract = (((1,), (1,)), ((), ()))
+    scores = lax.dot_general(keys, queries, contract, preferred_element_type=jnp.float32)
+    dprob = lax.dot_general(values, grads, contract, preferred_element_type=jnp.float32)
+    scores = scores.reshape(blocks, BLK, -1)
+    probs = jnp.exp2(scores * (scale * LOG2E) - offset[:, None, :]).reshape(dprob.shape)
+    dscore = (probs * (dprob - delta)).astype(jnp.bfloat16)
+    return probs.astype(jnp.bfloat16), dscore
+
+
+def beside(value, half):
+    row = lax.broadcasted_iota(jnp.int32, value.shape, 0)
+    zero = jnp.zeros_like(value)
+    return jnp.concatenate(
+        [jnp.where(row < half, value, zero), jnp.where(row < half, zero, value)], axis=1
+    )
+
+
+def query_kernel(scale, shard_ref, r0, r1, *refs):
+    count = r0.shape[0] // 4
+    pairs, (q_own, q_out) = refs[:-2], refs[-2:]
+    queries, grads, delta, lse, ids = unpack((r0[...], r1[...], r0[...], r1[...]), count)
+    half, size = 2 * count, queries.shape[1]
+    rows = (beside(queries, half), beside(grads, half), delta, lse, ids)
+    lane = lax.broadcasted_iota(jnp.int32, (1, 2 * half), 1)
+    total = None
+    for k in range(0, len(pairs), 4):
+        left, right = shard_ref[0] ^ (k // 2), shard_ref[0] ^ (k // 2 + 1)
+        keys = jnp.concatenate([pairs[k][...], pairs[k + 2][...]], axis=1)
+        values = jnp.concatenate([pairs[k + 1][...], pairs[k + 3][...]], axis=1)
+        base = jnp.where(lane < half, left, right) * (keys.shape[0] // BLK)
+        _, dscore = terms(rows, keys, values, base, scale)
+        part = lax.dot_general(
+            dscore, keys, (((0,), (0,)), ((), ())), preferred_element_type=jnp.float32
+        )
+        part = part[:half, :size] + part[half:, size:]
+        total = part if total is None else total + part
+    q_own[...] = total[:count]
+    q_out[...] = total[count:].astype(q_out.dtype)
+
+
+def key_sums(shard, lane, keys, values, scale):
+    count = lane.shape[1] // 4
+    rows = unpack([lane[k] for k in range(lane.shape[0])], count)
+    base = shard * (keys.shape[0] // BLK)
+    probs, dscore = terms(rows, keys[...], values[...], base, scale)
+    v_sum = jnp.dot(probs, rows[1], preferred_element_type=jnp.float32)
+    k_sum = jnp.dot(dscore, rows[0], preferred_element_type=jnp.float32)
+    return k_sum, v_sum
+
+
+def key_kernel(scale, shard_ref, lane, keys, values, k_part, v_part):
+    k_part[...], v_part[...] = key_sums(shard_ref[0], lane, keys, values, scale)
+
+
+def query_sum_kernel(scale, q_own, q_back, q_sum):
+    q_sum[...] = ((q_own[...] + q_back[...].astype(jnp.float32)) * scale).astype(q_sum.dtype)
+
+
+def finish_kernel(
+    scale, shard_ref, lane, keys, values, k_part, v_part, q_sum, q_out, k_out, v_out
+):
+    k_sum, v_sum = key_sums(shard_ref[0], lane, keys, values, scale)
+    k_out[...] = ((k_sum + k_part[...]) * scale).astype(k_out.dtype)
+    v_out[...] = (v_sum + v_part[...]).astype(v_out.dtype)
+    q_out[...] = q_sum[...]
+
+
+def fast_local(query_rows, key_rows, value_rows, attn_out, out_grad, logsumexp, shard_pick, block_pick):
+    count, size = query_rows.shape
+    n_seq, n_head = lax.axis_size("seq"), lax.axis_size("head")
+    seq, head = lax.axis_index("seq"), lax.axis_index("head")
+    scale = size ** (-0.5)
+    f32, bf16 = jnp.float32, jnp.bfloat16
+    mine = jnp.stack([out_grad, attn_out])
+    near = swap(mine, "head", n_head, 1)
+    mine, keys, values = lax.optimization_barrier((mine, key_rows, value_rows))
+    keys_side = swap(keys, "seq", n_seq, 2)
+    values_side = swap(values, "seq", n_seq, 2)
+    near, shard_pick, block_pick, query_rows, logsumexp = lax.optimization_barrier(
+        (near, shard_pick, block_pick, query_rows, logsumexp)
+    )
+
+    def pieces(which):
+        both = jnp.stack([mine, near], axis=1)
+        return lax.dynamic_slice_in_dim(both, which * size, size, axis=3)
+
+    here = pieces(head)
+    other = swap(pieces(head ^ 2), "head", n_head, 2)
+    near, keys, values = lax.optimization_barrier((near, key_rows, value_rows))
+    keys_core = swap(keys, "seq", n_seq, 1)
+    values_core = swap(values, "seq", n_seq, 1)
+    keys_side_core = swap(keys_side, "seq", n_seq, 1)
+    values_side_core = swap(values_side, "seq", n_seq, 1)
+    blocks_dev = key_rows.shape[0] // BLK
+    ids = shard_pick[0][:, :, None] * blocks_dev + block_pick[0]
+    ids = ids.reshape(count, -1).T.astype(bf16)
+    top = ids.shape[0]
+    stats = jnp.concatenate([logsumexp, jnp.zeros((top - 1, count), bf16)], axis=0)
+    small = jnp.tile(jnp.concatenate([stats, ids], axis=0), (1, size // count))
+    early = jnp.concatenate([query_rows, small], axis=0)
+    early, other = lax.optimization_barrier((early, other))
+    odd, high = (head & 1) == 1, (head & 2) == 2
+    both = jnp.stack([jnp.where(high, other, here), jnp.where(high, here, other)], axis=1)
+    both = jnp.where(odd, both[:, :, ::-1], both)
+    both = both.reshape(2 * count, size)
+    block = jnp.concatenate([early[:count], both, early[count:]], axis=0)
+    block, keys_core, values_core = lax.optimization_barrier((block, keys_core, values_core))
+    block_y = swap(block, "seq", n_seq, 4)
+    block_x = swap(block, "seq", n_seq, 2)
+    block_d = swap(block, "seq", n_seq, 6)
+    kv = key_rows.shape
+    vmem = pl.BlockSpec(memory_space=pltpu.VMEM)
+    smem = pl.BlockSpec(memory_space=pltpu.SMEM)
+    params = pltpu.CompilerParams(vmem_limit_bytes=32 * 1024 * 1024)
+    shard = seq[None].astype(jnp.int32)
+    q_own, q_out = pl.pallas_call(
+        functools.partial(query_kernel, scale),
+        out_shape=(
+            jax.ShapeDtypeStruct((count, size), f32),
+            jax.ShapeDtypeStruct((count, size), bf16),
+        ),
+        in_specs=[smem] + [vmem] * 10,
+        out_specs=(vmem,) * 2,
+        compiler_params=params,
+        name="query_terms",
+    )(
+        shard, block, block_y, key_rows, value_rows, keys_core, values_core,
+        keys_side, values_side, keys_side_core, values_side_core,
+    )
+    _, block_x, block_d = lax.optimization_barrier((q_out, block_x, block_d))
+    q_back = swap(q_out, "seq", n_seq, 4)
+    lane = jnp.stack([block, block_y, block_x, block_d])
+    lane_core = swap(lane, "seq", n_seq, 1)
+    k_part, v_part = pl.pallas_call(
+        functools.partial(key_kernel, scale),
+        out_shape=(jax.ShapeDtypeStruct(kv, f32),) * 2,
+        in_specs=[smem] + [vmem] * 3,
+        out_specs=(vmem,) * 2,
+        compiler_params=params,
+        cost_estimate=pl.CostEstimate(flops=1, bytes_accessed=1, transcendentals=0),
+        name="key_terms",
+    )(shard, lane, key_rows, value_rows)
+    q_sum = pl.pallas_call(
+        functools.partial(query_sum_kernel, scale),
+        out_shape=jax.ShapeDtypeStruct((count, size), bf16),
+        in_specs=[vmem] * 2,
+        out_specs=vmem,
+        compiler_params=params,
+        cost_estimate=pl.CostEstimate(flops=10**11, bytes_accessed=10**8, transcendentals=0),
+        name="query_sum",
+    )(q_own, q_back)
+    return pl.pallas_call(
+        functools.partial(finish_kernel, scale),
+        out_shape=tuple(jax.ShapeDtypeStruct(v, bf16) for v in ((count, size), kv, kv)),
+        in_specs=[smem] + [vmem] * 6,
+        compiler_params=params,
+        name="finish",
+    )(shard, lane_core, key_rows, value_rows, k_part, v_part, q_sum)
+
+
 def solution(mesh):
     placed = (
         P("seq", "head"),
@@ -133,6 +337,13 @@
         P("head", "seq", None),
         P("head", "seq", None, None),
     )
+    small = mesh.shape["seq"] == 8 and mesh.shape["head"] == 4
+
+    def local(*args):
+        count, size = args[0].shape
+        fits = small and count * 4 == size == 128 and args[7].shape[2] * args[7].shape[3] == 16
+        return (fast_local if fits else general_local)(*args)
+
     return jax.shard_map(
         local,
         mesh=mesh,

time: 53.5 us -> 22.8 us (0.43)
  waiting for transfers between devices: 23.4 us -> 3.21 us
  starting transfers between devices: 20.3 us -> 13.6 us
  matrix products: 5.57 us -> 0 us
  Pallas kernels: 0 us -> 2.41 us
  local copies, waits for them, and re-layouts: 2.63 us -> 0.24 us
  other arithmetic: 0.18 us -> 2.28 us
    all_to_all x5 -> x0, waiting for transfers between devices: 23.4 us -> none  [the longest x1 5.44 us: local(): lax.all_to_all(attn_out, 'head', split_axis=1, concat_axis=0, tiled=True)]
    all_to_all x5 -> x0, starting transfers between devices: 20.3 us -> none  [the longest x1 6.46 us: local(): lax.all_to_all(attn_out, 'head', split_axis=1, concat_axis=0, tiled=True)]
    ppermute x0 -> x13, starting transfers between devices: none -> 13.6 us  [swap(): return lax.ppermute(value, axis, [(i, i ^ bit) for i in range(count)])]
    dot_general x9 -> x0, matrix products: 5.57 us -> none  [the longest x1 1 us: local(): jnp.einsum('scr,scd->rd', dispatch, returned, precision=lax.Precision.HIG...]
    ppermute x0 -> x13, waiting for transfers between devices: none -> 3.21 us  [swap(): return lax.ppermute(value, axis, [(i, i ^ bit) for i in range(count)])]
    pallas_call x0 -> x4, Pallas kernels: none -> 2.41 us  [the longest x1 1.12 us: fast_local(): pl.pallas_call(functools.partial(finish_kernel, scale), out_shape=tuple((...]
    unnamed x14 -> x8, local copies, waits for them, and re-layouts: 2.16 us -> 0.04 us
    another operation x0 -> x5, other arithmetic: none -> 0.79 us  [the longest x1 0.75 us: fast_local(): mine = jnp.stack([out_grad, attn_out])]
  transfers between devices with their start and end apart: 5 -> 13, of which waited for: 5 -> 6; matrix products, arithmetic and copies ran while one was open for 5% -> 8% of each run, Pallas kernels for 0% -> 6%
where the time goes in v2:
time: 22.8 us; the launch traced here: 22.5 us
  starting transfers between devices  13.6 us (60%)
  waiting for transfers between devices  3.21 us (14%)
  Pallas kernels  2.41 us (11%)
  other arithmetic  2.28 us (10%)
  between operations  0.75 us (3%)
  local copies, waits for them, and re-layouts  0.24 us (1%)
    ppermute x13, starting transfers between devices, swap(): return lax.ppermute(value, axis, [(i, i ^ bit) for i in range(count)])  13.6 us
    ppermute x13, waiting for transfers between devices, swap(): return lax.ppermute(value, axis, [(i, i ^ bit) for i in range(count)])  3.21 us
    pallas_call x1, Pallas kernels, fast_local(): pl.pallas_call(functools.partial(finish_kernel, scale), out_shape=tuple((...  1.12 us
    pallas_call x1, Pallas kernels, fast_local(): pl.pallas_call(functools.partial(query_kernel, scale), out_shape=(jax.Sha...  0.87 us
    another operation x1, other arithmetic, fast_local(): mine = jnp.stack([out_grad, attn_out])  0.75 us
    convert_element_type x1, other arithmetic, fast_local(): ids = ids.reshape(count, -1).T.astype(bf16)  0.71 us
    mul x1, other arithmetic, fast_local(): ids = shard_pick[0][:, :, None] * blocks_dev + block_pick[0]  0.68 us
  transfers between devices with their start and end apart: 13, of which 6 were waited for; matrix products, arithmetic and copies ran while one was open for 8% of the time, Pallas kernels for 6%

profile of v2, /device:TPU:0, one launch (start us, length us, event | category | flops | bytes accessed | tf_op | source)
XLA Modules:
  0.0 22.5 jit_solution(9972139837008232039)
XLA Ops:
  0.6 0.0 copy-start
  0.6 0.8 %pad_maximum_fusion.2 = bf16[2,8,512]{2,1,0:T(8,128)(2,1)S(1)} fusion(bf16[1,8,512]{2,1,0:T(8,128)(2,1)} %bitcast.31, bf16[1,8,512]{2,1,0:T(8,128)(2,1)} %bitcast.32), kind=kLoop, calls=%fused_computation.7 | loop fusion | flops 8192 | bytes 32768 | tf_op jit(solution)/shard_map/stack | solution.py:242
  1.4 3.0 %collective-permute-start = (bf16[2,8,512]{2,1,0:T(8,128)(2,1)S(1)}, bf16[2,8,512]{2,1,0:T(8,128)(2,1)S(1)}, u32[]{:S(2)}, u32[]{:S(2)}) collective-permute-start(bf16[2,8,512]{2,1,0:T(8,128)(2,1)S(1)} %pad_maximum_fusion.2), channel_id=1, source_target_pairs={{0,1},{1,0},{2,3},{3,2},{4,5},{5,4},{6,7},{7,6},{8,9},{9,8},{10,11... | collective-permute-start | bytes 49160 | tf_op jit(solution)/shard_map/ppermute | solution.py:131
  4.4 1.5 %collective-permute-start.5 = (bf16[512,128]{1,0:T(8,128)(2,1)}, bf16[512,128]{1,0:T(8,128)(2,1)S(1)}, u32[]{:S(2)}, u32[]{:S(2)}) collective-permute-start(bf16[512,128]{1,0:T(8,128)(2,1)} %keys.3), channel_id=1, source_target_pairs={{0,8},{4,12},{8,0},{12,4},{16,24},{20,28},{24,16},{28,20},{1,9},{5... | collective-permute-start | bytes 393224 | tf_op jit(solution)/shard_map/ppermute | solution.py:131
  5.9 0.5 %collective-permute-start.6 = (bf16[512,128]{1,0:T(8,128)(2,1)}, bf16[512,128]{1,0:T(8,128)(2,1)S(1)}, u32[]{:S(2)}, u32[]{:S(2)}) collective-permute-start(bf16[512,128]{1,0:T(8,128)(2,1)} %values.3), channel_id=1, source_target_pairs={{0,8},{4,12},{8,0},{12,4},{16,24},{20,28},{24,16},{28,20},{1,9},{5... | collective-permute-start | bytes 393224 | tf_op jit(solution)/shard_map/ppermute | solution.py:131
  6.4 0.1 pad.14.clone
  6.5 0.0 collective-permute-done
  6.5 2.6 %collective-permute-start.1 = (bf16[2,2,8,128]{3,2,0,1:T(8,128)(2,1)S(1)}, bf16[2,2,8,128]{3,2,0,1:T(8,128)(2,1)S(1)}, u32[]{:S(2)}, u32[]{:S(2)}) collective-permute-start(bf16[2,2,8,128]{3,2,0,1:T(8,128)(2,1)S(1)} %fusion.1), channel_id=1, source_target_pairs={{0,2},{1,3},{2,0},{3,1},{4,6},{5,7},{6,4},{7,5},{8,10},{9,11},{10,... | collective-permute-start | bytes 24584 | tf_op jit(solution)/shard_map/ppermute | solution.py:131
  9.2 0.7 %multiply_bitcast_fusion = s32[32,4]{0,1:T(4,128)S(1)} fusion(s32[1,32,4]{1,2,0:T(4,128)} %param.14), kind=kLoop, calls=%fused_computation.17 | loop fusion | flops 128 | bytes 1024 | tf_op jit(solution)/shard_map/mul | solution.py:263
  9.9 0.7 %fusion.2 = bf16[16,32]{1,0:T(8,128)(2,1)S(1)} fusion(s32[32,16]{0,1:T(8,128)S(1)} %bitcast.27, s32[32,16]{0,1:T(8,128)} %bitcast.30), kind=kLoop, calls=%fused_computation.16 | loop fusion | flops 1024 | bytes 5120 | tf_op jit(solution)/shard_map/convert_element_type | solution.py:264
  10.6 0.1 pad_maximum_fusion.5
  10.7 0.0 copy-start.2
  10.7 0.1 tile.10
  10.8 0.1 collective-permute-start.2
  10.9 0.5 %collective-permute-start.3 = (bf16[512,128]{1,0:T(8,128)(2,1)}, bf16[512,128]{1,0:T(8,128)(2,1)S(1)}, u32[]{:S(2)}, u32[]{:S(2)}) collective-permute-start(bf16[512,128]{1,0:T(8,128)(2,1)} %values.3), channel_id=1, source_target_pairs={{0,4},{4,0},{8,12},{12,8},{16,20},{20,16},{24,28},{28,24},{1,5},{5... | collective-permute-start | bytes 393224 | tf_op jit(solution)/shard_map/ppermute | solution.py:131
  11.4 0.0 copy-done.2
  11.5 0.1 collective-permute-start.7
  11.6 0.8 %collective-permute-done.6.refs_5_ = bf16[512,128]{1,0:T(8,128)(2,1)S(1)} collective-permute-done((bf16[512,128]{1,0:T(8,128)(2,1)}, bf16[512,128]{1,0:T(8,128)(2,1)S(1)}, u32[]{:S(2)}, u32[]{:S(2)}) %collective-permute-start.6) | collective-permute-done | bytes 131104 | tf_op jit(solution)/shard_map/ppermute | solution.py:131
  12.4 0.0 collective-permute-start.8
  12.4 0.2 collective-permute-done.3.refs_3_
  12.6 1.6 %collective-permute-start.4 = (bf16[128,128]{1,0:T(8,128)(2,1)S(1)}, bf16[128,128]{1,0:T(8,128)(2,1)S(1)}, u32[]{:S(2)}, u32[]{:S(2)}) collective-permute-start(bf16[128,128]{1,0:T(8,128)(2,1)S(1)} %pad_maximum_fusion.1.r0), channel_id=1, source_target_pairs={{0,16},{4,20},{8,24},{12,28},{16,0},{20,4},{24,8},{28,12},{1,17},{... | collective-permute-start | bytes 98312 | tf_op jit(solution)/shard_map/ppermute | solution.py:131
  14.1 1.4 %collective-permute-start.10 = (bf16[128,128]{1,0:T(8,128)(2,1)S(1)}, bf16[128,128]{1,0:T(8,128)(2,1)S(1)}, u32[]{:S(2)}, u32[]{:S(2)}) collective-permute-start(bf16[128,128]{1,0:T(8,128)(2,1)S(1)} %pad_maximum_fusion.1.r0), channel_id=1, source_target_pairs={{0,24},{4,28},{8,16},{12,20},{16,8},{20,12},{24,0},{28,4},{1,25},{... | collective-permute-start | bytes 98312 | tf_op jit(solution)/shard_map/ppermute | solution.py:131
  15.6 0.5 %collective-permute-start.9 = (bf16[128,128]{1,0:T(8,128)(2,1)S(1)}, bf16[128,128]{1,0:T(8,128)(2,1)S(1)}, u32[]{:S(2)}, u32[]{:S(2)}) collective-permute-start(bf16[128,128]{1,0:T(8,128)(2,1)S(1)} %pad_maximum_fusion.1.r0), channel_id=1, source_target_pairs={{0,8},{4,12},{8,0},{12,4},{16,24},{20,28},{24,16},{28,20},{1,9},{5... | collective-permute-start | bytes 98312 | tf_op jit(solution)/shard_map/ppermute | solution.py:131
  16.1 0.4 %collective-permute-done.4.r1 = bf16[128,128]{1,0:T(8,128)(2,1)S(1)} collective-permute-done((bf16[128,128]{1,0:T(8,128)(2,1)S(1)}, bf16[128,128]{1,0:T(8,128)(2,1)S(1)}, u32[]{:S(2)}, u32[]{:S(2)}) %collective-permute-start.4) | collective-permute-done | bytes 32800 | tf_op jit(solution)/shard_map/ppermute | solution.py:131
  16.6 0.9 %query_terms.1 = (f32[32,128]{1,0:T(8,128)S(1)}, bf16[32,128]{1,0:T(8,128)(2,1)S(1)}) custom-call(s32[1]{0:T(128)} %bitcast.shard_ref, bf16[128,128]{1,0:T(8,128)(2,1)S(1)} %pad_maximum_fusion.1.r0, bf16[128,128]{1,0:T(8,128)(2,1)S(1)} %collective-permute-done.4.r1, bf16[512,128]{1,0:T(8,128)(2,1)S(1)} %copy-done, bf16[512,128]{1,0:T(8,128)(2,1)S(1)} %copy-done.1, ...), custom_call_target="tpu_custom_call" | custom-call | tf_op jit(solution)/shard_map/query_terms/pallas_call | solution.py:284
  17.4 1.6 %collective-permute-start.12 = (bf16[32,128]{1,0:T(8,128)(2,1)S(1)}, bf16[32,128]{1,0:T(8,128)(2,1)S(1)}, u32[]{:S(2)}, u32[]{:S(2)}) collective-permute-start(bf16[32,128]{1,0:T(8,128)(2,1)S(1)} %get-tuple-element.39), channel_id=1, source_target_pairs={{0,16},{4,20},{8,24},{12,28},{16,0},{20,4},{24,8},{28,12},{1,17},{... | collective-permute-start | bytes 24584 | tf_op jit(solution)/shard_map/ppermute | solution.py:131
  19.0 0.5 %collective-permute-done.9 = bf16[128,128]{1,0:T(8,128)(2,1)S(1)} collective-permute-done((bf16[128,128]{1,0:T(8,128)(2,1)S(1)}, bf16[128,128]{1,0:T(8,128)(2,1)S(1)}, u32[]{:S(2)}, u32[]{:S(2)}) %collective-permute-start.9) | collective-permute-done | bytes 32800 | tf_op jit(solution)/shard_map/ppermute | solution.py:131
  19.5 0.4 %key_terms.1 = (f32[512,128]{1,0:T(8,128)S(1)}, f32[512,128]{1,0:T(8,128)S(1)}) custom-call(s32[1]{0:T(128)} %bitcast.shard_ref, bf16[4,128,128]{2,1,0:T(8,128)(2,1)S(1)} %pad_maximum_fusion.lane, bf16[512,128]{1,0:T(8,128)(2,1)S(1)} %copy-done, bf16[512,128]{1,0:T(8,128)(2,1)S(1)} %copy-done.1), custom_call_target="tpu_custom_call" | custom-call | flops 1 | bytes 1 | tf_op jit(solution)/shard_map/key_terms/pallas_call | solution.py:302
  19.9 0.1 collective-permute-start.11
  20.0 1.1 %collective-permute-done.12.q_back = bf16[32,128]{1,0:T(8,128)(2,1)S(1)} collective-permute-done((bf16[32,128]{1,0:T(8,128)(2,1)S(1)}, bf16[32,128]{1,0:T(8,128)(2,1)S(1)}, u32[]{:S(2)}, u32[]{:S(2)}) %collective-permute-start.12) | collective-permute-done | bytes 8224 | tf_op jit(solution)/shard_map/ppermute | solution.py:131
  21.2 0.2 collective-permute-done.11.lane
  21.3 1.1 %finish.1 = (bf16[32,128]{1,0:T(8,128)(2,1)}, bf16[512,128]{1,0:T(8,128)(2,1)}, bf16[512,128]{1,0:T(8,128)(2,1)}) custom-call(s32[1]{0:T(128)} %bitcast.shard_ref, bf16[4,128,128]{2,1,0:T(8,128)(2,1)S(1)} %collective-permute-done.11.lane, bf16[512,128]{1,0:T(8,128)(2,1)S(1)} %copy-done, bf16[512,128]{1,0:T(8,128)(2,1)S(1)} %copy-done.1, ...), custom_call_target="tpu_custom_call" | custom-call | tf_op jit(solution)/shard_map/finish/pallas_call | solution.py:320
  (24 shorter events, 0.1 us)
Async XLA Ops:
  0.6 10.2 %copy-start = (bf16[512,128]{1,0:T(8,128)(2,1)S(1)}, bf16[512,128]{1,0:T(8,128)(2,1)}, u32[]{:S(2)}) copy-start(bf16[512,128]{1,0:T(8,128)(2,1)} %keys.3) | copy-start | bytes 393220
  1.4 5.1 %collective-permute-start = (bf16[2,8,512]{2,1,0:T(8,128)(2,1)S(1)}, bf16[2,8,512]{2,1,0:T(8,128)(2,1)S(1)}, u32[]{:S(2)}, u32[]{:S(2)}) collective-permute-start(bf16[2,8,512]{2,1,0:T(8,128)(2,1)S(1)} %pad_maximum_fusion.2), channel_id=1, source_target_pairs={{0,1},{1,0},{2,3},{3,2},{4,5},{5,4},{6,7},{7,6},{8,9},{9,8},{10,11... | collective-permute-start | bytes 49160 | tf_op jit(solution)/shard_map/ppermute | solution.py:131
  4.4 7.0 %collective-permute-start.5 = (bf16[512,128]{1,0:T(8,128)(2,1)}, bf16[512,128]{1,0:T(8,128)(2,1)S(1)}, u32[]{:S(2)}, u32[]{:S(2)}) collective-permute-start(bf16[512,128]{1,0:T(8,128)(2,1)} %keys.3), channel_id=1, source_target_pairs={{0,8},{4,12},{8,0},{12,4},{16,24},{20,28},{24,16},{28,20},{1,9},{5... | collective-permute-start | bytes 393224 | tf_op jit(solution)/shard_map/ppermute | solution.py:131
  5.9 6.5 %collective-permute-start.6 = (bf16[512,128]{1,0:T(8,128)(2,1)}, bf16[512,128]{1,0:T(8,128)(2,1)S(1)}, u32[]{:S(2)}, u32[]{:S(2)}) collective-permute-start(bf16[512,128]{1,0:T(8,128)(2,1)} %values.3), channel_id=1, source_target_pairs={{0,8},{4,12},{8,0},{12,4},{16,24},{20,28},{24,16},{28,20},{1,9},{5... | collective-permute-start | bytes 393224 | tf_op jit(solution)/shard_map/ppermute | solution.py:131
  6.5 4.8 %collective-permute-start.1 = (bf16[2,2,8,128]{3,2,0,1:T(8,128)(2,1)S(1)}, bf16[2,2,8,128]{3,2,0,1:T(8,128)(2,1)S(1)}, u32[]{:S(2)}, u32[]{:S(2)}) collective-permute-start(bf16[2,2,8,128]{3,2,0,1:T(8,128)(2,1)S(1)} %fusion.1), channel_id=1, source_target_pairs={{0,2},{1,3},{2,0},{3,1},{4,6},{5,7},{6,4},{7,5},{8,10},{9,11},{10,... | collective-permute-start | bytes 24584 | tf_op jit(solution)/shard_map/ppermute | solution.py:131
  9.9 0.7 %copy-start.3 = (bf16[1,32]{1,0:T(2,128)(2,1)S(1)}, bf16[1,32]{1,0:T(2,128)(2,1)}, u32[]{:S(2)}) copy-start(bf16[1,32]{1,0:T(2,128)(2,1)} %param.13) | copy-start | bytes 196
  10.7 0.7 %copy-start.2 = (bf16[32,128]{1,0:T(8,128)(2,1)S(1)}, bf16[32,128]{1,0:T(8,128)(2,1)}, u32[]{:S(2)}) copy-start(bf16[32,128]{1,0:T(8,128)(2,1)} %param.8) | copy-start | bytes 24580
  10.8 1.6 %collective-permute-start.2 = (bf16[512,128]{1,0:T(8,128)(2,1)S(1)}, bf16[512,128]{1,0:T(8,128)(2,1)S(1)}, u32[]{:S(2)}, u32[]{:S(2)}) collective-permute-start(bf16[512,128]{1,0:T(8,128)(2,1)S(1)} %copy-done), channel_id=1, source_target_pairs={{0,4},{4,0},{8,12},{12,8},{16,20},{20,16},{24,28},{28,24},{1,5},{5... | collective-permute-start | bytes 393224 | tf_op jit(solution)/shard_map/ppermute | solution.py:131
  10.9 1.7 %collective-permute-start.3 = (bf16[512,128]{1,0:T(8,128)(2,1)}, bf16[512,128]{1,0:T(8,128)(2,1)S(1)}, u32[]{:S(2)}, u32[]{:S(2)}) collective-permute-start(bf16[512,128]{1,0:T(8,128)(2,1)} %values.3), channel_id=1, source_target_pairs={{0,4},{4,0},{8,12},{12,8},{16,20},{20,16},{24,28},{28,24},{1,5},{5... | collective-permute-start | bytes 393224 | tf_op jit(solution)/shard_map/ppermute | solution.py:131
  11.4 5.2 %copy-start.1 = (bf16[512,128]{1,0:T(8,128)(2,1)S(1)}, bf16[512,128]{1,0:T(8,128)(2,1)}, u32[]{:S(2)}) copy-start(bf16[512,128]{1,0:T(8,128)(2,1)} %values.3) | copy-start | bytes 393220
  11.5 5.1 %collective-permute-start.7 = (bf16[512,128]{1,0:T(8,128)(2,1)S(1)}, bf16[512,128]{1,0:T(8,128)(2,1)S(1)}, u32[]{:S(2)}, u32[]{:S(2)}) collective-permute-start(bf16[512,128]{1,0:T(8,128)(2,1)S(1)} %collective-permute-done.5.refs_4_), channel_id=1, source_target_pairs={{0,4},{4,0},{8,12},{12,8},{16,20},{20,16},{24,28},{28,24},{1,5},{5... | collective-permute-start | bytes 393224 | tf_op jit(solution)/shard_map/ppermute | solution.py:131
  12.4 4.1 %collective-permute-start.8 = (bf16[512,128]{1,0:T(8,128)(2,1)S(1)}, bf16[512,128]{1,0:T(8,128)(2,1)S(1)}, u32[]{:S(2)}, u32[]{:S(2)}) collective-permute-start(bf16[512,128]{1,0:T(8,128)(2,1)S(1)} %collective-permute-done.6.refs_5_), channel_id=1, source_target_pairs={{0,4},{4,0},{8,12},{12,8},{16,20},{20,16},{24,28},{28,24},{1,5},{5... | collective-permute-start | bytes 393224 | tf_op jit(solution)/shard_map/ppermute | solution.py:131
  12.6 3.9 %collective-permute-start.4 = (bf16[128,128]{1,0:T(8,128)(2,1)S(1)}, bf16[128,128]{1,0:T(8,128)(2,1)S(1)}, u32[]{:S(2)}, u32[]{:S(2)}) collective-permute-start(bf16[128,128]{1,0:T(8,128)(2,1)S(1)} %pad_maximum_fusion.1.r0), channel_id=1, source_target_pairs={{0,16},{4,20},{8,24},{12,28},{16,0},{20,4},{24,8},{28,12},{1,17},{... | collective-permute-start | bytes 98312 | tf_op jit(solution)/shard_map/ppermute | solution.py:131
  14.1 4.9 %collective-permute-start.10 = (bf16[128,128]{1,0:T(8,128)(2,1)S(1)}, bf16[128,128]{1,0:T(8,128)(2,1)S(1)}, u32[]{:S(2)}, u32[]{:S(2)}) collective-permute-start(bf16[128,128]{1,0:T(8,128)(2,1)S(1)} %pad_maximum_fusion.1.r0), channel_id=1, source_target_pairs={{0,24},{4,28},{8,16},{12,20},{16,8},{20,12},{24,0},{28,4},{1,25},{... | collective-permute-start | bytes 98312 | tf_op jit(solution)/shard_map/ppermute | solution.py:131
  15.6 3.9 %collective-permute-start.9 = (bf16[128,128]{1,0:T(8,128)(2,1)S(1)}, bf16[128,128]{1,0:T(8,128)(2,1)S(1)}, u32[]{:S(2)}, u32[]{:S(2)}) collective-permute-start(bf16[128,128]{1,0:T(8,128)(2,1)S(1)} %pad_maximum_fusion.1.r0), channel_id=1, source_target_pairs={{0,8},{4,12},{8,0},{12,4},{16,24},{20,28},{24,16},{28,20},{1,9},{5... | collective-permute-start | bytes 98312 | tf_op jit(solution)/shard_map/ppermute | solution.py:131
  17.4 3.7 %collective-permute-start.12 = (bf16[32,128]{1,0:T(8,128)(2,1)S(1)}, bf16[32,128]{1,0:T(8,128)(2,1)S(1)}, u32[]{:S(2)}, u32[]{:S(2)}) collective-permute-start(bf16[32,128]{1,0:T(8,128)(2,1)S(1)} %get-tuple-element.39), channel_id=1, source_target_pairs={{0,16},{4,20},{8,24},{12,28},{16,0},{20,4},{24,8},{28,12},{1,17},{... | collective-permute-start | bytes 24584 | tf_op jit(solution)/shard_map/ppermute | solution.py:131
  19.9 1.4 %collective-permute-start.11 = (bf16[4,128,128]{2,1,0:T(8,128)(2,1)S(1)}, bf16[4,128,128]{2,1,0:T(8,128)(2,1)S(1)}, u32[]{:S(2)}, u32[]{:S(2)}) collective-permute-start(bf16[4,128,128]{2,1,0:T(8,128)(2,1)S(1)} %pad_maximum_fusion.lane), channel_id=1, source_target_pairs={{0,4},{4,0},{8,12},{12,8},{16,20},{20,16},{24,28},{28,24},{1,5},{5... | collective-permute-start | bytes 393224 | tf_op jit(solution)/shard_map/ppermute | solution.py:131

commit v3 on v2

--- a/solution.py
+++ b/solution.py
@@ -146,78 +146,91 @@
     queries, grads, outs = (
         jnp.concatenate([r[k * count : (k + 1) * count] for r in parts], axis=0) for k in range(3)
     )
-    small = [r[3 * count :].astype(jnp.float32) for r in parts]
+    small = [r[3 * count : 4 * count].astype(jnp.float32) for r in parts]
     lane = lax.broadcasted_iota(jnp.int32, small[0].shape, 1) // count
     merged = small[0]
     for k in range(1, len(parts)):
         merged = jnp.where(lane == k, small[k], merged)
-    merged = merged[:, : queries.shape[0]]
     half = merged.shape[0] // 2
     delta = row_sums(outs, grads).astype(jnp.bfloat16).astype(jnp.float32)
     return queries, grads, delta, merged[0:1], merged[half:]
 
 
-def terms(rows, keys, values, base, scale):
-    queries, grads, delta, lse, ids = rows
-    blocks = keys.shape[0] // BLK
+def chosen_offset(lse, ids, blocks, base):
     number = lax.broadcasted_iota(jnp.int32, (blocks, ids.shape[1]), 0) + base
     number = number.astype(jnp.float32)
     chosen = ids[0:1] == number
     for k in range(1, ids.shape[0]):
         chosen = chosen | (ids[k : k + 1] == number)
-    offset = jnp.where(chosen, lse * LOG2E, 1e30)
+    return jnp.where(chosen, lse * LOG2E, 1e30)
+
+
+def terms(queries, grads, delta, offset, keys, values, scale):
     contract = (((1,), (1,)), ((), ()))
     scores = lax.dot_general(keys, queries, contract, preferred_element_type=jnp.float32)
     dprob = lax.dot_general(values, grads, contract, preferred_element_type=jnp.float32)
-    scores = scores.reshape(blocks, BLK, -1)
+    scores = scores.reshape(offset.shape[0], BLK, -1)
     probs = jnp.exp2(scores * (scale * LOG2E) - offset[:, None, :]).reshape(dprob.shape)
-    dscore = (probs * (dprob - delta)).astype(jnp.bfloat16)
-    return probs.astype(jnp.bfloat16), dscore
-
-
-def beside(value, half):
-    row = lax.broadcasted_iota(jnp.int32, value.shape, 0)
-    zero = jnp.zeros_like(value)
-    return jnp.concatenate(
-        [jnp.where(row < half, value, zero), jnp.where(row < half, zero, value)], axis=1
-    )
-
-
-def query_kernel(scale, shard_ref, r0, r1, *refs):
+    return probs, probs * (dprob - delta)
+
+
+def query_sums(scale, shard, bits, r0, r1, pairs):
+    parts, count = (r0[...], r1[...]), r0.shape[0] // 4
+    queries, grads, delta, lse, ids = unpack(parts + parts, count)
+    half, size = 2 * count, queries.shape[1]
+    row = lax.broadcasted_iota(jnp.int32, queries.shape, 0)
+    lane = lax.broadcasted_iota(jnp.int32, (1, 2 * half), 1)
+
+    def beside(value):
+        zero = jnp.zeros_like(value)
+        return jnp.concatenate(
+            [jnp.where(row < half, value, zero), jnp.where(row < half, zero, value)], axis=1
+        )
+
+    queries, grads = beside(queries), beside(grads)
+    wide, scored = [], []
+    for (left_bit, right_bit), (left, right) in zip(bits, pairs):
+        keys = jnp.concatenate([left[0], right[0]], axis=1)
+        values = jnp.concatenate([left[1], right[1]], axis=1)
+        blocks = keys.shape[0] // BLK
+        base = jnp.where(lane < half, shard ^ left_bit, shard ^ right_bit) * blocks
+        offset = chosen_offset(lse, ids, blocks, base)
+        _, dscore = terms(queries, grads, delta, offset, keys, values, scale)
+        wide.append(keys)
+        scored.append(dscore.T.astype(jnp.bfloat16))
+    scored, wide = jnp.concatenate(scored, axis=1), jnp.concatenate(wide, axis=0)
+    total = jnp.dot(scored, wide, preferred_element_type=jnp.float32)
+    return total[:half, :size] + total[half:, size:]
+
+
+def near_kernel(scale, shard_ref, r0, r1, k0, v0, k1, v1, q_part):
+    pair = ((k0[...], v0[...]), (k1[...], v1[...]))
+    q_part[...] = query_sums(scale, shard_ref[0], ((0, 1),), r0, r1, (pair,))
+
+
+def side_kernel(scale, shard_ref, r0, r1, q_part, k2, v2, k3, v3, q_own, q_out):
     count = r0.shape[0] // 4
-    pairs, (q_own, q_out) = refs[:-2], refs[-2:]
-    queries, grads, delta, lse, ids = unpack((r0[...], r1[...], r0[...], r1[...]), count)
-    half, size = 2 * count, queries.shape[1]
-    rows = (beside(queries, half), beside(grads, half), delta, lse, ids)
-    lane = lax.broadcasted_iota(jnp.int32, (1, 2 * half), 1)
-    total = None
-    for k in range(0, len(pairs), 4):
-        left, right = shard_ref[0] ^ (k // 2), shard_ref[0] ^ (k // 2 + 1)
-        keys = jnp.concatenate([pairs[k][...], pairs[k + 2][...]], axis=1)
-        values = jnp.concatenate([pairs[k + 1][...], pairs[k + 3][...]], axis=1)
-        base = jnp.where(lane < half, left, right) * (keys.shape[0] // BLK)
-        _, dscore = terms(rows, keys, values, base, scale)
-        part = lax.dot_general(
-            dscore, keys, (((0,), (0,)), ((), ())), preferred_element_type=jnp.float32
-        )
-        part = part[:half, :size] + part[half:, size:]
-        total = part if total is None else total + part
+    pair = ((k2[...], v2[...]), (k3[...], v3[...]))
+    total = q_part[...] + query_sums(scale, shard_ref[0], ((2, 3),), r0, r1, (pair,))
     q_own[...] = total[:count]
     q_out[...] = total[count:].astype(q_out.dtype)
 
 
-def key_sums(shard, lane, keys, values, scale):
-    count = lane.shape[1] // 4
-    rows = unpack([lane[k] for k in range(lane.shape[0])], count)
-    base = shard * (keys.shape[0] // BLK)
-    probs, dscore = terms(rows, keys[...], values[...], base, scale)
-    v_sum = jnp.dot(probs, rows[1], preferred_element_type=jnp.float32)
-    k_sum = jnp.dot(dscore, rows[0], preferred_element_type=jnp.float32)
+def key_sums(shard, parts, keys, values, scale):
+    count = parts[0].shape[0] // 4
+    queries, grads, delta, lse, ids = unpack(parts, count)
+    blocks = keys.shape[0] // BLK
+    offset = chosen_offset(lse, ids, blocks, shard * blocks)
+    probs, dscore = terms(queries, grads, delta, offset, keys, values, scale)
+    low = jnp.bfloat16
+    v_sum = jnp.dot(probs.astype(low), grads, preferred_element_type=jnp.float32)
+    k_sum = jnp.dot(dscore.astype(low), queries, preferred_element_type=jnp.float32)
     return k_sum, v_sum
 
 
 def key_kernel(scale, shard_ref, lane, keys, values, k_part, v_part):
-    k_part[...], v_part[...] = key_sums(shard_ref[0], lane, keys, values, scale)
+    parts = [lane[k] for k in range(lane.shape[0])]
+    k_part[...], v_part[...] = key_sums(shard_ref[0], parts, keys[...], values[...], scale)
 
 
 def query_sum_kernel(scale, q_own, q_back, q_sum):
@@ -227,18 +240,53 @@
 def finish_kernel(
     scale, shard_ref, lane, keys, values, k_part, v_part, q_sum, q_out, k_out, v_out
 ):
-    k_sum, v_sum = key_sums(shard_ref[0], lane, keys, values, scale)
+    parts = [lane[k] for k in range(lane.shape[0])]
+    k_sum, v_sum = key_sums(shard_ref[0], parts, keys[...], values[...], scale)
     k_out[...] = ((k_sum + k_part[...]) * scale).astype(k_out.dtype)
     v_out[...] = (v_sum + v_part[...]).astype(v_out.dtype)
     q_out[...] = q_sum[...]
 
 
+def small_kernel(blocks_dev, queries, lse, shards, picks, early):
+    count, size = queries.shape
+    row = lax.broadcasted_iota(jnp.int32, (count, size), 0)
+    lane = lax.broadcasted_iota(jnp.int32, (count, size), 1)
+    repeat = (lane % count == row).astype(jnp.bfloat16)
+    ids = [shards[g : g + 1] * blocks_dev + picks[g] for g in range(shards.shape[0])]
+    ids = jnp.concatenate(ids, axis=0).astype(jnp.float32)
+    stats = jnp.broadcast_to(lse[...].astype(jnp.float32), ids.shape)
+    both = jnp.concatenate([stats, ids], axis=0).astype(jnp.bfloat16)
+    early[:count] = queries[...]
+    both = jnp.dot(both, repeat, preferred_element_type=jnp.float32)
+    early[count:] = both.astype(early.dtype)
+
+
 def fast_local(query_rows, key_rows, value_rows, attn_out, out_grad, logsumexp, shard_pick, block_pick):
     count, size = query_rows.shape
+    kv = key_rows.shape
     n_seq, n_head = lax.axis_size("seq"), lax.axis_size("head")
     seq, head = lax.axis_index("seq"), lax.axis_index("head")
     scale = size ** (-0.5)
     f32, bf16 = jnp.float32, jnp.bfloat16
+    vmem = pl.BlockSpec(memory_space=pltpu.VMEM)
+    smem = pl.BlockSpec(memory_space=pltpu.SMEM)
+
+    def kernel(body, name, outs, scalars, args, flops=None, last=False):
+        cost = None
+        if flops is not None:
+            cost = pl.CostEstimate(
+                flops=flops, bytes_accessed=max(flops // 1000, 1), transcendentals=0
+            )
+        return pl.pallas_call(
+            body,
+            out_shape=tuple(jax.ShapeDtypeStruct(v, t) for v, t in outs),
+            in_specs=[smem] * len(scalars) + [vmem] * len(args),
+            compiler_params=pltpu.CompilerParams(vmem_limit_bytes=32 * 1024 * 1024),
+            cost_estimate=cost,
+            name=name,
+            **({} if last else dict(out_specs=(vmem,) * len(outs))),
+        )(*(v[None].astype(jnp.int32) for v in scalars), *args)
+
     mine = jnp.stack([out_grad, attn_out])
     near = swap(mine, "head", n_head, 1)
     mine, keys, values = lax.optimization_barrier((mine, key_rows, value_rows))
@@ -259,13 +307,10 @@
     values_core = swap(values, "seq", n_seq, 1)
     keys_side_core = swap(keys_side, "seq", n_seq, 1)
     values_side_core = swap(values_side, "seq", n_seq, 1)
-    blocks_dev = key_rows.shape[0] // BLK
-    ids = shard_pick[0][:, :, None] * blocks_dev + block_pick[0]
-    ids = ids.reshape(count, -1).T.astype(bf16)
-    top = ids.shape[0]
-    stats = jnp.concatenate([logsumexp, jnp.zeros((top - 1, count), bf16)], axis=0)
-    small = jnp.tile(jnp.concatenate([stats, ids], axis=0), (1, size // count))
-    early = jnp.concatenate([query_rows, small], axis=0)
+    (early,) = kernel(
+        functools.partial(small_kernel, kv[0] // BLK), "small", [((2 * count, size), bf16)], (),
+        (query_rows, logsumexp, shard_pick[0].T, block_pick[0].transpose(1, 2, 0)), flops=10**9,
+    )
     early, other = lax.optimization_barrier((early, other))
     odd, high = (head & 1) == 1, (head & 2) == 2
     both = jnp.stack([jnp.where(high, other, here), jnp.where(high, here, other)], axis=1)
@@ -276,54 +321,32 @@
     block_y = swap(block, "seq", n_seq, 4)
     block_x = swap(block, "seq", n_seq, 2)
     block_d = swap(block, "seq", n_seq, 6)
-    kv = key_rows.shape
-    vmem = pl.BlockSpec(memory_space=pltpu.VMEM)
-    smem = pl.BlockSpec(memory_space=pltpu.SMEM)
-    params = pltpu.CompilerParams(vmem_limit_bytes=32 * 1024 * 1024)
-    shard = seq[None].astype(jnp.int32)
-    q_own, q_out = pl.pallas_call(
-        functools.partial(query_kernel, scale),
-        out_shape=(
-            jax.ShapeDtypeStruct((count, size), f32),
-            jax.ShapeDtypeStruct((count, size), bf16),
-        ),
-        in_specs=[smem] + [vmem] * 10,
-        out_specs=(vmem,) * 2,
-        compiler_params=params,
-        name="query_terms",
-    )(
-        shard, block, block_y, key_rows, value_rows, keys_core, values_core,
-        keys_side, values_side, keys_side_core, values_side_core,
+    (q_part,) = kernel(
+        functools.partial(near_kernel, scale), "near_terms", [((2 * count, size), f32)], (seq,),
+        (block, block_y, key_rows, value_rows, keys_core, values_core), flops=10**11,
+    )
+    q_own, q_out = kernel(
+        functools.partial(side_kernel, scale), "side_terms",
+        [((count, size), f32), ((count, size), bf16)], (seq,),
+        (block, block_y, q_part, keys_side, values_side, keys_side_core, values_side_core),
     )
     _, block_x, block_d = lax.optimization_barrier((q_out, block_x, block_d))
     q_back = swap(q_out, "seq", n_seq, 4)
     lane = jnp.stack([block, block_y, block_x, block_d])
     lane_core = swap(lane, "seq", n_seq, 1)
-    k_part, v_part = pl.pallas_call(
-        functools.partial(key_kernel, scale),
-        out_shape=(jax.ShapeDtypeStruct(kv, f32),) * 2,
-        in_specs=[smem] + [vmem] * 3,
-        out_specs=(vmem,) * 2,
-        compiler_params=params,
-        cost_estimate=pl.CostEstimate(flops=1, bytes_accessed=1, transcendentals=0),
-        name="key_terms",
-    )(shard, lane, key_rows, value_rows)
-    q_sum = pl.pallas_call(
-        functools.partial(query_sum_kernel, scale),
-        out_shape=jax.ShapeDtypeStruct((count, size), bf16),
-        in_specs=[vmem] * 2,
-        out_specs=vmem,
-        compiler_params=params,
-        cost_estimate=pl.CostEstimate(flops=10**11, bytes_accessed=10**8, transcendentals=0),
-        name="query_sum",
-    )(q_own, q_back)
-    return pl.pallas_call(
-        functools.partial(finish_kernel, scale),
-        out_shape=tuple(jax.ShapeDtypeStruct(v, bf16) for v in ((count, size), kv, kv)),
-        in_specs=[smem] + [vmem] * 6,
-        compiler_params=params,
-        name="finish",
-    )(shard, lane_core, key_rows, value_rows, k_part, v_part, q_sum)
+    k_part, v_part = kernel(
+        functools.partial(key_kernel, scale), "key_terms", [(kv, f32)] * 2, (seq,),
+        (lane, key_rows, value_rows), flops=1,
+    )
+    (q_sum,) = kernel(
+        functools.partial(query_sum_kernel, scale), "query_sum", [((count, size), bf16)], (),
+        (q_own, q_back), flops=3 * 10**9,
+    )
+    return kernel(
+        functools.partial(finish_kernel, scale), "finish",
+        [((count, size), bf16), (kv, bf16), (kv, bf16)], (seq,),
+        (lane_core, key_rows, value_rows, k_part, v_part, q_sum), last=True,
+    )
 
 
 def solution(mesh):

time: 22.8 us -> 21.6 us (0.947)
  other arithmetic: 2.28 us -> 0.77 us
  waiting for transfers between devices: 3.21 us -> 2.17 us
  starting transfers between devices: 13.6 us -> 14.2 us
  local copies, waits for them, and re-layouts: 0.24 us -> 0.67 us
  Pallas kernels: 2.41 us -> 2.78 us
    ppermute x13, waiting for transfers between devices: 3.21 us -> 2.17 us  [swap(): return lax.ppermute(value, axis, [(i, i ^ bit) for i in range(count)])]
    convert_element_type x1 -> x0, other arithmetic: 0.71 us -> none  [fast_local(): ids = ids.reshape(count, -1).T.astype(bf16)]
    mul x1 -> x0, other arithmetic: 0.68 us -> none  [fast_local(): ids = shard_pick[0][:, :, None] * blocks_dev + block_pick[0]]
    unnamed x8 -> x12, local copies, waits for them, and re-layouts: 0.04 us -> 0.67 us
    ppermute x13, starting transfers between devices: 13.6 us -> 14.2 us  [swap(): return lax.ppermute(value, axis, [(i, i ^ bit) for i in range(count)])]
    pallas_call x4 -> x6, Pallas kernels: 2.41 us -> 2.78 us  [kernel(): pl.pallas_call(body, out_shape=tuple((jax.ShapeDtypeStruct(v, t) for v, t...]
  transfers between devices with their start and end apart: 13 -> 13, of which waited for: 6 -> 4; matrix products, arithmetic and copies ran while one was open for 8% -> 0% of each run, Pallas kernels for 6% -> 8%
where the time goes in v3:
time: 21.6 us; the launch traced here: 21.4 us
  starting transfers between devices  14.2 us (66%)
  Pallas kernels  2.78 us (13%)
  waiting for transfers between devices  2.17 us (10%)
  other arithmetic  0.77 us (4%)
  between operations  0.77 us (4%)
  local copies, waits for them, and re-layouts  0.67 us (3%)
    ppermute x13, starting transfers between devices, swap(): return lax.ppermute(value, axis, [(i, i ^ bit) for i in range(count)])  14.2 us
    pallas_call x6, Pallas kernels, kernel(): pl.pallas_call(body, out_shape=tuple((jax.ShapeDtypeStruct(v, t) for v, t...  2.78 us
    ppermute x13, waiting for transfers between devices, swap(): return lax.ppermute(value, axis, [(i, i ^ bit) for i in range(count)])  2.17 us
    another operation x1, other arithmetic, fast_local(): mine = jnp.stack([out_grad, attn_out])  0.72 us
    unnamed x12, local copies, waits for them, and re-layouts  0.67 us
  transfers between devices with their start and end apart: 13, of which 4 were waited for; matrix products, arithmetic and copies ran while one was open for 0% of the time, Pallas kernels for 8%

profile of v3, /device:TPU:0, one launch (start us, length us, event | category | flops | bytes accessed | tf_op | source)
XLA Modules:
  0.0 21.4 jit_solution(11562266297250016514)
XLA Ops:
  0.6 0.7 %pad_maximum_fusion.2 = bf16[2,8,512]{2,1,0:T(8,128)(2,1)S(1)} fusion(bf16[1,8,512]{2,1,0:T(8,128)(2,1)} %bitcast.31, bf16[1,8,512]{2,1,0:T(8,128)(2,1)} %bitcast.32), kind=kLoop, calls=%fused_computation.7 | loop fusion | flops 8192 | bytes 32768 | tf_op jit(solution)/shard_map/stack | solution.py:290
  1.3 3.0 %collective-permute-start = (bf16[2,8,512]{2,1,0:T(8,128)(2,1)S(1)}, bf16[2,8,512]{2,1,0:T(8,128)(2,1)S(1)}, u32[]{:S(2)}, u32[]{:S(2)}) collective-permute-start(bf16[2,8,512]{2,1,0:T(8,128)(2,1)S(1)} %pad_maximum_fusion.2), channel_id=1, source_target_pairs={{0,1},{1,0},{2,3},{3,2},{4,5},{5,4},{6,7},{7,6},{8,9},{9,8},{10,11... | collective-permute-start | bytes 49160 | tf_op jit(solution)/shard_map/ppermute | solution.py:131
  4.4 1.5 %collective-permute-start.5 = (bf16[512,128]{1,0:T(8,128)(2,1)}, bf16[512,128]{1,0:T(8,128)(2,1)S(1)}, u32[]{:S(2)}, u32[]{:S(2)}) collective-permute-start(bf16[512,128]{1,0:T(8,128)(2,1)} %keys.3), channel_id=1, source_target_pairs={{0,8},{4,12},{8,0},{12,4},{16,24},{20,28},{24,16},{28,20},{1,9},{5... | collective-permute-start | bytes 393224 | tf_op jit(solution)/shard_map/ppermute | solution.py:131
  5.9 0.5 %collective-permute-start.6 = (bf16[512,128]{1,0:T(8,128)(2,1)}, bf16[512,128]{1,0:T(8,128)(2,1)S(1)}, u32[]{:S(2)}, u32[]{:S(2)}) collective-permute-start(bf16[512,128]{1,0:T(8,128)(2,1)} %values.3), channel_id=1, source_target_pairs={{0,8},{4,12},{8,0},{12,4},{16,24},{20,28},{24,16},{28,20},{1,9},{5... | collective-permute-start | bytes 393224 | tf_op jit(solution)/shard_map/ppermute | solution.py:131
  6.4 0.0 collective-permute-done
  6.4 0.0 copy-start.4
  6.4 2.8 %collective-permute-start.1 = (bf16[2,2,8,128]{3,2,0,1:T(8,128)(2,1)S(1)}, bf16[2,2,8,128]{3,2,0,1:T(8,128)(2,1)S(1)}, u32[]{:S(2)}, u32[]{:S(2)}) collective-permute-start(bf16[2,2,8,128]{3,2,0,1:T(8,128)(2,1)S(1)} %fusion.1), channel_id=1, source_target_pairs={{0,2},{1,3},{2,0},{3,1},{4,6},{5,7},{6,4},{7,5},{8,10},{9,11},{10,... | collective-permute-start | bytes 24584 | tf_op jit(solution)/shard_map/ppermute | solution.py:131
  9.2 0.0 collective-permute-start.2
  9.2 0.5 %collective-permute-start.3 = (bf16[512,128]{1,0:T(8,128)(2,1)}, bf16[512,128]{1,0:T(8,128)(2,1)S(1)}, u32[]{:S(2)}, u32[]{:S(2)}) collective-permute-start(bf16[512,128]{1,0:T(8,128)(2,1)} %values.3), channel_id=1, source_target_pairs={{0,4},{4,0},{8,12},{12,8},{16,20},{20,16},{24,28},{28,24},{1,5},{5... | collective-permute-start | bytes 393224 | tf_op jit(solution)/shard_map/ppermute | solution.py:131
  9.7 0.6 %copy-done.5 = bf16[1,32]{1,0:T(2,128)(2,1)S(1)} copy-done((bf16[1,32]{1,0:T(2,128)(2,1)S(1)}, bf16[1,32]{1,0:T(2,128)(2,1)}, u32[]{:S(2)}) %copy-start.5) | copy-done | bytes 88
  10.4 0.1 small.1
  10.5 0.5 %collective-permute-done.1 = bf16[2,2,8,128]{3,2,0,1:T(8,128)(2,1)S(1)} collective-permute-done((bf16[2,2,8,128]{3,2,0,1:T(8,128)(2,1)S(1)}, bf16[2,2,8,128]{3,2,0,1:T(8,128)(2,1)S(1)}, u32[]{:S(2)}, u32[]{:S(2)}) %collective-permute-start.1) | collective-permute-done | bytes 8224 | tf_op jit(solution)/shard_map/ppermute | solution.py:131
  11.1 0.0 collective-permute-done.2.k1
  11.1 0.0 collective-permute-done.3.v1
  11.1 1.7 %collective-permute-start.4 = (bf16[128,128]{1,0:T(8,128)(2,1)S(1)}, bf16[128,128]{1,0:T(8,128)(2,1)S(1)}, u32[]{:S(2)}, u32[]{:S(2)}) collective-permute-start(bf16[128,128]{1,0:T(8,128)(2,1)S(1)} %pad_maximum_fusion.1.r0), channel_id=1, source_target_pairs={{0,16},{4,20},{8,24},{12,28},{16,0},{20,4},{24,8},{28,12},{1,17},{... | collective-permute-start | bytes 98312 | tf_op jit(solution)/shard_map/ppermute | solution.py:131
  12.9 0.0 collective-permute-done.5.k2
  12.9 0.0 collective-permute-start.7
  12.9 0.5 %collective-permute-start.8 = (bf16[512,128]{1,0:T(8,128)(2,1)S(1)}, bf16[512,128]{1,0:T(8,128)(2,1)S(1)}, u32[]{:S(2)}, u32[]{:S(2)}) collective-permute-start(bf16[512,128]{1,0:T(8,128)(2,1)S(1)} %collective-permute-done.6.v2), channel_id=1, source_target_pairs={{0,4},{4,0},{8,12},{12,8},{16,20},{20,16},{24,28},{28,24},{1,5},{5... | collective-permute-start | bytes 393224 | tf_op jit(solution)/shard_map/ppermute | solution.py:131
  13.4 1.4 %collective-permute-start.10 = (bf16[128,128]{1,0:T(8,128)(2,1)S(1)}, bf16[128,128]{1,0:T(8,128)(2,1)S(1)}, u32[]{:S(2)}, u32[]{:S(2)}) collective-permute-start(bf16[128,128]{1,0:T(8,128)(2,1)S(1)} %pad_maximum_fusion.1.r0), channel_id=1, source_target_pairs={{0,24},{4,28},{8,16},{12,20},{16,8},{20,12},{24,0},{28,4},{1,25},{... | collective-permute-start | bytes 98312 | tf_op jit(solution)/shard_map/ppermute | solution.py:131
  14.8 0.5 %collective-permute-start.9 = (bf16[128,128]{1,0:T(8,128)(2,1)S(1)}, bf16[128,128]{1,0:T(8,128)(2,1)S(1)}, u32[]{:S(2)}, u32[]{:S(2)}) collective-permute-start(bf16[128,128]{1,0:T(8,128)(2,1)S(1)} %pad_maximum_fusion.1.r0), channel_id=1, source_target_pairs={{0,8},{4,12},{8,0},{12,4},{16,24},{20,28},{24,16},{28,20},{1,9},{5... | collective-permute-start | bytes 98312 | tf_op jit(solution)/shard_map/ppermute | solution.py:131
  15.3 0.0 collective-permute-done.4.r1
  15.3 0.6 %near_terms.1.q_part = f32[64,128]{1,0:T(8,128)S(1)} custom-call(s32[1]{0:T(128)} %bitcast.shard_ref, bf16[128,128]{1,0:T(8,128)(2,1)S(1)} %pad_maximum_fusion.1.r0, bf16[128,128]{1,0:T(8,128)(2,1)S(1)} %collective-permute-done.4.r1, bf16[512,128]{1,0:T(8,128)(2,1)S(1)} %copy-done, bf16[512,128]{1,0:T(8,128)(2,1)S(1)} %copy-done.1, ...), custom_call_target="tpu_custom_call" | custom-call | flops 99999997952 | bytes 100000000 | tf_op jit(solution)/shard_map/near_terms/pallas_call | solution.py:280
  15.9 0.0 collective-permute-done.7.k3
  15.9 0.6 %side_terms.1 = (f32[32,128]{1,0:T(8,128)S(1)}, bf16[32,128]{1,0:T(8,128)(2,1)S(1)}) custom-call(s32[1]{0:T(128)} %bitcast.shard_ref, bf16[128,128]{1,0:T(8,128)(2,1)S(1)} %pad_maximum_fusion.1.r0, bf16[128,128]{1,0:T(8,128)(2,1)S(1)} %collective-permute-done.4.r1, f32[64,128]{1,0:T(8,128)S(1)} %near_terms.1.q_part, ...), custom_call_target="tpu_custom_call" | custom-call | tf_op jit(solution)/shard_map/side_terms/pallas_call | solution.py:280
  16.5 1.6 %collective-permute-start.12 = (bf16[32,128]{1,0:T(8,128)(2,1)S(1)}, bf16[32,128]{1,0:T(8,128)(2,1)S(1)}, u32[]{:S(2)}, u32[]{:S(2)}) collective-permute-start(bf16[32,128]{1,0:T(8,128)(2,1)S(1)} %get-tuple-element.39), channel_id=1, source_target_pairs={{0,16},{4,20},{8,24},{12,28},{16,0},{20,4},{24,8},{28,12},{1,17},{... | collective-permute-start | bytes 24584 | tf_op jit(solution)/shard_map/ppermute | solution.py:131
  18.1 0.1 collective-permute-done.10
  18.2 0.5 %collective-permute-done.9 = bf16[128,128]{1,0:T(8,128)(2,1)S(1)} collective-permute-done((bf16[128,128]{1,0:T(8,128)(2,1)S(1)}, bf16[128,128]{1,0:T(8,128)(2,1)S(1)}, u32[]{:S(2)}, u32[]{:S(2)}) %collective-permute-start.9) | collective-permute-done | bytes 32800 | tf_op jit(solution)/shard_map/ppermute | solution.py:131
  18.7 0.1 collective-permute-start.11
  18.8 0.4 %key_terms.1 = (f32[512,128]{1,0:T(8,128)S(1)}, f32[512,128]{1,0:T(8,128)S(1)}) custom-call(s32[1]{0:T(128)} %bitcast.shard_ref, bf16[4,128,128]{2,1,0:T(8,128)(2,1)S(1)} %pad_maximum_fusion.lane, bf16[512,128]{1,0:T(8,128)(2,1)S(1)} %copy-done, bf16[512,128]{1,0:T(8,128)(2,1)S(1)} %copy-done.1), custom_call_target="tpu_custom_call" | custom-call | flops 1 | bytes 1 | tf_op jit(solution)/shard_map/key_terms/pallas_call | solution.py:280
  19.2 1.0 %collective-permute-done.12.q_back = bf16[32,128]{1,0:T(8,128)(2,1)S(1)} collective-permute-done((bf16[32,128]{1,0:T(8,128)(2,1)S(1)}, bf16[32,128]{1,0:T(8,128)(2,1)S(1)}, u32[]{:S(2)}, u32[]{:S(2)}) %collective-permute-start.12) | collective-permute-done | bytes 8224 | tf_op jit(solution)/shard_map/ppermute | solution.py:131
  20.2 0.0 collective-permute-done.11.lane
  20.2 1.1 %finish.1 = (bf16[32,128]{1,0:T(8,128)(2,1)}, bf16[512,128]{1,0:T(8,128)(2,1)}, bf16[512,128]{1,0:T(8,128)(2,1)}) custom-call(s32[1]{0:T(128)} %bitcast.shard_ref, bf16[4,128,128]{2,1,0:T(8,128)(2,1)S(1)} %collective-permute-done.11.lane, bf16[512,128]{1,0:T(8,128)(2,1)S(1)} %copy-done, bf16[512,128]{1,0:T(8,128)(2,1)S(1)} %copy-done.1, ...), custom_call_target="tpu_custom_call" | custom-call | tf_op jit(solution)/shard_map/finish/pallas_call | solution.py:280
  (21 shorter events, 0.1 us)
Async XLA Ops:
  1.3 5.1 %collective-permute-start = (bf16[2,8,512]{2,1,0:T(8,128)(2,1)S(1)}, bf16[2,8,512]{2,1,0:T(8,128)(2,1)S(1)}, u32[]{:S(2)}, u32[]{:S(2)}) collective-permute-start(bf16[2,8,512]{2,1,0:T(8,128)(2,1)S(1)} %pad_maximum_fusion.2), channel_id=1, source_target_pairs={{0,1},{1,0},{2,3},{3,2},{4,5},{5,4},{6,7},{7,6},{8,9},{9,8},{10,11... | collective-permute-start | bytes 49160 | tf_op jit(solution)/shard_map/ppermute | solution.py:131
  4.4 8.5 %collective-permute-start.5 = (bf16[512,128]{1,0:T(8,128)(2,1)}, bf16[512,128]{1,0:T(8,128)(2,1)S(1)}, u32[]{:S(2)}, u32[]{:S(2)}) collective-permute-start(bf16[512,128]{1,0:T(8,128)(2,1)} %keys.3), channel_id=1, source_target_pairs={{0,8},{4,12},{8,0},{12,4},{16,24},{20,28},{24,16},{28,20},{1,9},{5... | collective-permute-start | bytes 393224 | tf_op jit(solution)/shard_map/ppermute | solution.py:131
  5.9 7.0 %collective-permute-start.6 = (bf16[512,128]{1,0:T(8,128)(2,1)}, bf16[512,128]{1,0:T(8,128)(2,1)S(1)}, u32[]{:S(2)}, u32[]{:S(2)}) collective-permute-start(bf16[512,128]{1,0:T(8,128)(2,1)} %values.3), channel_id=1, source_target_pairs={{0,8},{4,12},{8,0},{12,4},{16,24},{20,28},{24,16},{28,20},{1,9},{5... | collective-permute-start | bytes 393224 | tf_op jit(solution)/shard_map/ppermute | solution.py:131
  6.4 3.3 %copy-start.2 = (bf16[32,128]{1,0:T(8,128)(2,1)S(1)}, bf16[32,128]{1,0:T(8,128)(2,1)}, u32[]{:S(2)}) copy-start(bf16[32,128]{1,0:T(8,128)(2,1)} %queries) | copy-start | bytes 24580
  6.4 3.3 %copy-start.3 = (s32[1,32,4,4]{1,3,2,0:T(4,128)S(1)}, s32[1,32,4,4]{1,3,2,0:T(4,128)}, u32[]{:S(2)}) copy-start(s32[1,32,4,4]{1,3,2,0:T(4,128)} %param.15) | copy-start | bytes 6148
  6.4 3.3 %copy-start.4 = (s32[1,32,4]{1,2,0:T(4,128)S(1)}, s32[1,32,4]{1,2,0:T(4,128)}, u32[]{:S(2)}) copy-start(s32[1,32,4]{1,2,0:T(4,128)} %param.14) | copy-start | bytes 1540
  6.4 4.6 %collective-permute-start.1 = (bf16[2,2,8,128]{3,2,0,1:T(8,128)(2,1)S(1)}, bf16[2,2,8,128]{3,2,0,1:T(8,128)(2,1)S(1)}, u32[]{:S(2)}, u32[]{:S(2)}) collective-permute-start(bf16[2,2,8,128]{3,2,0,1:T(8,128)(2,1)S(1)} %fusion.1), channel_id=1, source_target_pairs={{0,2},{1,3},{2,0},{3,1},{4,6},{5,7},{6,4},{7,5},{8,10},{9,11},{10,... | collective-permute-start | bytes 24584 | tf_op jit(solution)/shard_map/ppermute | solution.py:131
  9.2 1.9 %collective-permute-start.2 = (bf16[512,128]{1,0:T(8,128)(2,1)}, bf16[512,128]{1,0:T(8,128)(2,1)S(1)}, u32[]{:S(2)}, u32[]{:S(2)}) collective-permute-start(bf16[512,128]{1,0:T(8,128)(2,1)} %keys.3), channel_id=1, source_target_pairs={{0,4},{4,0},{8,12},{12,8},{16,20},{20,16},{24,28},{28,24},{1,5},{5... | collective-permute-start | bytes 393224 | tf_op jit(solution)/shard_map/ppermute | solution.py:131
  9.2 1.9 %collective-permute-start.3 = (bf16[512,128]{1,0:T(8,128)(2,1)}, bf16[512,128]{1,0:T(8,128)(2,1)S(1)}, u32[]{:S(2)}, u32[]{:S(2)}) collective-permute-start(bf16[512,128]{1,0:T(8,128)(2,1)} %values.3), channel_id=1, source_target_pairs={{0,4},{4,0},{8,12},{12,8},{16,20},{20,16},{24,28},{28,24},{1,5},{5... | collective-permute-start | bytes 393224 | tf_op jit(solution)/shard_map/ppermute | solution.py:131
  9.7 0.7 %copy-start.5 = (bf16[1,32]{1,0:T(2,128)(2,1)S(1)}, bf16[1,32]{1,0:T(2,128)(2,1)}, u32[]{:S(2)}) copy-start(bf16[1,32]{1,0:T(2,128)(2,1)} %lse) | copy-start | bytes 196
  10.5 4.8 %copy-start = (bf16[512,128]{1,0:T(8,128)(2,1)S(1)}, bf16[512,128]{1,0:T(8,128)(2,1)}, u32[]{:S(2)}) copy-start(bf16[512,128]{1,0:T(8,128)(2,1)} %keys.3) | copy-start | bytes 393220
  10.5 4.8 %copy-start.1 = (bf16[512,128]{1,0:T(8,128)(2,1)S(1)}, bf16[512,128]{1,0:T(8,128)(2,1)}, u32[]{:S(2)}) copy-start(bf16[512,128]{1,0:T(8,128)(2,1)} %values.3) | copy-start | bytes 393220
  11.1 4.2 %collective-permute-start.4 = (bf16[128,128]{1,0:T(8,128)(2,1)S(1)}, bf16[128,128]{1,0:T(8,128)(2,1)S(1)}, u32[]{:S(2)}, u32[]{:S(2)}) collective-permute-start(bf16[128,128]{1,0:T(8,128)(2,1)S(1)} %pad_maximum_fusion.1.r0), channel_id=1, source_target_pairs={{0,16},{4,20},{8,24},{12,28},{16,0},{20,4},{24,8},{28,12},{1,17},{... | collective-permute-start | bytes 98312 | tf_op jit(solution)/shard_map/ppermute | solution.py:131
  12.9 3.1 %collective-permute-start.7 = (bf16[512,128]{1,0:T(8,128)(2,1)S(1)}, bf16[512,128]{1,0:T(8,128)(2,1)S(1)}, u32[]{:S(2)}, u32[]{:S(2)}) collective-permute-start(bf16[512,128]{1,0:T(8,128)(2,1)S(1)} %collective-permute-done.5.k2), channel_id=1, source_target_pairs={{0,4},{4,0},{8,12},{12,8},{16,20},{20,16},{24,28},{28,24},{1,5},{5... | collective-permute-start | bytes 393224 | tf_op jit(solution)/shard_map/ppermute | solution.py:131
  12.9 3.1 %collective-permute-start.8 = (bf16[512,128]{1,0:T(8,128)(2,1)S(1)}, bf16[512,128]{1,0:T(8,128)(2,1)S(1)}, u32[]{:S(2)}, u32[]{:S(2)}) collective-permute-start(bf16[512,128]{1,0:T(8,128)(2,1)S(1)} %collective-permute-done.6.v2), channel_id=1, source_target_pairs={{0,4},{4,0},{8,12},{12,8},{16,20},{20,16},{24,28},{28,24},{1,5},{5... | collective-permute-start | bytes 393224 | tf_op jit(solution)/shard_map/ppermute | solution.py:131
  13.4 4.9 %collective-permute-start.10 = (bf16[128,128]{1,0:T(8,128)(2,1)S(1)}, bf16[128,128]{1,0:T(8,128)(2,1)S(1)}, u32[]{:S(2)}, u32[]{:S(2)}) collective-permute-start(bf16[128,128]{1,0:T(8,128)(2,1)S(1)} %pad_maximum_fusion.1.r0), channel_id=1, source_target_pairs={{0,24},{4,28},{8,16},{12,20},{16,8},{20,12},{24,0},{28,4},{1,25},{... | collective-permute-start | bytes 98312 | tf_op jit(solution)/shard_map/ppermute | solution.py:131
  14.8 3.9 %collective-permute-start.9 = (bf16[128,128]{1,0:T(8,128)(2,1)S(1)}, bf16[128,128]{1,0:T(8,128)(2,1)S(1)}, u32[]{:S(2)}, u32[]{:S(2)}) collective-permute-start(bf16[128,128]{1,0:T(8,128)(2,1)S(1)} %pad_maximum_fusion.1.r0), channel_id=1, source_target_pairs={{0,8},{4,12},{8,0},{12,4},{16,24},{20,28},{24,16},{28,20},{1,9},{5... | collective-permute-start | bytes 98312 | tf_op jit(solution)/shard_map/ppermute | solution.py:131
  16.5 3.7 %collective-permute-start.12 = (bf16[32,128]{1,0:T(8,128)(2,1)S(1)}, bf16[32,128]{1,0:T(8,128)(2,1)S(1)}, u32[]{:S(2)}, u32[]{:S(2)}) collective-permute-start(bf16[32,128]{1,0:T(8,128)(2,1)S(1)} %get-tuple-element.39), channel_id=1, source_target_pairs={{0,16},{4,20},{8,24},{12,28},{16,0},{20,4},{24,8},{28,12},{1,17},{... | collective-permute-start | bytes 24584 | tf_op jit(solution)/shard_map/ppermute | solution.py:131
  18.7 1.5 %collective-permute-start.11 = (bf16[4,128,128]{2,1,0:T(8,128)(2,1)S(1)}, bf16[4,128,128]{2,1,0:T(8,128)(2,1)S(1)}, u32[]{:S(2)}, u32[]{:S(2)}) collective-permute-start(bf16[4,128,128]{2,1,0:T(8,128)(2,1)S(1)} %pad_maximum_fusion.lane), channel_id=1, source_target_pairs={{0,4},{4,0},{8,12},{12,8},{16,20},{20,16},{24,28},{28,24},{1,5},{5... | collective-permute-start | bytes 393224 | tf_op jit(solution)/shard_map/ppermute | solution.py:131

commit v4 on v3

--- a/solution.py
+++ b/solution.py
@@ -174,44 +174,44 @@
     return probs, probs * (dprob - delta)
 
 
-def query_sums(scale, shard, bits, r0, r1, pairs):
+def doubled(r0, r1):
     parts, count = (r0[...], r1[...]), r0.shape[0] // 4
     queries, grads, delta, lse, ids = unpack(parts + parts, count)
-    half, size = 2 * count, queries.shape[1]
     row = lax.broadcasted_iota(jnp.int32, queries.shape, 0)
-    lane = lax.broadcasted_iota(jnp.int32, (1, 2 * half), 1)
 
     def beside(value):
         zero = jnp.zeros_like(value)
         return jnp.concatenate(
-            [jnp.where(row < half, value, zero), jnp.where(row < half, zero, value)], axis=1
+            [jnp.where(row < 2 * count, value, zero), jnp.where(row < 2 * count, zero, value)], axis=1
         )
 
-    queries, grads = beside(queries), beside(grads)
+    return beside(queries), beside(grads), delta, lse, ids
+
+
+def rows_kernel(r0, r1, queries, grads, stats):
+    queries[...], grads[...], delta, lse, ids = doubled(r0, r1)
+    stats[0:1], stats[1:2], stats[8:] = delta, lse, ids
+
+
+def query_kernel(
+    scale, shard_ref, queries, grads, stats, k0, v0, k1, v1, k2, v2, k3, v3, q_own, q_out
+):
+    half, size, count = queries.shape[0] // 2, queries.shape[1] // 2, q_own.shape[0]
+    delta, lse, ids = stats[0:1], stats[1:2], stats[8:]
+    lane = lax.broadcasted_iota(jnp.int32, (1, 2 * half), 1)
     wide, scored = [], []
-    for (left_bit, right_bit), (left, right) in zip(bits, pairs):
-        keys = jnp.concatenate([left[0], right[0]], axis=1)
-        values = jnp.concatenate([left[1], right[1]], axis=1)
+    for bit, left, right in ((0, (k0, v0), (k1, v1)), (2, (k2, v2), (k3, v3))):
+        keys = jnp.concatenate([left[0][...], right[0][...]], axis=1)
+        values = jnp.concatenate([left[1][...], right[1][...]], axis=1)
         blocks = keys.shape[0] // BLK
-        base = jnp.where(lane < half, shard ^ left_bit, shard ^ right_bit) * blocks
+        base = jnp.where(lane < half, shard_ref[0] ^ bit, shard_ref[0] ^ (bit + 1)) * blocks
         offset = chosen_offset(lse, ids, blocks, base)
-        _, dscore = terms(queries, grads, delta, offset, keys, values, scale)
+        _, dscore = terms(queries[...], grads[...], delta, offset, keys, values, scale)
         wide.append(keys)
         scored.append(dscore.T.astype(jnp.bfloat16))
     scored, wide = jnp.concatenate(scored, axis=1), jnp.concatenate(wide, axis=0)
     total = jnp.dot(scored, wide, preferred_element_type=jnp.float32)
-    return total[:half, :size] + total[half:, size:]
-
-
-def near_kernel(scale, shard_ref, r0, r1, k0, v0, k1, v1, q_part):
-    pair = ((k0[...], v0[...]), (k1[...], v1[...]))
-    q_part[...] = query_sums(scale, shard_ref[0], ((0, 1),), r0, r1, (pair,))
-
-
-def side_kernel(scale, shard_ref, r0, r1, q_part, k2, v2, k3, v3, q_own, q_out):
-    count = r0.shape[0] // 4
-    pair = ((k2[...], v2[...]), (k3[...], v3[...]))
-    total = q_part[...] + query_sums(scale, shard_ref[0], ((2, 3),), r0, r1, (pair,))
+    total = total[:half, :size] + total[half:, size:]
     q_own[...] = total[:count]
     q_out[...] = total[count:].astype(q_out.dtype)
 
@@ -321,14 +321,17 @@
     block_y = swap(block, "seq", n_seq, 4)
     block_x = swap(block, "seq", n_seq, 2)
     block_d = swap(block, "seq", n_seq, 6)
-    (q_part,) = kernel(
-        functools.partial(near_kernel, scale), "near_terms", [((2 * count, size), f32)], (seq,),
-        (block, block_y, key_rows, value_rows, keys_core, values_core), flops=10**11,
+    wide = (4 * count, 2 * size)
+    rows = kernel(
+        rows_kernel, "rows", [(wide, bf16), (wide, bf16), ((24, 4 * count), f32)], (),
+        (block, block_y), flops=10**11,
     )
     q_own, q_out = kernel(
-        functools.partial(side_kernel, scale), "side_terms",
+        functools.partial(query_kernel, scale), "query_terms",
         [((count, size), f32), ((count, size), bf16)], (seq,),
-        (block, block_y, q_part, keys_side, values_side, keys_side_core, values_side_core),
+        (*rows, key_rows, value_rows, keys_core, values_core)
+        + (keys_side, values_side, keys_side_core, values_side_core),
+        flops=1,
     )
     _, block_x, block_d = lax.optimization_barrier((q_out, block_x, block_d))
     q_back = swap(q_out, "seq", n_seq, 4)
@@ -336,11 +339,11 @@
     lane_core = swap(lane, "seq", n_seq, 1)
     k_part, v_part = kernel(
         functools.partial(key_kernel, scale), "key_terms", [(kv, f32)] * 2, (seq,),
-        (lane, key_rows, value_rows), flops=1,
+        (lane, key_rows, value_rows), flops=3 * 10**9,
     )
     (q_sum,) = kernel(
         functools.partial(query_sum_kernel, scale), "query_sum", [((count, size), bf16)], (),
-        (q_own, q_back), flops=3 * 10**9,
+        (q_own, q_back), flops=10**9,
     )
     return kernel(
         functools.partial(finish_kernel, scale), "finish",

time: 21.6 us -> 21.6 us (level)
  Pallas kernels: 2.78 us -> 2.51 us
    pallas_call x6, Pallas kernels: 2.78 us -> 2.51 us  [kernel(): pl.pallas_call(body, out_shape=tuple((jax.ShapeDtypeStruct(v, t) for v, t...]
  transfers between devices with their start and end apart: 13 -> 13, of which waited for: 4 -> 5; matrix products, arithmetic and copies ran while one was open for 0% -> 0% of each run, Pallas kernels for 8% -> 7%
where the time goes in v4:
time: 21.6 us; the launch traced here: 21.3 us
  starting transfers between devices  14.2 us (66%)
  Pallas kernels  2.51 us (12%)
  waiting for transfers between devices  2.36 us (11%)
  between operations  0.78 us (4%)
  other arithmetic  0.77 us (4%)
  local copies, waits for them, and re-layouts  0.67 us (3%)
    ppermute x13, starting transfers between devices, swap(): return lax.ppermute(value, axis, [(i, i ^ bit) for i in range(count)])  14.2 us
    pallas_call x6, Pallas kernels, kernel(): pl.pallas_call(body, out_shape=tuple((jax.ShapeDtypeStruct(v, t) for v, t...  2.51 us
    ppermute x13, waiting for transfers between devices, swap(): return lax.ppermute(value, axis, [(i, i ^ bit) for i in range(count)])  2.36 us
    another operation x1, other arithmetic, fast_local(): mine = jnp.stack([out_grad, attn_out])  0.72 us
    unnamed x12, local copies, waits for them, and re-layouts  0.67 us
  transfers between devices with their start and end apart: 13, of which 5 were waited for; matrix products, arithmetic and copies ran while one was open for 0% of the time, Pallas kernels for 7%

profile of v4, /device:TPU:0, one launch (start us, length us, event | category | flops | bytes accessed | tf_op | source)
XLA Modules:
  0.0 21.3 jit_solution(15297341097220886106)
XLA Ops:
  0.6 0.7 %pad_maximum_fusion.2 = bf16[2,8,512]{2,1,0:T(8,128)(2,1)S(1)} fusion(bf16[1,8,512]{2,1,0:T(8,128)(2,1)} %bitcast.31, bf16[1,8,512]{2,1,0:T(8,128)(2,1)} %bitcast.32), kind=kLoop, calls=%fused_computation.7 | loop fusion | flops 8192 | bytes 32768 | tf_op jit(solution)/shard_map/stack | solution.py:290
  1.3 3.0 %collective-permute-start = (bf16[2,8,512]{2,1,0:T(8,128)(2,1)S(1)}, bf16[2,8,512]{2,1,0:T(8,128)(2,1)S(1)}, u32[]{:S(2)}, u32[]{:S(2)}) collective-permute-start(bf16[2,8,512]{2,1,0:T(8,128)(2,1)S(1)} %pad_maximum_fusion.2), channel_id=1, source_target_pairs={{0,1},{1,0},{2,3},{3,2},{4,5},{5,4},{6,7},{7,6},{8,9},{9,8},{10,11... | collective-permute-start | bytes 49160 | tf_op jit(solution)/shard_map/ppermute | solution.py:131
  4.4 1.5 %collective-permute-start.5 = (bf16[512,128]{1,0:T(8,128)(2,1)}, bf16[512,128]{1,0:T(8,128)(2,1)S(1)}, u32[]{:S(2)}, u32[]{:S(2)}) collective-permute-start(bf16[512,128]{1,0:T(8,128)(2,1)} %keys.3), channel_id=1, source_target_pairs={{0,8},{4,12},{8,0},{12,4},{16,24},{20,28},{24,16},{28,20},{1,9},{5... | collective-permute-start | bytes 393224 | tf_op jit(solution)/shard_map/ppermute | solution.py:131
  5.9 0.5 %collective-permute-start.6 = (bf16[512,128]{1,0:T(8,128)(2,1)}, bf16[512,128]{1,0:T(8,128)(2,1)S(1)}, u32[]{:S(2)}, u32[]{:S(2)}) collective-permute-start(bf16[512,128]{1,0:T(8,128)(2,1)} %values.3), channel_id=1, source_target_pairs={{0,8},{4,12},{8,0},{12,4},{16,24},{20,28},{24,16},{28,20},{1,9},{5... | collective-permute-start | bytes 393224 | tf_op jit(solution)/shard_map/ppermute | solution.py:131
  6.4 0.0 collective-permute-done
  6.4 0.0 copy-start.4
  6.4 2.8 %collective-permute-start.1 = (bf16[2,2,8,128]{3,2,0,1:T(8,128)(2,1)S(1)}, bf16[2,2,8,128]{3,2,0,1:T(8,128)(2,1)S(1)}, u32[]{:S(2)}, u32[]{:S(2)}) collective-permute-start(bf16[2,2,8,128]{3,2,0,1:T(8,128)(2,1)S(1)} %fusion.1), channel_id=1, source_target_pairs={{0,2},{1,3},{2,0},{3,1},{4,6},{5,7},{6,4},{7,5},{8,10},{9,11},{10,... | collective-permute-start | bytes 24584 | tf_op jit(solution)/shard_map/ppermute | solution.py:131
  9.2 0.0 collective-permute-start.2
  9.2 0.5 %collective-permute-start.3 = (bf16[512,128]{1,0:T(8,128)(2,1)}, bf16[512,128]{1,0:T(8,128)(2,1)S(1)}, u32[]{:S(2)}, u32[]{:S(2)}) collective-permute-start(bf16[512,128]{1,0:T(8,128)(2,1)} %values.3), channel_id=1, source_target_pairs={{0,4},{4,0},{8,12},{12,8},{16,20},{20,16},{24,28},{28,24},{1,5},{5... | collective-permute-start | bytes 393224 | tf_op jit(solution)/shard_map/ppermute | solution.py:131
  9.7 0.6 %copy-done.5 = bf16[1,32]{1,0:T(2,128)(2,1)S(1)} copy-done((bf16[1,32]{1,0:T(2,128)(2,1)S(1)}, bf16[1,32]{1,0:T(2,128)(2,1)}, u32[]{:S(2)}) %copy-start.5) | copy-done | bytes 88
  10.4 0.1 small.1
  10.5 0.5 %collective-permute-done.1 = bf16[2,2,8,128]{3,2,0,1:T(8,128)(2,1)S(1)} collective-permute-done((bf16[2,2,8,128]{3,2,0,1:T(8,128)(2,1)S(1)}, bf16[2,2,8,128]{3,2,0,1:T(8,128)(2,1)S(1)}, u32[]{:S(2)}, u32[]{:S(2)}) %collective-permute-start.1) | collective-permute-done | bytes 8224 | tf_op jit(solution)/shard_map/ppermute | solution.py:131
  11.1 0.0 collective-permute-done.2.k1
  11.1 0.0 collective-permute-done.3.v1
  11.1 1.7 %collective-permute-start.4 = (bf16[128,128]{1,0:T(8,128)(2,1)S(1)}, bf16[128,128]{1,0:T(8,128)(2,1)S(1)}, u32[]{:S(2)}, u32[]{:S(2)}) collective-permute-start(bf16[128,128]{1,0:T(8,128)(2,1)S(1)} %pad_maximum_fusion.1.r0), channel_id=1, source_target_pairs={{0,16},{4,20},{8,24},{12,28},{16,0},{20,4},{24,8},{28,12},{1,17},{... | collective-permute-start | bytes 98312 | tf_op jit(solution)/shard_map/ppermute | solution.py:131
  12.9 0.0 collective-permute-done.6.v2
  12.9 0.5 %collective-permute-start.8 = (bf16[512,128]{1,0:T(8,128)(2,1)S(1)}, bf16[512,128]{1,0:T(8,128)(2,1)S(1)}, u32[]{:S(2)}, u32[]{:S(2)}) collective-permute-start(bf16[512,128]{1,0:T(8,128)(2,1)S(1)} %collective-permute-done.6.v2), channel_id=1, source_target_pairs={{0,4},{4,0},{8,12},{12,8},{16,20},{20,16},{24,28},{28,24},{1,5},{5... | collective-permute-start | bytes 393224 | tf_op jit(solution)/shard_map/ppermute | solution.py:131
  13.4 1.4 %collective-permute-start.10 = (bf16[128,128]{1,0:T(8,128)(2,1)S(1)}, bf16[128,128]{1,0:T(8,128)(2,1)S(1)}, u32[]{:S(2)}, u32[]{:S(2)}) collective-permute-start(bf16[128,128]{1,0:T(8,128)(2,1)S(1)} %pad_maximum_fusion.1.r0), channel_id=1, source_target_pairs={{0,24},{4,28},{8,16},{12,20},{16,8},{20,12},{24,0},{28,4},{1,25},{... | collective-permute-start | bytes 98312 | tf_op jit(solution)/shard_map/ppermute | solution.py:131
  14.8 0.5 %collective-permute-start.9 = (bf16[128,128]{1,0:T(8,128)(2,1)S(1)}, bf16[128,128]{1,0:T(8,128)(2,1)S(1)}, u32[]{:S(2)}, u32[]{:S(2)}) collective-permute-start(bf16[128,128]{1,0:T(8,128)(2,1)S(1)} %pad_maximum_fusion.1.r0), channel_id=1, source_target_pairs={{0,8},{4,12},{8,0},{12,4},{16,24},{20,28},{24,16},{28,20},{1,9},{5... | collective-permute-start | bytes 98312 | tf_op jit(solution)/shard_map/ppermute | solution.py:131
  15.3 0.0 collective-permute-done.4.r1
  15.3 0.2 rows.1
  15.5 0.0 collective-permute-done.7.k3
  15.5 0.0 collective-permute-done.8.v3
  15.5 0.7 %query_terms.1 = (f32[32,128]{1,0:T(8,128)S(1)}, bf16[32,128]{1,0:T(8,128)(2,1)S(1)}) custom-call(s32[1]{0:T(128)} %bitcast.shard_ref, bf16[128,256]{1,0:T(8,128)(2,1)S(1)} %get-tuple-element.38.queries, bf16[128,256]{1,0:T(8,128)(2,1)S(1)} %get-tuple-element.39.grads, f32[24,128]{1,0:T(8,128)S(1)} %get-tuple-element.40.stats, bf16[512,128]{1,0:T(8,128)(2,1)S(1)} %copy-done, ...), custom_call_target="tpu_custom_call" | custom-call | flops 1 | bytes 1 | tf_op jit(solution)/shard_map/query_terms/pallas_call | solution.py:280
  16.2 1.6 %collective-permute-start.12 = (bf16[32,128]{1,0:T(8,128)(2,1)S(1)}, bf16[32,128]{1,0:T(8,128)(2,1)S(1)}, u32[]{:S(2)}, u32[]{:S(2)}) collective-permute-start(bf16[32,128]{1,0:T(8,128)(2,1)S(1)} %get-tuple-element.45), channel_id=1, source_target_pairs={{0,16},{4,20},{8,24},{12,28},{16,0},{20,4},{24,8},{28,12},{1,17},{... | collective-permute-start | bytes 24584 | tf_op jit(solution)/shard_map/ppermute | solution.py:131
  17.8 0.4 %collective-permute-done.10 = bf16[128,128]{1,0:T(8,128)(2,1)S(1)} collective-permute-done((bf16[128,128]{1,0:T(8,128)(2,1)S(1)}, bf16[128,128]{1,0:T(8,128)(2,1)S(1)}, u32[]{:S(2)}, u32[]{:S(2)}) %collective-permute-start.10) | collective-permute-done | bytes 32800 | tf_op jit(solution)/shard_map/ppermute | solution.py:131
  18.2 0.5 %collective-permute-done.9 = bf16[128,128]{1,0:T(8,128)(2,1)S(1)} collective-permute-done((bf16[128,128]{1,0:T(8,128)(2,1)S(1)}, bf16[128,128]{1,0:T(8,128)(2,1)S(1)}, u32[]{:S(2)}, u32[]{:S(2)}) %collective-permute-start.9) | collective-permute-done | bytes 32800 | tf_op jit(solution)/shard_map/ppermute | solution.py:131
  18.7 0.1 collective-permute-start.11
  18.8 0.4 %key_terms.1 = (f32[512,128]{1,0:T(8,128)S(1)}, f32[512,128]{1,0:T(8,128)S(1)}) custom-call(s32[1]{0:T(128)} %bitcast.shard_ref, bf16[4,128,128]{2,1,0:T(8,128)(2,1)S(1)} %pad_maximum_fusion.lane, bf16[512,128]{1,0:T(8,128)(2,1)S(1)} %copy-done, bf16[512,128]{1,0:T(8,128)(2,1)S(1)} %copy-done.1), custom_call_target="tpu_custom_call" | custom-call | flops 3000000000 | bytes 3000000 | tf_op jit(solution)/shard_map/key_terms/pallas_call | solution.py:280
  19.2 0.7 %collective-permute-done.12.q_back = bf16[32,128]{1,0:T(8,128)(2,1)S(1)} collective-permute-done((bf16[32,128]{1,0:T(8,128)(2,1)S(1)}, bf16[32,128]{1,0:T(8,128)(2,1)S(1)}, u32[]{:S(2)}, u32[]{:S(2)}) %collective-permute-start.12) | collective-permute-done | bytes 8224 | tf_op jit(solution)/shard_map/ppermute | solution.py:131
  20.0 0.2 collective-permute-done.11.lane
  20.2 1.1 %finish.1 = (bf16[32,128]{1,0:T(8,128)(2,1)}, bf16[512,128]{1,0:T(8,128)(2,1)}, bf16[512,128]{1,0:T(8,128)(2,1)}) custom-call(s32[1]{0:T(128)} %bitcast.shard_ref, bf16[4,128,128]{2,1,0:T(8,128)(2,1)S(1)} %collective-permute-done.11.lane, bf16[512,128]{1,0:T(8,128)(2,1)S(1)} %copy-done, bf16[512,128]{1,0:T(8,128)(2,1)S(1)} %copy-done.1, ...), custom_call_target="tpu_custom_call" | custom-call | tf_op jit(solution)/shard_map/finish/pallas_call | solution.py:280
  (21 shorter events, 0.1 us)
Async XLA Ops:
  1.3 5.1 %collective-permute-start = (bf16[2,8,512]{2,1,0:T(8,128)(2,1)S(1)}, bf16[2,8,512]{2,1,0:T(8,128)(2,1)S(1)}, u32[]{:S(2)}, u32[]{:S(2)}) collective-permute-start(bf16[2,8,512]{2,1,0:T(8,128)(2,1)S(1)} %pad_maximum_fusion.2), channel_id=1, source_target_pairs={{0,1},{1,0},{2,3},{3,2},{4,5},{5,4},{6,7},{7,6},{8,9},{9,8},{10,11... | collective-permute-start | bytes 49160 | tf_op jit(solution)/shard_map/ppermute | solution.py:131
  4.4 8.5 %collective-permute-start.5 = (bf16[512,128]{1,0:T(8,128)(2,1)}, bf16[512,128]{1,0:T(8,128)(2,1)S(1)}, u32[]{:S(2)}, u32[]{:S(2)}) collective-permute-start(bf16[512,128]{1,0:T(8,128)(2,1)} %keys.3), channel_id=1, source_target_pairs={{0,8},{4,12},{8,0},{12,4},{16,24},{20,28},{24,16},{28,20},{1,9},{5... | collective-permute-start | bytes 393224 | tf_op jit(solution)/shard_map/ppermute | solution.py:131
  5.9 7.0 %collective-permute-start.6 = (bf16[512,128]{1,0:T(8,128)(2,1)}, bf16[512,128]{1,0:T(8,128)(2,1)S(1)}, u32[]{:S(2)}, u32[]{:S(2)}) collective-permute-start(bf16[512,128]{1,0:T(8,128)(2,1)} %values.3), channel_id=1, source_target_pairs={{0,8},{4,12},{8,0},{12,4},{16,24},{20,28},{24,16},{28,20},{1,9},{5... | collective-permute-start | bytes 393224 | tf_op jit(solution)/shard_map/ppermute | solution.py:131
  6.4 3.3 %copy-start.2 = (bf16[32,128]{1,0:T(8,128)(2,1)S(1)}, bf16[32,128]{1,0:T(8,128)(2,1)}, u32[]{:S(2)}) copy-start(bf16[32,128]{1,0:T(8,128)(2,1)} %queries) | copy-start | bytes 24580
  6.4 3.3 %copy-start.3 = (s32[1,32,4,4]{1,3,2,0:T(4,128)S(1)}, s32[1,32,4,4]{1,3,2,0:T(4,128)}, u32[]{:S(2)}) copy-start(s32[1,32,4,4]{1,3,2,0:T(4,128)} %param.15) | copy-start | bytes 6148
  6.4 3.3 %copy-start.4 = (s32[1,32,4]{1,2,0:T(4,128)S(1)}, s32[1,32,4]{1,2,0:T(4,128)}, u32[]{:S(2)}) copy-start(s32[1,32,4]{1,2,0:T(4,128)} %param.14) | copy-start | bytes 1540
  6.4 4.6 %collective-permute-start.1 = (bf16[2,2,8,128]{3,2,0,1:T(8,128)(2,1)S(1)}, bf16[2,2,8,128]{3,2,0,1:T(8,128)(2,1)S(1)}, u32[]{:S(2)}, u32[]{:S(2)}) collective-permute-start(bf16[2,2,8,128]{3,2,0,1:T(8,128)(2,1)S(1)} %fusion.1), channel_id=1, source_target_pairs={{0,2},{1,3},{2,0},{3,1},{4,6},{5,7},{6,4},{7,5},{8,10},{9,11},{10,... | collective-permute-start | bytes 24584 | tf_op jit(solution)/shard_map/ppermute | solution.py:131
  9.2 1.9 %collective-permute-start.2 = (bf16[512,128]{1,0:T(8,128)(2,1)}, bf16[512,128]{1,0:T(8,128)(2,1)S(1)}, u32[]{:S(2)}, u32[]{:S(2)}) collective-permute-start(bf16[512,128]{1,0:T(8,128)(2,1)} %keys.3), channel_id=1, source_target_pairs={{0,4},{4,0},{8,12},{12,8},{16,20},{20,16},{24,28},{28,24},{1,5},{5... | collective-permute-start | bytes 393224 | tf_op jit(solution)/shard_map/ppermute | solution.py:131
  9.2 1.9 %collective-permute-start.3 = (bf16[512,128]{1,0:T(8,128)(2,1)}, bf16[512,128]{1,0:T(8,128)(2,1)S(1)}, u32[]{:S(2)}, u32[]{:S(2)}) collective-permute-start(bf16[512,128]{1,0:T(8,128)(2,1)} %values.3), channel_id=1, source_target_pairs={{0,4},{4,0},{8,12},{12,8},{16,20},{20,16},{24,28},{28,24},{1,5},{5... | collective-permute-start | bytes 393224 | tf_op jit(solution)/shard_map/ppermute | solution.py:131
  9.7 0.7 %copy-start.5 = (bf16[1,32]{1,0:T(2,128)(2,1)S(1)}, bf16[1,32]{1,0:T(2,128)(2,1)}, u32[]{:S(2)}) copy-start(bf16[1,32]{1,0:T(2,128)(2,1)} %lse) | copy-start | bytes 196
  11.1 4.2 %collective-permute-start.4 = (bf16[128,128]{1,0:T(8,128)(2,1)S(1)}, bf16[128,128]{1,0:T(8,128)(2,1)S(1)}, u32[]{:S(2)}, u32[]{:S(2)}) collective-permute-start(bf16[128,128]{1,0:T(8,128)(2,1)S(1)} %pad_maximum_fusion.1.r0), channel_id=1, source_target_pairs={{0,16},{4,20},{8,24},{12,28},{16,0},{20,4},{24,8},{28,12},{1,17},{... | collective-permute-start | bytes 98312 | tf_op jit(solution)/shard_map/ppermute | solution.py:131
  12.9 2.7 %copy-start = (bf16[512,128]{1,0:T(8,128)(2,1)S(1)}, bf16[512,128]{1,0:T(8,128)(2,1)}, u32[]{:S(2)}) copy-start(bf16[512,128]{1,0:T(8,128)(2,1)} %keys.3) | copy-start | bytes 393220
  12.9 2.7 %copy-start.1 = (bf16[512,128]{1,0:T(8,128)(2,1)S(1)}, bf16[512,128]{1,0:T(8,128)(2,1)}, u32[]{:S(2)}) copy-start(bf16[512,128]{1,0:T(8,128)(2,1)} %values.3) | copy-start | bytes 393220
  12.9 2.6 %collective-permute-start.7 = (bf16[512,128]{1,0:T(8,128)(2,1)S(1)}, bf16[512,128]{1,0:T(8,128)(2,1)S(1)}, u32[]{:S(2)}, u32[]{:S(2)}) collective-permute-start(bf16[512,128]{1,0:T(8,128)(2,1)S(1)} %collective-permute-done.5.k2), channel_id=1, source_target_pairs={{0,4},{4,0},{8,12},{12,8},{16,20},{20,16},{24,28},{28,24},{1,5},{5... | collective-permute-start | bytes 393224 | tf_op jit(solution)/shard_map/ppermute | solution.py:131
  12.9 2.6 %collective-permute-start.8 = (bf16[512,128]{1,0:T(8,128)(2,1)S(1)}, bf16[512,128]{1,0:T(8,128)(2,1)S(1)}, u32[]{:S(2)}, u32[]{:S(2)}) collective-permute-start(bf16[512,128]{1,0:T(8,128)(2,1)S(1)} %collective-permute-done.6.v2), channel_id=1, source_target_pairs={{0,4},{4,0},{8,12},{12,8},{16,20},{20,16},{24,28},{28,24},{1,5},{5... | collective-permute-start | bytes 393224 | tf_op jit(solution)/shard_map/ppermute | solution.py:131
  13.4 4.8 %collective-permute-start.10 = (bf16[128,128]{1,0:T(8,128)(2,1)S(1)}, bf16[128,128]{1,0:T(8,128)(2,1)S(1)}, u32[]{:S(2)}, u32[]{:S(2)}) collective-permute-start(bf16[128,128]{1,0:T(8,128)(2,1)S(1)} %pad_maximum_fusion.1.r0), channel_id=1, source_target_pairs={{0,24},{4,28},{8,16},{12,20},{16,8},{20,12},{24,0},{28,4},{1,25},{... | collective-permute-start | bytes 98312 | tf_op jit(solution)/shard_map/ppermute | solution.py:131
  14.8 3.9 %collective-permute-start.9 = (bf16[128,128]{1,0:T(8,128)(2,1)S(1)}, bf16[128,128]{1,0:T(8,128)(2,1)S(1)}, u32[]{:S(2)}, u32[]{:S(2)}) collective-permute-start(bf16[128,128]{1,0:T(8,128)(2,1)S(1)} %pad_maximum_fusion.1.r0), channel_id=1, source_target_pairs={{0,8},{4,12},{8,0},{12,4},{16,24},{20,28},{24,16},{28,20},{1,9},{5... | collective-permute-start | bytes 98312 | tf_op jit(solution)/shard_map/ppermute | solution.py:131
  16.2 3.7 %collective-permute-start.12 = (bf16[32,128]{1,0:T(8,128)(2,1)S(1)}, bf16[32,128]{1,0:T(8,128)(2,1)S(1)}, u32[]{:S(2)}, u32[]{:S(2)}) collective-permute-start(bf16[32,128]{1,0:T(8,128)(2,1)S(1)} %get-tuple-element.45), channel_id=1, source_target_pairs={{0,16},{4,20},{8,24},{12,28},{16,0},{20,4},{24,8},{28,12},{1,17},{... | collective-permute-start | bytes 24584 | tf_op jit(solution)/shard_map/ppermute | solution.py:131
  18.7 1.4 %collective-permute-start.11 = (bf16[4,128,128]{2,1,0:T(8,128)(2,1)S(1)}, bf16[4,128,128]{2,1,0:T(8,128)(2,1)S(1)}, u32[]{:S(2)}, u32[]{:S(2)}) collective-permute-start(bf16[4,128,128]{2,1,0:T(8,128)(2,1)S(1)} %pad_maximum_fusion.lane), channel_id=1, source_target_pairs={{0,4},{4,0},{8,12},{12,8},{16,20},{20,16},{24,28},{28,24},{1,5},{5... | collective-permute-start | bytes 393224 | tf_op jit(solution)/shard_map/ppermute | solution.py:131

commit v5 on v4

--- a/solution.py
+++ b/solution.py
@@ -135,11 +135,10 @@
     product = left.astype(jnp.float32) * right.astype(jnp.float32)
     high = product.astype(jnp.bfloat16)
     low = (product - high.astype(jnp.float32)).astype(jnp.bfloat16)
-    ones = jnp.ones((8, product.shape[1]), jnp.bfloat16)
+    both = jnp.concatenate([high, low], axis=1)
+    ones = jnp.ones((8, both.shape[1]), jnp.bfloat16)
     contract = (((1,), (1,)), ((), ()))
-    total = lax.dot_general(ones, high, contract, preferred_element_type=jnp.float32)
-    total = total + lax.dot_general(ones, low, contract, preferred_element_type=jnp.float32)
-    return total[0:1]
+    return lax.dot_general(ones, both, contract, preferred_element_type=jnp.float32)[0:1]
 
 
 def unpack(parts, count):

time: 21.6 us -> 21.5 us (level)
  transfers between devices with their start and end apart: 13 -> 13, of which waited for: 5 -> 5; matrix products, arithmetic and copies ran while one was open for 0% -> 0% of each run, Pallas kernels for 7% -> 6%
where the time goes in v5:
time: 21.5 us; the launch traced here: 21.3 us
  starting transfers between devices  14.2 us (66%)
  Pallas kernels  2.46 us (11%)
  waiting for transfers between devices  2.39 us (11%)
  other arithmetic  0.77 us (4%)
  between operations  0.77 us (4%)
  local copies, waits for them, and re-layouts  0.69 us (3%)
    ppermute x13, starting transfers between devices, swap(): return lax.ppermute(value, axis, [(i, i ^ bit) for i in range(count)])  14.2 us
    pallas_call x6, Pallas kernels, kernel(): pl.pallas_call(body, out_shape=tuple((jax.ShapeDtypeStruct(v, t) for v, t...  2.46 us
    ppermute x13, waiting for transfers between devices, swap(): return lax.ppermute(value, axis, [(i, i ^ bit) for i in range(count)])  2.39 us
    another operation x1, other arithmetic, fast_local(): mine = jnp.stack([out_grad, attn_out])  0.72 us
    unnamed x12, local copies, waits for them, and re-layouts  0.68 us
  transfers between devices with their start and end apart: 13, of which 5 were waited for; matrix products, arithmetic and copies ran while one was open for 0% of the time, Pallas kernels for 6%

profile of v5, /device:TPU:0, one launch (start us, length us, event | category | flops | bytes accessed | tf_op | source)
XLA Modules:
  0.0 21.3 jit_solution(12769033856031339907)
XLA Ops:
  0.6 0.7 %pad_maximum_fusion.2 = bf16[2,8,512]{2,1,0:T(8,128)(2,1)S(1)} fusion(bf16[1,8,512]{2,1,0:T(8,128)(2,1)} %bitcast.31, bf16[1,8,512]{2,1,0:T(8,128)(2,1)} %bitcast.32), kind=kLoop, calls=%fused_computation.7 | loop fusion | flops 8192 | bytes 32768 | tf_op jit(solution)/shard_map/stack | solution.py:289
  1.3 3.0 %collective-permute-start = (bf16[2,8,512]{2,1,0:T(8,128)(2,1)S(1)}, bf16[2,8,512]{2,1,0:T(8,128)(2,1)S(1)}, u32[]{:S(2)}, u32[]{:S(2)}) collective-permute-start(bf16[2,8,512]{2,1,0:T(8,128)(2,1)S(1)} %pad_maximum_fusion.2), channel_id=1, source_target_pairs={{0,1},{1,0},{2,3},{3,2},{4,5},{5,4},{6,7},{7,6},{8,9},{9,8},{10,11... | collective-permute-start | bytes 49160 | tf_op jit(solution)/shard_map/ppermute | solution.py:131
  4.4 1.5 %collective-permute-start.5 = (bf16[512,128]{1,0:T(8,128)(2,1)}, bf16[512,128]{1,0:T(8,128)(2,1)S(1)}, u32[]{:S(2)}, u32[]{:S(2)}) collective-permute-start(bf16[512,128]{1,0:T(8,128)(2,1)} %keys.3), channel_id=1, source_target_pairs={{0,8},{4,12},{8,0},{12,4},{16,24},{20,28},{24,16},{28,20},{1,9},{5... | collective-permute-start | bytes 393224 | tf_op jit(solution)/shard_map/ppermute | solution.py:131
  5.9 0.5 %collective-permute-start.6 = (bf16[512,128]{1,0:T(8,128)(2,1)}, bf16[512,128]{1,0:T(8,128)(2,1)S(1)}, u32[]{:S(2)}, u32[]{:S(2)}) collective-permute-start(bf16[512,128]{1,0:T(8,128)(2,1)} %values.3), channel_id=1, source_target_pairs={{0,8},{4,12},{8,0},{12,4},{16,24},{20,28},{24,16},{28,20},{1,9},{5... | collective-permute-start | bytes 393224 | tf_op jit(solution)/shard_map/ppermute | solution.py:131
  6.4 0.0 collective-permute-done
  6.4 0.0 copy-start.4
  6.4 2.8 %collective-permute-start.1 = (bf16[2,2,8,128]{3,2,0,1:T(8,128)(2,1)S(1)}, bf16[2,2,8,128]{3,2,0,1:T(8,128)(2,1)S(1)}, u32[]{:S(2)}, u32[]{:S(2)}) collective-permute-start(bf16[2,2,8,128]{3,2,0,1:T(8,128)(2,1)S(1)} %fusion.1), channel_id=1, source_target_pairs={{0,2},{1,3},{2,0},{3,1},{4,6},{5,7},{6,4},{7,5},{8,10},{9,11},{10,... | collective-permute-start | bytes 24584 | tf_op jit(solution)/shard_map/ppermute | solution.py:131
  9.2 0.0 collective-permute-start.2
  9.2 0.5 %collective-permute-start.3 = (bf16[512,128]{1,0:T(8,128)(2,1)}, bf16[512,128]{1,0:T(8,128)(2,1)S(1)}, u32[]{:S(2)}, u32[]{:S(2)}) collective-permute-start(bf16[512,128]{1,0:T(8,128)(2,1)} %values.3), channel_id=1, source_target_pairs={{0,4},{4,0},{8,12},{12,8},{16,20},{20,16},{24,28},{28,24},{1,5},{5... | collective-permute-start | bytes 393224 | tf_op jit(solution)/shard_map/ppermute | solution.py:131
  9.7 0.6 %copy-done.5 = bf16[1,32]{1,0:T(2,128)(2,1)S(1)} copy-done((bf16[1,32]{1,0:T(2,128)(2,1)S(1)}, bf16[1,32]{1,0:T(2,128)(2,1)}, u32[]{:S(2)}) %copy-start.5) | copy-done | bytes 88
  10.4 0.1 small.1
  10.5 0.5 %collective-permute-done.1 = bf16[2,2,8,128]{3,2,0,1:T(8,128)(2,1)S(1)} collective-permute-done((bf16[2,2,8,128]{3,2,0,1:T(8,128)(2,1)S(1)}, bf16[2,2,8,128]{3,2,0,1:T(8,128)(2,1)S(1)}, u32[]{:S(2)}, u32[]{:S(2)}) %collective-permute-start.1) | collective-permute-done | bytes 8224 | tf_op jit(solution)/shard_map/ppermute | solution.py:131
  11.1 0.0 collective-permute-done.2.k1
  11.1 0.0 collective-permute-done.3.v1
  11.1 1.7 %collective-permute-start.4 = (bf16[128,128]{1,0:T(8,128)(2,1)S(1)}, bf16[128,128]{1,0:T(8,128)(2,1)S(1)}, u32[]{:S(2)}, u32[]{:S(2)}) collective-permute-start(bf16[128,128]{1,0:T(8,128)(2,1)S(1)} %pad_maximum_fusion.1.r0), channel_id=1, source_target_pairs={{0,16},{4,20},{8,24},{12,28},{16,0},{20,4},{24,8},{28,12},{1,17},{... | collective-permute-start | bytes 98312 | tf_op jit(solution)/shard_map/ppermute | solution.py:131
  12.9 0.0 collective-permute-done.5.k2
  12.9 0.0 collective-permute-start.7
  12.9 0.5 %collective-permute-start.8 = (bf16[512,128]{1,0:T(8,128)(2,1)S(1)}, bf16[512,128]{1,0:T(8,128)(2,1)S(1)}, u32[]{:S(2)}, u32[]{:S(2)}) collective-permute-start(bf16[512,128]{1,0:T(8,128)(2,1)S(1)} %collective-permute-done.6.v2), channel_id=1, source_target_pairs={{0,4},{4,0},{8,12},{12,8},{16,20},{20,16},{24,28},{28,24},{1,5},{5... | collective-permute-start | bytes 393224 | tf_op jit(solution)/shard_map/ppermute | solution.py:131
  13.4 1.4 %collective-permute-start.10 = (bf16[128,128]{1,0:T(8,128)(2,1)S(1)}, bf16[128,128]{1,0:T(8,128)(2,1)S(1)}, u32[]{:S(2)}, u32[]{:S(2)}) collective-permute-start(bf16[128,128]{1,0:T(8,128)(2,1)S(1)} %pad_maximum_fusion.1.r0), channel_id=1, source_target_pairs={{0,24},{4,28},{8,16},{12,20},{16,8},{20,12},{24,0},{28,4},{1,25},{... | collective-permute-start | bytes 98312 | tf_op jit(solution)/shard_map/ppermute | solution.py:131
  14.8 0.5 %collective-permute-start.9 = (bf16[128,128]{1,0:T(8,128)(2,1)S(1)}, bf16[128,128]{1,0:T(8,128)(2,1)S(1)}, u32[]{:S(2)}, u32[]{:S(2)}) collective-permute-start(bf16[128,128]{1,0:T(8,128)(2,1)S(1)} %pad_maximum_fusion.1.r0), channel_id=1, source_target_pairs={{0,8},{4,12},{8,0},{12,4},{16,24},{20,28},{24,16},{28,20},{1,9},{5... | collective-permute-start | bytes 98312 | tf_op jit(solution)/shard_map/ppermute | solution.py:131
  15.3 0.0 collective-permute-done.4.r1
  15.3 0.1 rows.1
  15.5 0.0 copy-done
  15.5 0.7 %query_terms.1 = (f32[32,128]{1,0:T(8,128)S(1)}, bf16[32,128]{1,0:T(8,128)(2,1)S(1)}) custom-call(s32[1]{0:T(128)} %bitcast.shard_ref, bf16[128,256]{1,0:T(8,128)(2,1)S(1)} %get-tuple-element.38.queries, bf16[128,256]{1,0:T(8,128)(2,1)S(1)} %get-tuple-element.39.grads, f32[24,128]{1,0:T(8,128)S(1)} %get-tuple-element.40.stats, bf16[512,128]{1,0:T(8,128)(2,1)S(1)} %copy-done, ...), custom_call_target="tpu_custom_call" | custom-call | flops 1 | bytes 1 | tf_op jit(solution)/shard_map/query_terms/pallas_call | solution.py:279
  16.2 1.6 %collective-permute-start.12 = (bf16[32,128]{1,0:T(8,128)(2,1)S(1)}, bf16[32,128]{1,0:T(8,128)(2,1)S(1)}, u32[]{:S(2)}, u32[]{:S(2)}) collective-permute-start(bf16[32,128]{1,0:T(8,128)(2,1)S(1)} %get-tuple-element.45), channel_id=1, source_target_pairs={{0,16},{4,20},{8,24},{12,28},{16,0},{20,4},{24,8},{28,12},{1,17},{... | collective-permute-start | bytes 24584 | tf_op jit(solution)/shard_map/ppermute | solution.py:131
  17.8 0.4 %collective-permute-done.10 = bf16[128,128]{1,0:T(8,128)(2,1)S(1)} collective-permute-done((bf16[128,128]{1,0:T(8,128)(2,1)S(1)}, bf16[128,128]{1,0:T(8,128)(2,1)S(1)}, u32[]{:S(2)}, u32[]{:S(2)}) %collective-permute-start.10) | collective-permute-done | bytes 32800 | tf_op jit(solution)/shard_map/ppermute | solution.py:131
  18.2 0.5 %collective-permute-done.9 = bf16[128,128]{1,0:T(8,128)(2,1)S(1)} collective-permute-done((bf16[128,128]{1,0:T(8,128)(2,1)S(1)}, bf16[128,128]{1,0:T(8,128)(2,1)S(1)}, u32[]{:S(2)}, u32[]{:S(2)}) %collective-permute-start.9) | collective-permute-done | bytes 32800 | tf_op jit(solution)/shard_map/ppermute | solution.py:131
  18.7 0.1 collective-permute-start.11
  18.8 0.4 %key_terms.1 = (f32[512,128]{1,0:T(8,128)S(1)}, f32[512,128]{1,0:T(8,128)S(1)}) custom-call(s32[1]{0:T(128)} %bitcast.shard_ref, bf16[4,128,128]{2,1,0:T(8,128)(2,1)S(1)} %pad_maximum_fusion.lane, bf16[512,128]{1,0:T(8,128)(2,1)S(1)} %copy-done, bf16[512,128]{1,0:T(8,128)(2,1)S(1)} %copy-done.1), custom_call_target="tpu_custom_call" | custom-call | flops 3000000000 | bytes 3000000 | tf_op jit(solution)/shard_map/key_terms/pallas_call | solution.py:279
  19.2 0.7 %collective-permute-done.12.q_back = bf16[32,128]{1,0:T(8,128)(2,1)S(1)} collective-permute-done((bf16[32,128]{1,0:T(8,128)(2,1)S(1)}, bf16[32,128]{1,0:T(8,128)(2,1)S(1)}, u32[]{:S(2)}, u32[]{:S(2)}) %collective-permute-start.12) | collective-permute-done | bytes 8224 | tf_op jit(solution)/shard_map/ppermute | solution.py:131
  20.0 0.2 collective-permute-done.11.lane
  20.2 1.1 %finish.1 = (bf16[32,128]{1,0:T(8,128)(2,1)}, bf16[512,128]{1,0:T(8,128)(2,1)}, bf16[512,128]{1,0:T(8,128)(2,1)}) custom-call(s32[1]{0:T(128)} %bitcast.shard_ref, bf16[4,128,128]{2,1,0:T(8,128)(2,1)S(1)} %collective-permute-done.11.lane, bf16[512,128]{1,0:T(8,128)(2,1)S(1)} %copy-done, bf16[512,128]{1,0:T(8,128)(2,1)S(1)} %copy-done.1, ...), custom_call_target="tpu_custom_call" | custom-call | tf_op jit(solution)/shard_map/finish/pallas_call | solution.py:279
  (21 shorter events, 0.1 us)
Async XLA Ops:
  1.3 5.1 %collective-permute-start = (bf16[2,8,512]{2,1,0:T(8,128)(2,1)S(1)}, bf16[2,8,512]{2,1,0:T(8,128)(2,1)S(1)}, u32[]{:S(2)}, u32[]{:S(2)}) collective-permute-start(bf16[2,8,512]{2,1,0:T(8,128)(2,1)S(1)} %pad_maximum_fusion.2), channel_id=1, source_target_pairs={{0,1},{1,0},{2,3},{3,2},{4,5},{5,4},{6,7},{7,6},{8,9},{9,8},{10,11... | collective-permute-start | bytes 49160 | tf_op jit(solution)/shard_map/ppermute | solution.py:131
  4.4 8.5 %collective-permute-start.5 = (bf16[512,128]{1,0:T(8,128)(2,1)}, bf16[512,128]{1,0:T(8,128)(2,1)S(1)}, u32[]{:S(2)}, u32[]{:S(2)}) collective-permute-start(bf16[512,128]{1,0:T(8,128)(2,1)} %keys.3), channel_id=1, source_target_pairs={{0,8},{4,12},{8,0},{12,4},{16,24},{20,28},{24,16},{28,20},{1,9},{5... | collective-permute-start | bytes 393224 | tf_op jit(solution)/shard_map/ppermute | solution.py:131
  5.9 7.0 %collective-permute-start.6 = (bf16[512,128]{1,0:T(8,128)(2,1)}, bf16[512,128]{1,0:T(8,128)(2,1)S(1)}, u32[]{:S(2)}, u32[]{:S(2)}) collective-permute-start(bf16[512,128]{1,0:T(8,128)(2,1)} %values.3), channel_id=1, source_target_pairs={{0,8},{4,12},{8,0},{12,4},{16,24},{20,28},{24,16},{28,20},{1,9},{5... | collective-permute-start | bytes 393224 | tf_op jit(solution)/shard_map/ppermute | solution.py:131
  6.4 3.3 %copy-start.2 = (bf16[32,128]{1,0:T(8,128)(2,1)S(1)}, bf16[32,128]{1,0:T(8,128)(2,1)}, u32[]{:S(2)}) copy-start(bf16[32,128]{1,0:T(8,128)(2,1)} %queries) | copy-start | bytes 24580
  6.4 3.3 %copy-start.3 = (s32[1,32,4,4]{1,3,2,0:T(4,128)S(1)}, s32[1,32,4,4]{1,3,2,0:T(4,128)}, u32[]{:S(2)}) copy-start(s32[1,32,4,4]{1,3,2,0:T(4,128)} %param.15) | copy-start | bytes 6148
  6.4 3.3 %copy-start.4 = (s32[1,32,4]{1,2,0:T(4,128)S(1)}, s32[1,32,4]{1,2,0:T(4,128)}, u32[]{:S(2)}) copy-start(s32[1,32,4]{1,2,0:T(4,128)} %param.14) | copy-start | bytes 1540
  6.4 4.6 %collective-permute-start.1 = (bf16[2,2,8,128]{3,2,0,1:T(8,128)(2,1)S(1)}, bf16[2,2,8,128]{3,2,0,1:T(8,128)(2,1)S(1)}, u32[]{:S(2)}, u32[]{:S(2)}) collective-permute-start(bf16[2,2,8,128]{3,2,0,1:T(8,128)(2,1)S(1)} %fusion.1), channel_id=1, source_target_pairs={{0,2},{1,3},{2,0},{3,1},{4,6},{5,7},{6,4},{7,5},{8,10},{9,11},{10,... | collective-permute-start | bytes 24584 | tf_op jit(solution)/shard_map/ppermute | solution.py:131
  9.2 1.9 %collective-permute-start.2 = (bf16[512,128]{1,0:T(8,128)(2,1)}, bf16[512,128]{1,0:T(8,128)(2,1)S(1)}, u32[]{:S(2)}, u32[]{:S(2)}) collective-permute-start(bf16[512,128]{1,0:T(8,128)(2,1)} %keys.3), channel_id=1, source_target_pairs={{0,4},{4,0},{8,12},{12,8},{16,20},{20,16},{24,28},{28,24},{1,5},{5... | collective-permute-start | bytes 393224 | tf_op jit(solution)/shard_map/ppermute | solution.py:131
  9.2 1.9 %collective-permute-start.3 = (bf16[512,128]{1,0:T(8,128)(2,1)}, bf16[512,128]{1,0:T(8,128)(2,1)S(1)}, u32[]{:S(2)}, u32[]{:S(2)}) collective-permute-start(bf16[512,128]{1,0:T(8,128)(2,1)} %values.3), channel_id=1, source_target_pairs={{0,4},{4,0},{8,12},{12,8},{16,20},{20,16},{24,28},{28,24},{1,5},{5... | collective-permute-start | bytes 393224 | tf_op jit(solution)/shard_map/ppermute | solution.py:131
  9.7 0.7 %copy-start.5 = (bf16[1,32]{1,0:T(2,128)(2,1)S(1)}, bf16[1,32]{1,0:T(2,128)(2,1)}, u32[]{:S(2)}) copy-start(bf16[1,32]{1,0:T(2,128)(2,1)} %lse) | copy-start | bytes 196
  11.1 4.2 %collective-permute-start.4 = (bf16[128,128]{1,0:T(8,128)(2,1)S(1)}, bf16[128,128]{1,0:T(8,128)(2,1)S(1)}, u32[]{:S(2)}, u32[]{:S(2)}) collective-permute-start(bf16[128,128]{1,0:T(8,128)(2,1)S(1)} %pad_maximum_fusion.1.r0), channel_id=1, source_target_pairs={{0,16},{4,20},{8,24},{12,28},{16,0},{20,4},{24,8},{28,12},{1,17},{... | collective-permute-start | bytes 98312 | tf_op jit(solution)/shard_map/ppermute | solution.py:131
  12.9 2.7 %copy-start = (bf16[512,128]{1,0:T(8,128)(2,1)S(1)}, bf16[512,128]{1,0:T(8,128)(2,1)}, u32[]{:S(2)}) copy-start(bf16[512,128]{1,0:T(8,128)(2,1)} %keys.3) | copy-start | bytes 393220
  12.9 2.7 %copy-start.1 = (bf16[512,128]{1,0:T(8,128)(2,1)S(1)}, bf16[512,128]{1,0:T(8,128)(2,1)}, u32[]{:S(2)}) copy-start(bf16[512,128]{1,0:T(8,128)(2,1)} %values.3) | copy-start | bytes 393220
  12.9 2.6 %collective-permute-start.7 = (bf16[512,128]{1,0:T(8,128)(2,1)S(1)}, bf16[512,128]{1,0:T(8,128)(2,1)S(1)}, u32[]{:S(2)}, u32[]{:S(2)}) collective-permute-start(bf16[512,128]{1,0:T(8,128)(2,1)S(1)} %collective-permute-done.5.k2), channel_id=1, source_target_pairs={{0,4},{4,0},{8,12},{12,8},{16,20},{20,16},{24,28},{28,24},{1,5},{5... | collective-permute-start | bytes 393224 | tf_op jit(solution)/shard_map/ppermute | solution.py:131
  12.9 2.6 %collective-permute-start.8 = (bf16[512,128]{1,0:T(8,128)(2,1)S(1)}, bf16[512,128]{1,0:T(8,128)(2,1)S(1)}, u32[]{:S(2)}, u32[]{:S(2)}) collective-permute-start(bf16[512,128]{1,0:T(8,128)(2,1)S(1)} %collective-permute-done.6.v2), channel_id=1, source_target_pairs={{0,4},{4,0},{8,12},{12,8},{16,20},{20,16},{24,28},{28,24},{1,5},{5... | collective-permute-start | bytes 393224 | tf_op jit(solution)/shard_map/ppermute | solution.py:131
  13.4 4.8 %collective-permute-start.10 = (bf16[128,128]{1,0:T(8,128)(2,1)S(1)}, bf16[128,128]{1,0:T(8,128)(2,1)S(1)}, u32[]{:S(2)}, u32[]{:S(2)}) collective-permute-start(bf16[128,128]{1,0:T(8,128)(2,1)S(1)} %pad_maximum_fusion.1.r0), channel_id=1, source_target_pairs={{0,24},{4,28},{8,16},{12,20},{16,8},{20,12},{24,0},{28,4},{1,25},{... | collective-permute-start | bytes 98312 | tf_op jit(solution)/shard_map/ppermute | solution.py:131
  14.8 3.9 %collective-permute-start.9 = (bf16[128,128]{1,0:T(8,128)(2,1)S(1)}, bf16[128,128]{1,0:T(8,128)(2,1)S(1)}, u32[]{:S(2)}, u32[]{:S(2)}) collective-permute-start(bf16[128,128]{1,0:T(8,128)(2,1)S(1)} %pad_maximum_fusion.1.r0), channel_id=1, source_target_pairs={{0,8},{4,12},{8,0},{12,4},{16,24},{20,28},{24,16},{28,20},{1,9},{5... | collective-permute-start | bytes 98312 | tf_op jit(solution)/shard_map/ppermute | solution.py:131
  16.2 3.7 %collective-permute-start.12 = (bf16[32,128]{1,0:T(8,128)(2,1)S(1)}, bf16[32,128]{1,0:T(8,128)(2,1)S(1)}, u32[]{:S(2)}, u32[]{:S(2)}) collective-permute-start(bf16[32,128]{1,0:T(8,128)(2,1)S(1)} %get-tuple-element.45), channel_id=1, source_target_pairs={{0,16},{4,20},{8,24},{12,28},{16,0},{20,4},{24,8},{28,12},{1,17},{... | collective-permute-start | bytes 24584 | tf_op jit(solution)/shard_map/ppermute | solution.py:131
  18.7 1.4 %collective-permute-start.11 = (bf16[4,128,128]{2,1,0:T(8,128)(2,1)S(1)}, bf16[4,128,128]{2,1,0:T(8,128)(2,1)S(1)}, u32[]{:S(2)}, u32[]{:S(2)}) collective-permute-start(bf16[4,128,128]{2,1,0:T(8,128)(2,1)S(1)} %pad_maximum_fusion.lane), channel_id=1, source_target_pairs={{0,4},{4,0},{8,12},{12,8},{16,20},{20,16},{24,28},{28,24},{1,5},{5... | collective-permute-start | bytes 393224 | tf_op jit(solution)/shard_map/ppermute | solution.py:131

commit v6 on v5

--- a/solution.py
+++ b/solution.py
@@ -141,17 +141,19 @@
     return lax.dot_general(ones, both, contract, preferred_element_type=jnp.float32)[0:1]
 
 
-def unpack(parts, count):
+def unpack(parts, count, times=1):
     queries, grads, outs = (
         jnp.concatenate([r[k * count : (k + 1) * count] for r in parts], axis=0) for k in range(3)
     )
     small = [r[3 * count : 4 * count].astype(jnp.float32) for r in parts]
     lane = lax.broadcasted_iota(jnp.int32, small[0].shape, 1) // count
     merged = small[0]
-    for k in range(1, len(parts)):
-        merged = jnp.where(lane == k, small[k], merged)
+    for k in range(1, len(parts) * times):
+        merged = jnp.where(lane == k, small[k % len(parts)], merged)
     half = merged.shape[0] // 2
-    delta = row_sums(outs, grads).astype(jnp.bfloat16).astype(jnp.float32)
+    delta = row_sums(
+        jnp.concatenate([outs] * times, axis=0), jnp.concatenate([grads] * times, axis=0)
+    ).astype(jnp.bfloat16).astype(jnp.float32)
     return queries, grads, delta, merged[0:1], merged[half:]
 
 
@@ -175,14 +177,12 @@
 
 def doubled(r0, r1):
     parts, count = (r0[...], r1[...]), r0.shape[0] // 4
-    queries, grads, delta, lse, ids = unpack(parts + parts, count)
-    row = lax.broadcasted_iota(jnp.int32, queries.shape, 0)
+    queries, grads, delta, lse, ids = unpack(parts, count, 2)
 
     def beside(value):
         zero = jnp.zeros_like(value)
-        return jnp.concatenate(
-            [jnp.where(row < 2 * count, value, zero), jnp.where(row < 2 * count, zero, value)], axis=1
-        )
+        left, right = jnp.concatenate([value, zero], axis=1), jnp.concatenate([zero, value], axis=1)
+        return jnp.concatenate([left, right], axis=0)
 
     return beside(queries), beside(grads), delta, lse, ids
 

time: 21.5 us -> 21.5 us (level)
  no operation moved by 1% of the time
where the time goes in v6:
time: 21.5 us; the launch traced here: 21.3 us
  starting transfers between devices  14.2 us (66%)
  Pallas kernels  2.46 us (11%)
  waiting for transfers between devices  2.39 us (11%)
  other arithmetic  0.77 us (4%)
  between operations  0.77 us (4%)
  local copies, waits for them, and re-layouts  0.69 us (3%)
    ppermute x13, starting transfers between devices, swap(): return lax.ppermute(value, axis, [(i, i ^ bit) for i in range(count)])  14.2 us
    pallas_call x6, Pallas kernels, kernel(): pl.pallas_call(body, out_shape=tuple((jax.ShapeDtypeStruct(v, t) for v, t...  2.46 us
    ppermute x13, waiting for transfers between devices, swap(): return lax.ppermute(value, axis, [(i, i ^ bit) for i in range(count)])  2.39 us
    another operation x1, other arithmetic, fast_local(): mine = jnp.stack([out_grad, attn_out])  0.72 us
    unnamed x12, local copies, waits for them, and re-layouts  0.68 us
  transfers between devices with their start and end apart: 13, of which 5 were waited for; matrix products, arithmetic and copies ran while one was open for 0% of the time, Pallas kernels for 6%

profile of v6, /device:TPU:0, one launch (start us, length us, event | category | flops | bytes accessed | tf_op | source)
XLA Modules:
  0.0 21.3 jit_solution(10211737144583299885)
XLA Ops:
  0.6 0.7 %pad_maximum_fusion.2 = bf16[2,8,512]{2,1,0:T(8,128)(2,1)S(1)} fusion(bf16[1,8,512]{2,1,0:T(8,128)(2,1)} %bitcast.31, bf16[1,8,512]{2,1,0:T(8,128)(2,1)} %bitcast.32), kind=kLoop, calls=%fused_computation.7 | loop fusion | flops 8192 | bytes 32768 | tf_op jit(solution)/shard_map/stack | solution.py:289
  1.3 3.0 %collective-permute-start = (bf16[2,8,512]{2,1,0:T(8,128)(2,1)S(1)}, bf16[2,8,512]{2,1,0:T(8,128)(2,1)S(1)}, u32[]{:S(2)}, u32[]{:S(2)}) collective-permute-start(bf16[2,8,512]{2,1,0:T(8,128)(2,1)S(1)} %pad_maximum_fusion.2), channel_id=1, source_target_pairs={{0,1},{1,0},{2,3},{3,2},{4,5},{5,4},{6,7},{7,6},{8,9},{9,8},{10,11... | collective-permute-start | bytes 49160 | tf_op jit(solution)/shard_map/ppermute | solution.py:131
  4.4 1.5 %collective-permute-start.5 = (bf16[512,128]{1,0:T(8,128)(2,1)}, bf16[512,128]{1,0:T(8,128)(2,1)S(1)}, u32[]{:S(2)}, u32[]{:S(2)}) collective-permute-start(bf16[512,128]{1,0:T(8,128)(2,1)} %keys.3), channel_id=1, source_target_pairs={{0,8},{4,12},{8,0},{12,4},{16,24},{20,28},{24,16},{28,20},{1,9},{5... | collective-permute-start | bytes 393224 | tf_op jit(solution)/shard_map/ppermute | solution.py:131
  5.9 0.5 %collective-permute-start.6 = (bf16[512,128]{1,0:T(8,128)(2,1)}, bf16[512,128]{1,0:T(8,128)(2,1)S(1)}, u32[]{:S(2)}, u32[]{:S(2)}) collective-permute-start(bf16[512,128]{1,0:T(8,128)(2,1)} %values.3), channel_id=1, source_target_pairs={{0,8},{4,12},{8,0},{12,4},{16,24},{20,28},{24,16},{28,20},{1,9},{5... | collective-permute-start | bytes 393224 | tf_op jit(solution)/shard_map/ppermute | solution.py:131
  6.4 0.0 copy-start.4
  6.4 2.8 %collective-permute-start.1 = (bf16[2,2,8,128]{3,2,0,1:T(8,128)(2,1)S(1)}, bf16[2,2,8,128]{3,2,0,1:T(8,128)(2,1)S(1)}, u32[]{:S(2)}, u32[]{:S(2)}) collective-permute-start(bf16[2,2,8,128]{3,2,0,1:T(8,128)(2,1)S(1)} %fusion.1), channel_id=1, source_target_pairs={{0,2},{1,3},{2,0},{3,1},{4,6},{5,7},{6,4},{7,5},{8,10},{9,11},{10,... | collective-permute-start | bytes 24584 | tf_op jit(solution)/shard_map/ppermute | solution.py:131
  9.2 0.0 collective-permute-start.2
  9.2 0.5 %collective-permute-start.3 = (bf16[512,128]{1,0:T(8,128)(2,1)}, bf16[512,128]{1,0:T(8,128)(2,1)S(1)}, u32[]{:S(2)}, u32[]{:S(2)}) collective-permute-start(bf16[512,128]{1,0:T(8,128)(2,1)} %values.3), channel_id=1, source_target_pairs={{0,4},{4,0},{8,12},{12,8},{16,20},{20,16},{24,28},{28,24},{1,5},{5... | collective-permute-start | bytes 393224 | tf_op jit(solution)/shard_map/ppermute | solution.py:131
  9.7 0.6 %copy-done.5 = bf16[1,32]{1,0:T(2,128)(2,1)S(1)} copy-done((bf16[1,32]{1,0:T(2,128)(2,1)S(1)}, bf16[1,32]{1,0:T(2,128)(2,1)}, u32[]{:S(2)}) %copy-start.5) | copy-done | bytes 88
  10.4 0.1 small.1
  10.5 0.5 %collective-permute-done.1 = bf16[2,2,8,128]{3,2,0,1:T(8,128)(2,1)S(1)} collective-permute-done((bf16[2,2,8,128]{3,2,0,1:T(8,128)(2,1)S(1)}, bf16[2,2,8,128]{3,2,0,1:T(8,128)(2,1)S(1)}, u32[]{:S(2)}, u32[]{:S(2)}) %collective-permute-start.1) | collective-permute-done | bytes 8224 | tf_op jit(solution)/shard_map/ppermute | solution.py:131
  11.1 0.0 collective-permute-done.3.v1
  11.1 1.7 %collective-permute-start.4 = (bf16[128,128]{1,0:T(8,128)(2,1)S(1)}, bf16[128,128]{1,0:T(8,128)(2,1)S(1)}, u32[]{:S(2)}, u32[]{:S(2)}) collective-permute-start(bf16[128,128]{1,0:T(8,128)(2,1)S(1)} %pad_maximum_fusion.1.r0), channel_id=1, source_target_pairs={{0,16},{4,20},{8,24},{12,28},{16,0},{20,4},{24,8},{28,12},{1,17},{... | collective-permute-start | bytes 98312 | tf_op jit(solution)/shard_map/ppermute | solution.py:131
  12.9 0.0 collective-permute-done.5.k2
  12.9 0.0 collective-permute-start.7
  12.9 0.5 %collective-permute-start.8 = (bf16[512,128]{1,0:T(8,128)(2,1)S(1)}, bf16[512,128]{1,0:T(8,128)(2,1)S(1)}, u32[]{:S(2)}, u32[]{:S(2)}) collective-permute-start(bf16[512,128]{1,0:T(8,128)(2,1)S(1)} %collective-permute-done.6.v2), channel_id=1, source_target_pairs={{0,4},{4,0},{8,12},{12,8},{16,20},{20,16},{24,28},{28,24},{1,5},{5... | collective-permute-start | bytes 393224 | tf_op jit(solution)/shard_map/ppermute | solution.py:131
  13.4 1.4 %collective-permute-start.10 = (bf16[128,128]{1,0:T(8,128)(2,1)S(1)}, bf16[128,128]{1,0:T(8,128)(2,1)S(1)}, u32[]{:S(2)}, u32[]{:S(2)}) collective-permute-start(bf16[128,128]{1,0:T(8,128)(2,1)S(1)} %pad_maximum_fusion.1.r0), channel_id=1, source_target_pairs={{0,24},{4,28},{8,16},{12,20},{16,8},{20,12},{24,0},{28,4},{1,25},{... | collective-permute-start | bytes 98312 | tf_op jit(solution)/shard_map/ppermute | solution.py:131
  14.8 0.5 %collective-permute-start.9 = (bf16[128,128]{1,0:T(8,128)(2,1)S(1)}, bf16[128,128]{1,0:T(8,128)(2,1)S(1)}, u32[]{:S(2)}, u32[]{:S(2)}) collective-permute-start(bf16[128,128]{1,0:T(8,128)(2,1)S(1)} %pad_maximum_fusion.1.r0), channel_id=1, source_target_pairs={{0,8},{4,12},{8,0},{12,4},{16,24},{20,28},{24,16},{28,20},{1,9},{5... | collective-permute-start | bytes 98312 | tf_op jit(solution)/shard_map/ppermute | solution.py:131
  15.3 0.0 collective-permute-done.4.r1
  15.3 0.1 rows.1
  15.5 0.0 collective-permute-done.7.k3
  15.5 0.0 collective-permute-done.8.v3
  15.5 0.0 copy-done
  15.5 0.7 %query_terms.1 = (f32[32,128]{1,0:T(8,128)S(1)}, bf16[32,128]{1,0:T(8,128)(2,1)S(1)}) custom-call(s32[1]{0:T(128)} %bitcast.shard_ref, bf16[128,256]{1,0:T(8,128)(2,1)S(1)} %get-tuple-element.38.queries, bf16[128,256]{1,0:T(8,128)(2,1)S(1)} %get-tuple-element.39.grads, f32[24,128]{1,0:T(8,128)S(1)} %get-tuple-element.40.stats, bf16[512,128]{1,0:T(8,128)(2,1)S(1)} %copy-done, ...), custom_call_target="tpu_custom_call" | custom-call | flops 1 | bytes 1 | tf_op jit(solution)/shard_map/query_terms/pallas_call | solution.py:279
  16.2 1.6 %collective-permute-start.12 = (bf16[32,128]{1,0:T(8,128)(2,1)S(1)}, bf16[32,128]{1,0:T(8,128)(2,1)S(1)}, u32[]{:S(2)}, u32[]{:S(2)}) collective-permute-start(bf16[32,128]{1,0:T(8,128)(2,1)S(1)} %get-tuple-element.45), channel_id=1, source_target_pairs={{0,16},{4,20},{8,24},{12,28},{16,0},{20,4},{24,8},{28,12},{1,17},{... | collective-permute-start | bytes 24584 | tf_op jit(solution)/shard_map/ppermute | solution.py:131
  17.8 0.4 %collective-permute-done.10 = bf16[128,128]{1,0:T(8,128)(2,1)S(1)} collective-permute-done((bf16[128,128]{1,0:T(8,128)(2,1)S(1)}, bf16[128,128]{1,0:T(8,128)(2,1)S(1)}, u32[]{:S(2)}, u32[]{:S(2)}) %collective-permute-start.10) | collective-permute-done | bytes 32800 | tf_op jit(solution)/shard_map/ppermute | solution.py:131
  18.2 0.5 %collective-permute-done.9 = bf16[128,128]{1,0:T(8,128)(2,1)S(1)} collective-permute-done((bf16[128,128]{1,0:T(8,128)(2,1)S(1)}, bf16[128,128]{1,0:T(8,128)(2,1)S(1)}, u32[]{:S(2)}, u32[]{:S(2)}) %collective-permute-start.9) | collective-permute-done | bytes 32800 | tf_op jit(solution)/shard_map/ppermute | solution.py:131
  18.7 0.1 collective-permute-start.11
  18.8 0.4 %key_terms.1 = (f32[512,128]{1,0:T(8,128)S(1)}, f32[512,128]{1,0:T(8,128)S(1)}) custom-call(s32[1]{0:T(128)} %bitcast.shard_ref, bf16[4,128,128]{2,1,0:T(8,128)(2,1)S(1)} %pad_maximum_fusion.lane, bf16[512,128]{1,0:T(8,128)(2,1)S(1)} %copy-done, bf16[512,128]{1,0:T(8,128)(2,1)S(1)} %copy-done.1), custom_call_target="tpu_custom_call" | custom-call | flops 3000000000 | bytes 3000000 | tf_op jit(solution)/shard_map/key_terms/pallas_call | solution.py:279
  19.2 0.7 %collective-permute-done.12.q_back = bf16[32,128]{1,0:T(8,128)(2,1)S(1)} collective-permute-done((bf16[32,128]{1,0:T(8,128)(2,1)S(1)}, bf16[32,128]{1,0:T(8,128)(2,1)S(1)}, u32[]{:S(2)}, u32[]{:S(2)}) %collective-permute-start.12) | collective-permute-done | bytes 8224 | tf_op jit(solution)/shard_map/ppermute | solution.py:131
  20.0 0.2 collective-permute-done.11.lane
  20.2 1.1 %finish.1 = (bf16[32,128]{1,0:T(8,128)(2,1)}, bf16[512,128]{1,0:T(8,128)(2,1)}, bf16[512,128]{1,0:T(8,128)(2,1)}) custom-call(s32[1]{0:T(128)} %bitcast.shard_ref, bf16[4,128,128]{2,1,0:T(8,128)(2,1)S(1)} %collective-permute-done.11.lane, bf16[512,128]{1,0:T(8,128)(2,1)S(1)} %copy-done, bf16[512,128]{1,0:T(8,128)(2,1)S(1)} %copy-done.1, ...), custom_call_target="tpu_custom_call" | custom-call | tf_op jit(solution)/shard_map/finish/pallas_call | solution.py:279
  (21 shorter events, 0.1 us)
Async XLA Ops:
  1.3 5.1 %collective-permute-start = (bf16[2,8,512]{2,1,0:T(8,128)(2,1)S(1)}, bf16[2,8,512]{2,1,0:T(8,128)(2,1)S(1)}, u32[]{:S(2)}, u32[]{:S(2)}) collective-permute-start(bf16[2,8,512]{2,1,0:T(8,128)(2,1)S(1)} %pad_maximum_fusion.2), channel_id=1, source_target_pairs={{0,1},{1,0},{2,3},{3,2},{4,5},{5,4},{6,7},{7,6},{8,9},{9,8},{10,11... | collective-permute-start | bytes 49160 | tf_op jit(solution)/shard_map/ppermute | solution.py:131
  4.4 8.5 %collective-permute-start.5 = (bf16[512,128]{1,0:T(8,128)(2,1)}, bf16[512,128]{1,0:T(8,128)(2,1)S(1)}, u32[]{:S(2)}, u32[]{:S(2)}) collective-permute-start(bf16[512,128]{1,0:T(8,128)(2,1)} %keys.3), channel_id=1, source_target_pairs={{0,8},{4,12},{8,0},{12,4},{16,24},{20,28},{24,16},{28,20},{1,9},{5... | collective-permute-start | bytes 393224 | tf_op jit(solution)/shard_map/ppermute | solution.py:131
  5.9 7.0 %collective-permute-start.6 = (bf16[512,128]{1,0:T(8,128)(2,1)}, bf16[512,128]{1,0:T(8,128)(2,1)S(1)}, u32[]{:S(2)}, u32[]{:S(2)}) collective-permute-start(bf16[512,128]{1,0:T(8,128)(2,1)} %values.3), channel_id=1, source_target_pairs={{0,8},{4,12},{8,0},{12,4},{16,24},{20,28},{24,16},{28,20},{1,9},{5... | collective-permute-start | bytes 393224 | tf_op jit(solution)/shard_map/ppermute | solution.py:131
  6.4 3.3 %copy-start.2 = (bf16[32,128]{1,0:T(8,128)(2,1)S(1)}, bf16[32,128]{1,0:T(8,128)(2,1)}, u32[]{:S(2)}) copy-start(bf16[32,128]{1,0:T(8,128)(2,1)} %queries) | copy-start | bytes 24580
  6.4 3.3 %copy-start.3 = (s32[1,32,4,4]{1,3,2,0:T(4,128)S(1)}, s32[1,32,4,4]{1,3,2,0:T(4,128)}, u32[]{:S(2)}) copy-start(s32[1,32,4,4]{1,3,2,0:T(4,128)} %param.15) | copy-start | bytes 6148
  6.4 3.3 %copy-start.4 = (s32[1,32,4]{1,2,0:T(4,128)S(1)}, s32[1,32,4]{1,2,0:T(4,128)}, u32[]{:S(2)}) copy-start(s32[1,32,4]{1,2,0:T(4,128)} %param.14) | copy-start | bytes 1540
  6.4 4.6 %collective-permute-start.1 = (bf16[2,2,8,128]{3,2,0,1:T(8,128)(2,1)S(1)}, bf16[2,2,8,128]{3,2,0,1:T(8,128)(2,1)S(1)}, u32[]{:S(2)}, u32[]{:S(2)}) collective-permute-start(bf16[2,2,8,128]{3,2,0,1:T(8,128)(2,1)S(1)} %fusion.1), channel_id=1, source_target_pairs={{0,2},{1,3},{2,0},{3,1},{4,6},{5,7},{6,4},{7,5},{8,10},{9,11},{10,... | collective-permute-start | bytes 24584 | tf_op jit(solution)/shard_map/ppermute | solution.py:131
  9.2 1.9 %collective-permute-start.2 = (bf16[512,128]{1,0:T(8,128)(2,1)}, bf16[512,128]{1,0:T(8,128)(2,1)S(1)}, u32[]{:S(2)}, u32[]{:S(2)}) collective-permute-start(bf16[512,128]{1,0:T(8,128)(2,1)} %keys.3), channel_id=1, source_target_pairs={{0,4},{4,0},{8,12},{12,8},{16,20},{20,16},{24,28},{28,24},{1,5},{5... | collective-permute-start | bytes 393224 | tf_op jit(solution)/shard_map/ppermute | solution.py:131
  9.2 1.9 %collective-permute-start.3 = (bf16[512,128]{1,0:T(8,128)(2,1)}, bf16[512,128]{1,0:T(8,128)(2,1)S(1)}, u32[]{:S(2)}, u32[]{:S(2)}) collective-permute-start(bf16[512,128]{1,0:T(8,128)(2,1)} %values.3), channel_id=1, source_target_pairs={{0,4},{4,0},{8,12},{12,8},{16,20},{20,16},{24,28},{28,24},{1,5},{5... | collective-permute-start | bytes 393224 | tf_op jit(solution)/shard_map/ppermute | solution.py:131
  9.7 0.7 %copy-start.5 = (bf16[1,32]{1,0:T(2,128)(2,1)S(1)}, bf16[1,32]{1,0:T(2,128)(2,1)}, u32[]{:S(2)}) copy-start(bf16[1,32]{1,0:T(2,128)(2,1)} %lse) | copy-start | bytes 196
  11.1 4.2 %collective-permute-start.4 = (bf16[128,128]{1,0:T(8,128)(2,1)S(1)}, bf16[128,128]{1,0:T(8,128)(2,1)S(1)}, u32[]{:S(2)}, u32[]{:S(2)}) collective-permute-start(bf16[128,128]{1,0:T(8,128)(2,1)S(1)} %pad_maximum_fusion.1.r0), channel_id=1, source_target_pairs={{0,16},{4,20},{8,24},{12,28},{16,0},{20,4},{24,8},{28,12},{1,17},{... | collective-permute-start | bytes 98312 | tf_op jit(solution)/shard_map/ppermute | solution.py:131
  12.9 2.7 %copy-start = (bf16[512,128]{1,0:T(8,128)(2,1)S(1)}, bf16[512,128]{1,0:T(8,128)(2,1)}, u32[]{:S(2)}) copy-start(bf16[512,128]{1,0:T(8,128)(2,1)} %keys.3) | copy-start | bytes 393220
  12.9 2.7 %copy-start.1 = (bf16[512,128]{1,0:T(8,128)(2,1)S(1)}, bf16[512,128]{1,0:T(8,128)(2,1)}, u32[]{:S(2)}) copy-start(bf16[512,128]{1,0:T(8,128)(2,1)} %values.3) | copy-start | bytes 393220
  12.9 2.6 %collective-permute-start.7 = (bf16[512,128]{1,0:T(8,128)(2,1)S(1)}, bf16[512,128]{1,0:T(8,128)(2,1)S(1)}, u32[]{:S(2)}, u32[]{:S(2)}) collective-permute-start(bf16[512,128]{1,0:T(8,128)(2,1)S(1)} %collective-permute-done.5.k2), channel_id=1, source_target_pairs={{0,4},{4,0},{8,12},{12,8},{16,20},{20,16},{24,28},{28,24},{1,5},{5... | collective-permute-start | bytes 393224 | tf_op jit(solution)/shard_map/ppermute | solution.py:131
  12.9 2.6 %collective-permute-start.8 = (bf16[512,128]{1,0:T(8,128)(2,1)S(1)}, bf16[512,128]{1,0:T(8,128)(2,1)S(1)}, u32[]{:S(2)}, u32[]{:S(2)}) collective-permute-start(bf16[512,128]{1,0:T(8,128)(2,1)S(1)} %collective-permute-done.6.v2), channel_id=1, source_target_pairs={{0,4},{4,0},{8,12},{12,8},{16,20},{20,16},{24,28},{28,24},{1,5},{5... | collective-permute-start | bytes 393224 | tf_op jit(solution)/shard_map/ppermute | solution.py:131
  13.4 4.8 %collective-permute-start.10 = (bf16[128,128]{1,0:T(8,128)(2,1)S(1)}, bf16[128,128]{1,0:T(8,128)(2,1)S(1)}, u32[]{:S(2)}, u32[]{:S(2)}) collective-permute-start(bf16[128,128]{1,0:T(8,128)(2,1)S(1)} %pad_maximum_fusion.1.r0), channel_id=1, source_target_pairs={{0,24},{4,28},{8,16},{12,20},{16,8},{20,12},{24,0},{28,4},{1,25},{... | collective-permute-start | bytes 98312 | tf_op jit(solution)/shard_map/ppermute | solution.py:131
  14.8 3.9 %collective-permute-start.9 = (bf16[128,128]{1,0:T(8,128)(2,1)S(1)}, bf16[128,128]{1,0:T(8,128)(2,1)S(1)}, u32[]{:S(2)}, u32[]{:S(2)}) collective-permute-start(bf16[128,128]{1,0:T(8,128)(2,1)S(1)} %pad_maximum_fusion.1.r0), channel_id=1, source_target_pairs={{0,8},{4,12},{8,0},{12,4},{16,24},{20,28},{24,16},{28,20},{1,9},{5... | collective-permute-start | bytes 98312 | tf_op jit(solution)/shard_map/ppermute | solution.py:131
  16.2 3.7 %collective-permute-start.12 = (bf16[32,128]{1,0:T(8,128)(2,1)S(1)}, bf16[32,128]{1,0:T(8,128)(2,1)S(1)}, u32[]{:S(2)}, u32[]{:S(2)}) collective-permute-start(bf16[32,128]{1,0:T(8,128)(2,1)S(1)} %get-tuple-element.45), channel_id=1, source_target_pairs={{0,16},{4,20},{8,24},{12,28},{16,0},{20,4},{24,8},{28,12},{1,17},{... | collective-permute-start | bytes 24584 | tf_op jit(solution)/shard_map/ppermute | solution.py:131
  18.7 1.4 %collective-permute-start.11 = (bf16[4,128,128]{2,1,0:T(8,128)(2,1)S(1)}, bf16[4,128,128]{2,1,0:T(8,128)(2,1)S(1)}, u32[]{:S(2)}, u32[]{:S(2)}) collective-permute-start(bf16[4,128,128]{2,1,0:T(8,128)(2,1)S(1)} %pad_maximum_fusion.lane), channel_id=1, source_target_pairs={{0,4},{4,0},{8,12},{12,8},{16,20},{20,16},{24,28},{28,24},{1,5},{5... | collective-permute-start | bytes 393224 | tf_op jit(solution)/shard_map/ppermute | solution.py:131

commit v7 on v6

--- a/solution.py
+++ b/solution.py
@@ -145,11 +145,12 @@
     queries, grads, outs = (
         jnp.concatenate([r[k * count : (k + 1) * count] for r in parts], axis=0) for k in range(3)
     )
-    small = [r[3 * count : 4 * count].astype(jnp.float32) for r in parts]
+    small = [r[3 * count : 4 * count] for r in parts]
     lane = lax.broadcasted_iota(jnp.int32, small[0].shape, 1) // count
     merged = small[0]
     for k in range(1, len(parts) * times):
         merged = jnp.where(lane == k, small[k % len(parts)], merged)
+    merged = merged.astype(jnp.float32)
     half = merged.shape[0] // 2
     delta = row_sums(
         jnp.concatenate([outs] * times, axis=0), jnp.concatenate([grads] * times, axis=0)

time: 21.5 us -> 21.5 us (level)
  no operation moved by 1% of the time
where the time goes in v7:
time: 21.5 us; the launch traced here: 21.3 us
  starting transfers between devices  14.2 us (66%)
  Pallas kernels  2.46 us (11%)
  waiting for transfers between devices  2.39 us (11%)
  other arithmetic  0.77 us (4%)
  between operations  0.77 us (4%)
  local copies, waits for them, and re-layouts  0.69 us (3%)
    ppermute x13, starting transfers between devices, swap(): return lax.ppermute(value, axis, [(i, i ^ bit) for i in range(count)])  14.2 us
    pallas_call x6, Pallas kernels, kernel(): pl.pallas_call(body, out_shape=tuple((jax.ShapeDtypeStruct(v, t) for v, t...  2.46 us
    ppermute x13, waiting for transfers between devices, swap(): return lax.ppermute(value, axis, [(i, i ^ bit) for i in range(count)])  2.39 us
    another operation x1, other arithmetic, fast_local(): mine = jnp.stack([out_grad, attn_out])  0.72 us
    unnamed x12, local copies, waits for them, and re-layouts  0.68 us
  transfers between devices with their start and end apart: 13, of which 5 were waited for; matrix products, arithmetic and copies ran while one was open for 0% of the time, Pallas kernels for 6%

profile of v7, /device:TPU:0, one launch (start us, length us, event | category | flops | bytes accessed | tf_op | source)
XLA Modules:
  0.0 21.3 jit_solution(1603244798116980257)
XLA Ops:
  0.6 0.7 %pad_maximum_fusion.2 = bf16[2,8,512]{2,1,0:T(8,128)(2,1)S(1)} fusion(bf16[1,8,512]{2,1,0:T(8,128)(2,1)} %bitcast.31, bf16[1,8,512]{2,1,0:T(8,128)(2,1)} %bitcast.32), kind=kLoop, calls=%fused_computation.7 | loop fusion | flops 8192 | bytes 32768 | tf_op jit(solution)/shard_map/stack | solution.py:290
  1.3 3.0 %collective-permute-start = (bf16[2,8,512]{2,1,0:T(8,128)(2,1)S(1)}, bf16[2,8,512]{2,1,0:T(8,128)(2,1)S(1)}, u32[]{:S(2)}, u32[]{:S(2)}) collective-permute-start(bf16[2,8,512]{2,1,0:T(8,128)(2,1)S(1)} %pad_maximum_fusion.2), channel_id=1, source_target_pairs={{0,1},{1,0},{2,3},{3,2},{4,5},{5,4},{6,7},{7,6},{8,9},{9,8},{10,11... | collective-permute-start | bytes 49160 | tf_op jit(solution)/shard_map/ppermute | solution.py:131
  4.4 1.5 %collective-permute-start.5 = (bf16[512,128]{1,0:T(8,128)(2,1)}, bf16[512,128]{1,0:T(8,128)(2,1)S(1)}, u32[]{:S(2)}, u32[]{:S(2)}) collective-permute-start(bf16[512,128]{1,0:T(8,128)(2,1)} %keys.3), channel_id=1, source_target_pairs={{0,8},{4,12},{8,0},{12,4},{16,24},{20,28},{24,16},{28,20},{1,9},{5... | collective-permute-start | bytes 393224 | tf_op jit(solution)/shard_map/ppermute | solution.py:131
  5.9 0.5 %collective-permute-start.6 = (bf16[512,128]{1,0:T(8,128)(2,1)}, bf16[512,128]{1,0:T(8,128)(2,1)S(1)}, u32[]{:S(2)}, u32[]{:S(2)}) collective-permute-start(bf16[512,128]{1,0:T(8,128)(2,1)} %values.3), channel_id=1, source_target_pairs={{0,8},{4,12},{8,0},{12,4},{16,24},{20,28},{24,16},{28,20},{1,9},{5... | collective-permute-start | bytes 393224 | tf_op jit(solution)/shard_map/ppermute | solution.py:131
  6.4 0.0 collective-permute-done
  6.4 0.0 copy-start.4
  6.4 2.8 %collective-permute-start.1 = (bf16[2,2,8,128]{3,2,0,1:T(8,128)(2,1)S(1)}, bf16[2,2,8,128]{3,2,0,1:T(8,128)(2,1)S(1)}, u32[]{:S(2)}, u32[]{:S(2)}) collective-permute-start(bf16[2,2,8,128]{3,2,0,1:T(8,128)(2,1)S(1)} %fusion.1), channel_id=1, source_target_pairs={{0,2},{1,3},{2,0},{3,1},{4,6},{5,7},{6,4},{7,5},{8,10},{9,11},{10,... | collective-permute-start | bytes 24584 | tf_op jit(solution)/shard_map/ppermute | solution.py:131
  9.2 0.0 collective-permute-start.2
  9.2 0.5 %collective-permute-start.3 = (bf16[512,128]{1,0:T(8,128)(2,1)}, bf16[512,128]{1,0:T(8,128)(2,1)S(1)}, u32[]{:S(2)}, u32[]{:S(2)}) collective-permute-start(bf16[512,128]{1,0:T(8,128)(2,1)} %values.3), channel_id=1, source_target_pairs={{0,4},{4,0},{8,12},{12,8},{16,20},{20,16},{24,28},{28,24},{1,5},{5... | collective-permute-start | bytes 393224 | tf_op jit(solution)/shard_map/ppermute | solution.py:131
  9.7 0.6 %copy-done.5 = bf16[1,32]{1,0:T(2,128)(2,1)S(1)} copy-done((bf16[1,32]{1,0:T(2,128)(2,1)S(1)}, bf16[1,32]{1,0:T(2,128)(2,1)}, u32[]{:S(2)}) %copy-start.5) | copy-done | bytes 88
  10.4 0.1 small.1
  10.5 0.5 %collective-permute-done.1 = bf16[2,2,8,128]{3,2,0,1:T(8,128)(2,1)S(1)} collective-permute-done((bf16[2,2,8,128]{3,2,0,1:T(8,128)(2,1)S(1)}, bf16[2,2,8,128]{3,2,0,1:T(8,128)(2,1)S(1)}, u32[]{:S(2)}, u32[]{:S(2)}) %collective-permute-start.1) | collective-permute-done | bytes 8224 | tf_op jit(solution)/shard_map/ppermute | solution.py:131
  11.1 0.0 collective-permute-done.2.k1
  11.1 0.0 collective-permute-done.3.v1
  11.1 1.7 %collective-permute-start.4 = (bf16[128,128]{1,0:T(8,128)(2,1)S(1)}, bf16[128,128]{1,0:T(8,128)(2,1)S(1)}, u32[]{:S(2)}, u32[]{:S(2)}) collective-permute-start(bf16[128,128]{1,0:T(8,128)(2,1)S(1)} %pad_maximum_fusion.1.r0), channel_id=1, source_target_pairs={{0,16},{4,20},{8,24},{12,28},{16,0},{20,4},{24,8},{28,12},{1,17},{... | collective-permute-start | bytes 98312 | tf_op jit(solution)/shard_map/ppermute | solution.py:131
  12.9 0.0 collective-permute-done.5.k2
  12.9 0.0 collective-permute-start.7
  12.9 0.5 %collective-permute-start.8 = (bf16[512,128]{1,0:T(8,128)(2,1)S(1)}, bf16[512,128]{1,0:T(8,128)(2,1)S(1)}, u32[]{:S(2)}, u32[]{:S(2)}) collective-permute-start(bf16[512,128]{1,0:T(8,128)(2,1)S(1)} %collective-permute-done.6.v2), channel_id=1, source_target_pairs={{0,4},{4,0},{8,12},{12,8},{16,20},{20,16},{24,28},{28,24},{1,5},{5... | collective-permute-start | bytes 393224 | tf_op jit(solution)/shard_map/ppermute | solution.py:131
  13.4 1.4 %collective-permute-start.10 = (bf16[128,128]{1,0:T(8,128)(2,1)S(1)}, bf16[128,128]{1,0:T(8,128)(2,1)S(1)}, u32[]{:S(2)}, u32[]{:S(2)}) collective-permute-start(bf16[128,128]{1,0:T(8,128)(2,1)S(1)} %pad_maximum_fusion.1.r0), channel_id=1, source_target_pairs={{0,24},{4,28},{8,16},{12,20},{16,8},{20,12},{24,0},{28,4},{1,25},{... | collective-permute-start | bytes 98312 | tf_op jit(solution)/shard_map/ppermute | solution.py:131
  14.8 0.5 %collective-permute-start.9 = (bf16[128,128]{1,0:T(8,128)(2,1)S(1)}, bf16[128,128]{1,0:T(8,128)(2,1)S(1)}, u32[]{:S(2)}, u32[]{:S(2)}) collective-permute-start(bf16[128,128]{1,0:T(8,128)(2,1)S(1)} %pad_maximum_fusion.1.r0), channel_id=1, source_target_pairs={{0,8},{4,12},{8,0},{12,4},{16,24},{20,28},{24,16},{28,20},{1,9},{5... | collective-permute-start | bytes 98312 | tf_op jit(solution)/shard_map/ppermute | solution.py:131
  15.3 0.0 collective-permute-done.4.r1
  15.3 0.1 rows.1
  15.5 0.0 copy-done
  15.5 0.7 %query_terms.1 = (f32[32,128]{1,0:T(8,128)S(1)}, bf16[32,128]{1,0:T(8,128)(2,1)S(1)}) custom-call(s32[1]{0:T(128)} %bitcast.shard_ref, bf16[128,256]{1,0:T(8,128)(2,1)S(1)} %get-tuple-element.38.queries, bf16[128,256]{1,0:T(8,128)(2,1)S(1)} %get-tuple-element.39.grads, f32[24,128]{1,0:T(8,128)S(1)} %get-tuple-element.40.stats, bf16[512,128]{1,0:T(8,128)(2,1)S(1)} %copy-done, ...), custom_call_target="tpu_custom_call" | custom-call | flops 1 | bytes 1 | tf_op jit(solution)/shard_map/query_terms/pallas_call | solution.py:280
  16.2 1.6 %collective-permute-start.12 = (bf16[32,128]{1,0:T(8,128)(2,1)S(1)}, bf16[32,128]{1,0:T(8,128)(2,1)S(1)}, u32[]{:S(2)}, u32[]{:S(2)}) collective-permute-start(bf16[32,128]{1,0:T(8,128)(2,1)S(1)} %get-tuple-element.45), channel_id=1, source_target_pairs={{0,16},{4,20},{8,24},{12,28},{16,0},{20,4},{24,8},{28,12},{1,17},{... | collective-permute-start | bytes 24584 | tf_op jit(solution)/shard_map/ppermute | solution.py:131
  17.8 0.4 %collective-permute-done.10 = bf16[128,128]{1,0:T(8,128)(2,1)S(1)} collective-permute-done((bf16[128,128]{1,0:T(8,128)(2,1)S(1)}, bf16[128,128]{1,0:T(8,128)(2,1)S(1)}, u32[]{:S(2)}, u32[]{:S(2)}) %collective-permute-start.10) | collective-permute-done | bytes 32800 | tf_op jit(solution)/shard_map/ppermute | solution.py:131
  18.2 0.5 %collective-permute-done.9 = bf16[128,128]{1,0:T(8,128)(2,1)S(1)} collective-permute-done((bf16[128,128]{1,0:T(8,128)(2,1)S(1)}, bf16[128,128]{1,0:T(8,128)(2,1)S(1)}, u32[]{:S(2)}, u32[]{:S(2)}) %collective-permute-start.9) | collective-permute-done | bytes 32800 | tf_op jit(solution)/shard_map/ppermute | solution.py:131
  18.7 0.1 collective-permute-start.11
  18.8 0.4 %key_terms.1 = (f32[512,128]{1,0:T(8,128)S(1)}, f32[512,128]{1,0:T(8,128)S(1)}) custom-call(s32[1]{0:T(128)} %bitcast.shard_ref, bf16[4,128,128]{2,1,0:T(8,128)(2,1)S(1)} %pad_maximum_fusion.lane, bf16[512,128]{1,0:T(8,128)(2,1)S(1)} %copy-done, bf16[512,128]{1,0:T(8,128)(2,1)S(1)} %copy-done.1), custom_call_target="tpu_custom_call" | custom-call | flops 3000000000 | bytes 3000000 | tf_op jit(solution)/shard_map/key_terms/pallas_call | solution.py:280
  19.2 0.7 %collective-permute-done.12.q_back = bf16[32,128]{1,0:T(8,128)(2,1)S(1)} collective-permute-done((bf16[32,128]{1,0:T(8,128)(2,1)S(1)}, bf16[32,128]{1,0:T(8,128)(2,1)S(1)}, u32[]{:S(2)}, u32[]{:S(2)}) %collective-permute-start.12) | collective-permute-done | bytes 8224 | tf_op jit(solution)/shard_map/ppermute | solution.py:131
  20.0 0.2 collective-permute-done.11.lane
  20.2 1.1 %finish.1 = (bf16[32,128]{1,0:T(8,128)(2,1)}, bf16[512,128]{1,0:T(8,128)(2,1)}, bf16[512,128]{1,0:T(8,128)(2,1)}) custom-call(s32[1]{0:T(128)} %bitcast.shard_ref, bf16[4,128,128]{2,1,0:T(8,128)(2,1)S(1)} %collective-permute-done.11.lane, bf16[512,128]{1,0:T(8,128)(2,1)S(1)} %copy-done, bf16[512,128]{1,0:T(8,128)(2,1)S(1)} %copy-done.1, ...), custom_call_target="tpu_custom_call" | custom-call | tf_op jit(solution)/shard_map/finish/pallas_call | solution.py:280
  (21 shorter events, 0.1 us)
Async XLA Ops:
  1.3 5.1 %collective-permute-start = (bf16[2,8,512]{2,1,0:T(8,128)(2,1)S(1)}, bf16[2,8,512]{2,1,0:T(8,128)(2,1)S(1)}, u32[]{:S(2)}, u32[]{:S(2)}) collective-permute-start(bf16[2,8,512]{2,1,0:T(8,128)(2,1)S(1)} %pad_maximum_fusion.2), channel_id=1, source_target_pairs={{0,1},{1,0},{2,3},{3,2},{4,5},{5,4},{6,7},{7,6},{8,9},{9,8},{10,11... | collective-permute-start | bytes 49160 | tf_op jit(solution)/shard_map/ppermute | solution.py:131
  4.4 8.5 %collective-permute-start.5 = (bf16[512,128]{1,0:T(8,128)(2,1)}, bf16[512,128]{1,0:T(8,128)(2,1)S(1)}, u32[]{:S(2)}, u32[]{:S(2)}) collective-permute-start(bf16[512,128]{1,0:T(8,128)(2,1)} %keys.3), channel_id=1, source_target_pairs={{0,8},{4,12},{8,0},{12,4},{16,24},{20,28},{24,16},{28,20},{1,9},{5... | collective-permute-start | bytes 393224 | tf_op jit(solution)/shard_map/ppermute | solution.py:131
  5.9 7.0 %collective-permute-start.6 = (bf16[512,128]{1,0:T(8,128)(2,1)}, bf16[512,128]{1,0:T(8,128)(2,1)S(1)}, u32[]{:S(2)}, u32[]{:S(2)}) collective-permute-start(bf16[512,128]{1,0:T(8,128)(2,1)} %values.3), channel_id=1, source_target_pairs={{0,8},{4,12},{8,0},{12,4},{16,24},{20,28},{24,16},{28,20},{1,9},{5... | collective-permute-start | bytes 393224 | tf_op jit(solution)/shard_map/ppermute | solution.py:131
  6.4 3.3 %copy-start.2 = (bf16[32,128]{1,0:T(8,128)(2,1)S(1)}, bf16[32,128]{1,0:T(8,128)(2,1)}, u32[]{:S(2)}) copy-start(bf16[32,128]{1,0:T(8,128)(2,1)} %queries) | copy-start | bytes 24580
  6.4 3.3 %copy-start.3 = (s32[1,32,4,4]{1,3,2,0:T(4,128)S(1)}, s32[1,32,4,4]{1,3,2,0:T(4,128)}, u32[]{:S(2)}) copy-start(s32[1,32,4,4]{1,3,2,0:T(4,128)} %param.15) | copy-start | bytes 6148
  6.4 3.3 %copy-start.4 = (s32[1,32,4]{1,2,0:T(4,128)S(1)}, s32[1,32,4]{1,2,0:T(4,128)}, u32[]{:S(2)}) copy-start(s32[1,32,4]{1,2,0:T(4,128)} %param.14) | copy-start | bytes 1540
  6.4 4.6 %collective-permute-start.1 = (bf16[2,2,8,128]{3,2,0,1:T(8,128)(2,1)S(1)}, bf16[2,2,8,128]{3,2,0,1:T(8,128)(2,1)S(1)}, u32[]{:S(2)}, u32[]{:S(2)}) collective-permute-start(bf16[2,2,8,128]{3,2,0,1:T(8,128)(2,1)S(1)} %fusion.1), channel_id=1, source_target_pairs={{0,2},{1,3},{2,0},{3,1},{4,6},{5,7},{6,4},{7,5},{8,10},{9,11},{10,... | collective-permute-start | bytes 24584 | tf_op jit(solution)/shard_map/ppermute | solution.py:131
  9.2 1.9 %collective-permute-start.2 = (bf16[512,128]{1,0:T(8,128)(2,1)}, bf16[512,128]{1,0:T(8,128)(2,1)S(1)}, u32[]{:S(2)}, u32[]{:S(2)}) collective-permute-start(bf16[512,128]{1,0:T(8,128)(2,1)} %keys.3), channel_id=1, source_target_pairs={{0,4},{4,0},{8,12},{12,8},{16,20},{20,16},{24,28},{28,24},{1,5},{5... | collective-permute-start | bytes 393224 | tf_op jit(solution)/shard_map/ppermute | solution.py:131
  9.2 1.9 %collective-permute-start.3 = (bf16[512,128]{1,0:T(8,128)(2,1)}, bf16[512,128]{1,0:T(8,128)(2,1)S(1)}, u32[]{:S(2)}, u32[]{:S(2)}) collective-permute-start(bf16[512,128]{1,0:T(8,128)(2,1)} %values.3), channel_id=1, source_target_pairs={{0,4},{4,0},{8,12},{12,8},{16,20},{20,16},{24,28},{28,24},{1,5},{5... | collective-permute-start | bytes 393224 | tf_op jit(solution)/shard_map/ppermute | solution.py:131
  9.7 0.7 %copy-start.5 = (bf16[1,32]{1,0:T(2,128)(2,1)S(1)}, bf16[1,32]{1,0:T(2,128)(2,1)}, u32[]{:S(2)}) copy-start(bf16[1,32]{1,0:T(2,128)(2,1)} %lse) | copy-start | bytes 196
  11.1 4.2 %collective-permute-start.4 = (bf16[128,128]{1,0:T(8,128)(2,1)S(1)}, bf16[128,128]{1,0:T(8,128)(2,1)S(1)}, u32[]{:S(2)}, u32[]{:S(2)}) collective-permute-start(bf16[128,128]{1,0:T(8,128)(2,1)S(1)} %pad_maximum_fusion.1.r0), channel_id=1, source_target_pairs={{0,16},{4,20},{8,24},{12,28},{16,0},{20,4},{24,8},{28,12},{1,17},{... | collective-permute-start | bytes 98312 | tf_op jit(solution)/shard_map/ppermute | solution.py:131
  12.9 2.7 %copy-start = (bf16[512,128]{1,0:T(8,128)(2,1)S(1)}, bf16[512,128]{1,0:T(8,128)(2,1)}, u32[]{:S(2)}) copy-start(bf16[512,128]{1,0:T(8,128)(2,1)} %keys.3) | copy-start | bytes 393220
  12.9 2.7 %copy-start.1 = (bf16[512,128]{1,0:T(8,128)(2,1)S(1)}, bf16[512,128]{1,0:T(8,128)(2,1)}, u32[]{:S(2)}) copy-start(bf16[512,128]{1,0:T(8,128)(2,1)} %values.3) | copy-start | bytes 393220
  12.9 2.6 %collective-permute-start.7 = (bf16[512,128]{1,0:T(8,128)(2,1)S(1)}, bf16[512,128]{1,0:T(8,128)(2,1)S(1)}, u32[]{:S(2)}, u32[]{:S(2)}) collective-permute-start(bf16[512,128]{1,0:T(8,128)(2,1)S(1)} %collective-permute-done.5.k2), channel_id=1, source_target_pairs={{0,4},{4,0},{8,12},{12,8},{16,20},{20,16},{24,28},{28,24},{1,5},{5... | collective-permute-start | bytes 393224 | tf_op jit(solution)/shard_map/ppermute | solution.py:131
  12.9 2.6 %collective-permute-start.8 = (bf16[512,128]{1,0:T(8,128)(2,1)S(1)}, bf16[512,128]{1,0:T(8,128)(2,1)S(1)}, u32[]{:S(2)}, u32[]{:S(2)}) collective-permute-start(bf16[512,128]{1,0:T(8,128)(2,1)S(1)} %collective-permute-done.6.v2), channel_id=1, source_target_pairs={{0,4},{4,0},{8,12},{12,8},{16,20},{20,16},{24,28},{28,24},{1,5},{5... | collective-permute-start | bytes 393224 | tf_op jit(solution)/shard_map/ppermute | solution.py:131
  13.4 4.8 %collective-permute-start.10 = (bf16[128,128]{1,0:T(8,128)(2,1)S(1)}, bf16[128,128]{1,0:T(8,128)(2,1)S(1)}, u32[]{:S(2)}, u32[]{:S(2)}) collective-permute-start(bf16[128,128]{1,0:T(8,128)(2,1)S(1)} %pad_maximum_fusion.1.r0), channel_id=1, source_target_pairs={{0,24},{4,28},{8,16},{12,20},{16,8},{20,12},{24,0},{28,4},{1,25},{... | collective-permute-start | bytes 98312 | tf_op jit(solution)/shard_map/ppermute | solution.py:131
  14.8 3.9 %collective-permute-start.9 = (bf16[128,128]{1,0:T(8,128)(2,1)S(1)}, bf16[128,128]{1,0:T(8,128)(2,1)S(1)}, u32[]{:S(2)}, u32[]{:S(2)}) collective-permute-start(bf16[128,128]{1,0:T(8,128)(2,1)S(1)} %pad_maximum_fusion.1.r0), channel_id=1, source_target_pairs={{0,8},{4,12},{8,0},{12,4},{16,24},{20,28},{24,16},{28,20},{1,9},{5... | collective-permute-start | bytes 98312 | tf_op jit(solution)/shard_map/ppermute | solution.py:131
  16.2 3.7 %collective-permute-start.12 = (bf16[32,128]{1,0:T(8,128)(2,1)S(1)}, bf16[32,128]{1,0:T(8,128)(2,1)S(1)}, u32[]{:S(2)}, u32[]{:S(2)}) collective-permute-start(bf16[32,128]{1,0:T(8,128)(2,1)S(1)} %get-tuple-element.45), channel_id=1, source_target_pairs={{0,16},{4,20},{8,24},{12,28},{16,0},{20,4},{24,8},{28,12},{1,17},{... | collective-permute-start | bytes 24584 | tf_op jit(solution)/shard_map/ppermute | solution.py:131
  18.7 1.4 %collective-permute-start.11 = (bf16[4,128,128]{2,1,0:T(8,128)(2,1)S(1)}, bf16[4,128,128]{2,1,0:T(8,128)(2,1)S(1)}, u32[]{:S(2)}, u32[]{:S(2)}) collective-permute-start(bf16[4,128,128]{2,1,0:T(8,128)(2,1)S(1)} %pad_maximum_fusion.lane), channel_id=1, source_target_pairs={{0,4},{4,0},{8,12},{12,8},{16,20},{20,16},{24,28},{28,24},{1,5},{5... | collective-permute-start | bytes 393224 | tf_op jit(solution)/shard_map/ppermute | solution.py:131
